TPU v7x, 128 devices: a whole 4x4x4 slice. The times are simulated.
128 devices in a mesh: group: 2 (over z_lo), tensor: 16 (over y, x), seq: 4 (over z_hi, core).
Axes of the slice: x: 4, y: 4, z: 4 (z_hi: 2, z_lo: 2; z = z_hi * 2 + z_lo), core: 2. Of those that a mesh axis runs over, the one named last changes fastest.
Arguments:
- context: bfloat16 [1024, 3, 8192], P(('group', 'seq'), None, 'tensor'), may hold values from -6 to 6
- resid_in: bfloat16 [1024, 3, 8192], P('tensor', None, ('group', 'seq')), may hold values from -6 to 6
- target_out_w: bfloat16 [3, 8192, 8192], P(None, 'tensor', ('group', 'seq')), may hold values from -0.0625 to 0.0625
- embedded: bfloat16 [1024, 8192], P(('group', 'seq'), 'tensor'), may hold values from -6 to 6
- join_w: bfloat16 [3, 8192, 8192], P(None, ('group', 'seq'), 'tensor'), may hold values from -0.0390625 to 0.0390625
- embed_gain: bfloat16 [8192], P('tensor'), may hold values from 0.5 to 1.5
- joined_gain: bfloat16 [8192], P('tensor'), may hold values from 0.5 to 1.5
- query_w: bfloat16 [2, 8192, 8192], P(None, 'tensor', ('group', 'seq')), may hold values from -0.046875 to 0.046875
- key_w: bfloat16 [2, 8192, 1024], P(None, 'tensor', ('group', 'seq')), may hold values from -0.046875 to 0.046875
- value_w: bfloat16 [2, 8192, 1024], P(None, 'tensor', ('group', 'seq')), may hold values from -0.046875 to 0.046875
- out_w: bfloat16 [8192, 8192], P(('group', 'seq'), 'tensor'), may hold values from -0.0625 to 0.0625
- segment_ids: int32 [2, 512], replicated, may hold values from 0 to 7, never falling along the last dimension, each value on 1 to 128 neighbouring positions
- grad_hidden: bfloat16 [1024, 8192], P(('group', 'seq'), 'tensor'), may hold values from -0.1875 to 0.1875
Outputs:
- draft_hidden: bfloat16 [1024, 8192], P(('group', 'seq'), 'tensor')
- grad_join_w: bfloat16 [3, 8192, 8192], P(None, ('group', 'seq'), 'tensor')
- grad_query_w: bfloat16 [2, 8192, 8192], P(None, 'tensor', ('group', 'seq'))
- grad_key_w: bfloat16 [2, 8192, 1024], P(None, 'tensor', ('group', 'seq'))
- grad_value_w: bfloat16 [2, 8192, 1024], P(None, 'tensor', ('group', 'seq'))
- grad_out_w: bfloat16 [8192, 8192], P(('group', 'seq'), 'tensor')
Inputs may be any that keep to these rules, and one draw needn't show every extreme that they name: `segment_ids`: ids never fall along a sequence; each run of one id is a packed document.
All inputs are finite; a program needn't handle non-finite values.
Results may differ from a plain program's by a relative error of at most 0.035.
Values may be sent and summed in bfloat16 or wider, within the bound.
A program may use at most 128 MiB of HBM per device.

v0:
```python
import jax
import jax.numpy as jnp
from jax import lax
from jax.sharding import PartitionSpec as P

epsilon = 1e-05


def gather_groups(values):
    return lax.all_gather(values, ("group", "seq"), axis=0, tiled=True)


def gather_tensor(values):
    return lax.all_gather(values, "tensor", axis=0, tiled=True)


def partial_tensor(builder, row_count):
    return lax.psum_scatter(
        builder(jnp.int32(0), row_count * lax.axis_size("tensor")).astype(jnp.bfloat16),
        "tensor",
        scatter_dimension=0,
        tiled=True,
    ).astype(jnp.float32)


def partial_groups(builder, row_count):
    return lax.psum_scatter(
        builder(jnp.int32(0), row_count * lax.axis_size(("group", "seq"))),
        ("group", "seq"),
        scatter_dimension=0,
        tiled=True,
    )


def totals_tensor(values):
    return lax.psum(values, "tensor")


def local(
    context,
    resid_in,
    target_out_w,
    embedded,
    join_w,
    embed_gain,
    joined_gain,
    query_w,
    key_w,
    value_w,
    out_w,
    segment_ids,
    grad_hidden,
):
    tensor_count = lax.axis_size("tensor")
    group_count = lax.axis_size(("group", "seq"))
    tensor_index = lax.axis_index("tensor")
    group_rows = embedded.shape[0]
    token_count = group_rows * group_count
    tensor_rows = token_count // tensor_count
    model_width = embedded.shape[1] * tensor_count
    head_dim = key_w.shape[2]
    group_heads = query_w.shape[2] // head_dim
    seq_len = segment_ids.shape[1]
    score_scale = head_dim ** (-0.5)
    context_all = gather_groups(context)

    def target_term(first_row, row_count):
        return jnp.einsum(
            "tlk,lkm->tlm", context_all, target_out_w, preferred_element_type=jnp.float32
        )

    level_part = partial_tensor(target_term, tensor_rows)
    features = (resid_in.astype(jnp.float32) + level_part).astype(jnp.bfloat16)
    features_all = gather_tensor(features)

    def join_term(first_row, row_count):
        return jnp.einsum("tlk,lkm->tm", features_all, join_w, preferred_element_type=jnp.float32)

    joined = partial_groups(join_term, group_rows)
    embed_float = embedded.astype(jnp.float32)
    joined_squares, embed_squares = totals_tensor(
        (jnp.sum(joined * joined, -1), jnp.sum(embed_float * embed_float, -1))
    )
    joined_rate = lax.rsqrt(joined_squares / model_width + epsilon)[:, None]
    embed_rate = lax.rsqrt(embed_squares / model_width + epsilon)[:, None]
    joined_scale = joined_gain.astype(jnp.float32)
    hidden_norm = (joined * joined_rate * joined_scale).astype(jnp.bfloat16)
    embed_norm = (embed_float * embed_rate * embed_gain.astype(jnp.float32)).astype(jnp.bfloat16)
    inputs_all = gather_groups(jnp.stack([embed_norm, hidden_norm], 1))

    def query_term(first_row, row_count):
        return jnp.einsum("thk,hkm->tm", inputs_all, query_w, preferred_element_type=jnp.float32)

    query = partial_tensor(query_term, tensor_rows).astype(jnp.bfloat16)
    key_part = jnp.einsum("thk,hkm->tm", inputs_all, key_w, preferred_element_type=jnp.float32)
    value_part = jnp.einsum("thk,hkm->tm", inputs_all, value_w, preferred_element_type=jnp.float32)
    key_sum, value_sum = totals_tensor((key_part, value_part))
    key_full = key_sum.astype(jnp.bfloat16)
    value_full = value_sum.astype(jnp.bfloat16)
    first_query = tensor_index * tensor_rows
    seq_start = first_query // seq_len * seq_len
    flat_segments = segment_ids.reshape(-1)
    query_segment = lax.dynamic_slice_in_dim(flat_segments, first_query, tensor_rows, 0)
    key_segment = lax.dynamic_slice_in_dim(flat_segments, seq_start, seq_len, 0)
    query_pos = first_query + jnp.arange(tensor_rows, dtype=jnp.int32)
    key_pos = seq_start + jnp.arange(seq_len, dtype=jnp.int32)
    allowed = (query_segment[:, None] == key_segment[None, :]) & (
        key_pos[None, :] <= query_pos[:, None]
    )
    keys_local = lax.dynamic_slice_in_dim(key_full, seq_start, seq_len, 0)
    values_local = lax.dynamic_slice_in_dim(value_full, seq_start, seq_len, 0)
    query_heads = query.reshape(tensor_rows, group_heads, head_dim)
    scores = (
        jnp.einsum("igd,jd->gij", query_heads, keys_local, preferred_element_type=jnp.float32)
        * score_scale
    )
    scores = jnp.where(allowed[None], scores, -1e30)
    probs = jax.nn.softmax(scores, axis=-1)
    probs_low = probs.astype(jnp.bfloat16)
    attended = jnp.einsum(
        "gij,jd->igd", probs_low, values_local, preferred_element_type=jnp.float32
    )
    attended = attended.reshape(tensor_rows, group_heads * head_dim).astype(jnp.bfloat16)
    attended_all = gather_tensor(attended)

    def output_term(first_row, row_count):
        return jnp.dot(attended_all, out_w, preferred_element_type=jnp.float32)

    attn_sum = partial_groups(output_term, group_rows)
    draft_hidden = (joined + attn_sum).astype(jnp.bfloat16)
    cotangent_all = gather_groups(grad_hidden)
    grad_out = jnp.einsum(
        "tm,tn->mn", attended_all, cotangent_all, preferred_element_type=jnp.float32
    ).astype(jnp.bfloat16)

    def back_term(first_row, row_count):
        return jnp.einsum("tn,mn->tm", cotangent_all, out_w, preferred_element_type=jnp.float32)

    attended_grad = partial_tensor(back_term, tensor_rows).astype(jnp.bfloat16)
    grad_heads = attended_grad.reshape(tensor_rows, group_heads, head_dim)
    probs_grad = jnp.einsum(
        "igd,jd->gij", grad_heads, values_local, preferred_element_type=jnp.float32
    )
    score_grad = (
        probs * (probs_grad - jnp.sum(probs_grad * probs, -1, keepdims=True)) * score_scale
    ).astype(jnp.bfloat16)
    query_grad = jnp.einsum(
        "gij,jd->igd", score_grad, keys_local, preferred_element_type=jnp.float32
    )
    query_grad = query_grad.reshape(tensor_rows, group_heads * head_dim).astype(jnp.bfloat16)
    key_local = jnp.einsum(
        "gij,igd->jd", score_grad, query_heads, preferred_element_type=jnp.float32
    )
    value_local = jnp.einsum(
        "gij,igd->jd", probs_low, grad_heads, preferred_element_type=jnp.float32
    )
    zeros_full = jnp.zeros((token_count, head_dim), jnp.float32)
    key_grad_sum, value_grad_sum = totals_tensor(
        (
            lax.dynamic_update_slice_in_dim(zeros_full, key_local, seq_start, 0),
            lax.dynamic_update_slice_in_dim(zeros_full, value_local, seq_start, 0),
        )
    )
    key_grad = key_grad_sum.astype(jnp.bfloat16)
    value_grad = value_grad_sum.astype(jnp.bfloat16)
    query_grad_all = gather_tensor(query_grad)
    grad_query = jnp.einsum(
        "thk,tm->hkm", inputs_all, query_grad_all, preferred_element_type=jnp.float32
    ).astype(jnp.bfloat16)
    grad_key = jnp.einsum(
        "thk,tm->hkm", inputs_all, key_grad, preferred_element_type=jnp.float32
    ).astype(jnp.bfloat16)
    grad_value = jnp.einsum(
        "thk,tm->hkm", inputs_all, value_grad, preferred_element_type=jnp.float32
    ).astype(jnp.bfloat16)

    def input_term(first_row, row_count):
        running = jnp.einsum(
            "tm,km->tk", query_grad_all, query_w[1], preferred_element_type=jnp.float32
        )
        running = running + jnp.einsum(
            "tm,km->tk", key_grad, key_w[1], preferred_element_type=jnp.float32
        )
        return running + jnp.einsum(
            "tm,km->tk", value_grad, value_w[1], preferred_element_type=jnp.float32
        )

    hidden_grad = partial_groups(input_term, group_rows)
    scaled_grad = hidden_grad * joined_scale
    inner_sum = totals_tensor(jnp.sum(scaled_grad * joined, -1))
    joined_grad = (
        grad_hidden.astype(jnp.float32)
        + joined_rate * scaled_grad
        - joined * (joined_rate * joined_rate * joined_rate) * (inner_sum / model_width)[:, None]
    )
    joined_grad_all = gather_groups(joined_grad.astype(jnp.bfloat16))
    grad_join = jnp.einsum(
        "tlk,tm->lkm", features_all, joined_grad_all, preferred_element_type=jnp.float32
    ).astype(jnp.bfloat16)
    return (draft_hidden, grad_join, grad_query, grad_key, grad_value, grad_out)


def solution(mesh):
    in_specs = (
        P(("group", "seq"), None, "tensor"),
        P("tensor", None, ("group", "seq")),
        P(None, "tensor", ("group", "seq")),
        P(("group", "seq"), "tensor"),
        P(None, ("group", "seq"), "tensor"),
        P("tensor"),
        P("tensor"),
        P(None, "tensor", ("group", "seq")),
        P(None, "tensor", ("group", "seq")),
        P(None, "tensor", ("group", "seq")),
        P(("group", "seq"), "tensor"),
        P(),
        P(("group", "seq"), "tensor"),
    )
    out_specs = (
        P(("group", "seq"), "tensor"),
        P(None, ("group", "seq"), "tensor"),
        P(None, "tensor", ("group", "seq")),
        P(None, "tensor", ("group", "seq")),
        P(None, "tensor", ("group", "seq")),
        P(("group", "seq"), "tensor"),
    )
    return jax.shard_map(local, mesh=mesh, in_specs=in_specs, out_specs=out_specs, check_vma=False)
```

profile of v0, /device:TPU:1, one launch (start us, length us, event | category | flops | bytes accessed | tf_op | source)
XLA Modules:
  0.0 806.7 jit_solution(1776212183460946412)
XLA Ops:
  7.2 0.7 all-gather.8.cloned.1.call-update
  8.0 48.6 %all-gather.8.cloned.1.call-done = bf16[1024,3,512]{2,0,1:T(8,128)(2,1)} async-done(((bf16[128,3,512]{2,0,1:T(8,128)(2,1)}), bf16[1024,3,512]{2,0,1:T(8,128)(2,1)}) %all-gather.8.cloned.1.call-update) | async-done | bytes 3145744 | tf_op jit(solution)/shard_map/all_gather | solution.py:10
  56.5 7.5 convert_bitcast_fusion
  64.1 14.4 %copy.57 = bf16[1024,3,1024]{2,1,0:T(4,128)(2,1)} copy(bf16[1024,3,1024]{0,2,1:T(8,128)(2,1)} %convert_bitcast_fusion) | data formatting | bytes 12582912 | tf_op jit(solution)/shard_map/convert_element_type | solution.py:19
  78.5 0.0 all-gather.10.cloned.1.call-start
  78.5 0.6 copy-done.26
  79.1 0.6 dynamic-slice
  80.3 140.2 %all-reduce.8.cloned.1.call-done = bf16[1024,3,1024]{2,1,0:T(4,128)(2,1)} async-done(((bf16[1024,3,1024]{2,1,0:T(4,128)(2,1)}), bf16[1024,3,1024]{2,1,0:T(4,128)(2,1)}) %all-reduce.8.cloned.1.call-update) | async-done | bytes 6291472
  220.5 1.2 constant_dynamic-slice_fusion
  221.7 0.9 add_convert_fusion
  222.7 0.0 reduce-scatter.6.cloned.1.call-start
  222.8 61.4 %all-gather.10.cloned.1.call-done = bf16[1024,3,1024]{2,0,1:T(8,128)(2,1)} async-done(((bf16[64,3,1024]{2,0,1:T(8,128)(2,1)}), bf16[1024,3,1024]{2,0,1:T(8,128)(2,1)}) %all-gather.10.cloned.1.call-update) | async-done | bytes 6291472 | tf_op jit(solution)/shard_map/all_gather | solution.py:14
  284.2 8.4 %convolution_bitcast_fusion = f32[1024,512]{1,0:T(8,128)} fusion(bf16[1024,3,1024]{2,0,1:T(8,128)(2,1)} %all-gather.10.cloned.1.call-done, bf16[3,1024,512]{2,1,0:T(8,128)(2,1)} %param.17), kind=kOutput, calls=%fused_computation.10 | convolution fusion | flops 3221225472 | bytes 11534336 | tf_op jit(solution)/shard_map/tlk,lkm->tm/dot_general | solution.py:77
  292.7 0.5 all-gather.16.cloned.1.call-update
  293.3 0.2 copy-done.11
  293.5 0.1 fusion.30
  293.6 34.5 %reduce-scatter.6.cloned.1.call-done = f32[128,512]{1,0:T(8,128)} async-done(((f32[1024,512]{1,0:T(8,128)}), f32[128,512]{1,0:T(8,128)}) %reduce-scatter.6.cloned.1.call-update) | async-done | bytes 262160 | tf_op jit(solution)/shard_map/reduce_scatter | solution.py:27
  328.2 1.1 multiply_reduce_fusion.2
  329.2 33.6 %all-reduce.3 = (f32[128]{0:T(128)S(1)}, f32[128]{0:T(128)S(1)}) all-reduce(f32[128]{0:T(128)S(1)} %multiply_reduce_fusion.2, f32[128]{0:T(128)S(1)} %fusion.30), channel_id=1, replica_groups=mesh['group'=2,'tensor'=16,'seq'=4] {'tensor'}, use_global_device_ids=true, to_apply=%region_5.0 | all-reduce | flops 256 | bytes 2048 | tf_op jit(solution)/shard_map/psum | solution.py:36
  362.8 0.1 fusion.40
  363.0 1.0 fusion.37
  364.0 0.7 pad_maximum_fusion
  364.8 1.4 all-gather.16.cloned.1.call-done
  366.2 3.8 convolution_convert_fusion.1
  370.1 34.7 %all-gather.12.cloned.1.call-done = bf16[1024,2,512]{2,0,1:T(8,128)(2,1)} async-done(((bf16[128,2,512]{2,0,1:T(8,128)(2,1)}), bf16[1024,2,512]{2,0,1:T(8,128)(2,1)}) %all-gather.12.cloned.1.call-update) | async-done | bytes 2097168 | tf_op jit(solution)/shard_map/all_gather | solution.py:10
  404.8 5.3 bitcast_convert_fusion
  410.1 0.0 all-gather.18.cloned.1.call-start
  410.2 0.6 copy-done.15
  410.7 0.1 dynamic_slice.14
  410.8 0.1 dynamic_slice.13
  410.9 0.7 compare_and_fusion
  411.6 0.1 copy-done.2
  411.7 0.7 convolution_bitcast_fusion.3
  412.4 0.7 convolution_bitcast_fusion.2
  413.1 75.4 %all-reduce.9 = (bf16[1024,128]{1,0:T(8,128)(2,1)S(1)}, bf16[1024,128]{1,0:T(8,128)(2,1)}) all-reduce(f32[1024,128]{1,0:T(8,128)S(1)} %convolution_bitcast_fusion.3, f32[1024,128]{1,0:T(8,128)S(1)} %convolution_bitcast_fusion.2), channel_id=1, replica_groups=mesh['group'=2,'tensor'=16,'seq'=4] {'tensor'}, use_global_device_ids=true, to_apply=%region_6.0 | all-reduce | flops 262144 | bytes 1572864 | tf_op jit(solution)/shard_map/psum | solution.py:36
  488.5 1.2 convolution_bitcast_fusion.1
  489.7 71.9 %reduce-scatter.8.cloned.1.call-done = bf16[64,1024]{1,0:T(8,128)(2,1)} async-done(((bf16[1024,1024]{1,0:T(8,128)(2,1)}), bf16[64,1024]{1,0:T(8,128)(2,1)}) %reduce-scatter.8.cloned.1.call-update) | async-done | bytes 131088 | tf_op jit(solution)/shard_map/reduce_scatter | solution.py:18
  561.6 2.4 fusion.81
  563.9 4.1 fusion.18
  568.1 0.7 copy.110
  568.8 0.2 all-gather.14.cloned.1.call-start
  569.0 2.1 fusion.17
  571.2 0.7 copy.111
  571.9 0.0 reduce-scatter.14.cloned.1.call-start
  572.0 5.0 fusion.16
  577.1 2.1 fusion.15
  579.2 77.5 %all-reduce.10 = (bf16[1024,128]{1,0:T(8,128)(2,1)}, bf16[1024,128]{1,0:T(8,128)(2,1)S(1)}) all-reduce(f32[1024,128]{1,0:T(8,128)S(1)} %fusion.16, f32[1024,128]{1,0:T(8,128)S(1)} %fusion.15), channel_id=1, replica_groups=mesh['group'=2,'tensor'=16,'seq'=4] {'tensor'}, use_global_device_ids=true, to_apply=%region_14.15 | all-reduce | flops 262144 | bytes 1572864 | tf_op jit(solution)/shard_map/psum | solution.py:36
  656.7 2.7 fusion.46
  659.4 3.4 fusion.20
  662.8 1.8 add_add_fusion
  664.6 0.0 reduce-scatter.10.cloned.1.call-start
  664.7 1.1 copy-done.22
  665.8 4.2 fusion.93
  670.0 42.5 %reduce-scatter.14.cloned.1.call-done = f32[128,512]{1,0:T(8,128)} async-done(((f32[1024,512]{1,0:T(8,128)}), f32[128,512]{1,0:T(8,128)}) %reduce-scatter.14.cloned.1.call-update) | async-done | bytes 262160 | tf_op jit(solution)/shard_map/reduce_scatter | solution.py:27
  712.6 1.1 multiply_reduce_fusion.1
  713.6 33.3 %psum.55 = f32[128]{0:T(128)S(1)} all-reduce(f32[128]{0:T(128)S(1)} %multiply_reduce_fusion.1), channel_id=1, replica_groups=mesh['group'=2,'tensor'=16,'seq'=4] {'tensor'}, use_global_device_ids=true, to_apply=%region_18.19 | all-reduce | flops 128 | bytes 1024 | tf_op jit(solution)/shard_map/psum | solution.py:36
  746.9 7.0 reduce-scatter.10.cloned.1.call-done
  753.9 1.8 subtract_convert_fusion
  755.8 1.5 convolution_convert_fusion.4
  757.3 1.5 convolution_convert_fusion.3
  758.7 2.3 convolution_convert_fusion.2
  761.0 3.7 fusion.4
  764.7 27.1 %all-gather.20.cloned.1.call-done = bf16[1024,512]{1,0:T(8,128)(2,1)} async-done(((bf16[128,512]{1,0:T(8,128)(2,1)}), bf16[1024,512]{1,0:T(8,128)(2,1)}) %all-gather.20.cloned.1.call-update) | async-done | bytes 1048592 | tf_op jit(solution)/shard_map/all_gather | solution.py:10
  791.9 8.3 %convolution_convert_fusion = bf16[3,1024,512]{2,1,0:T(8,128)(2,1)} fusion(bf16[1024,3,1024]{2,0,1:T(8,128)(2,1)} %all-gather.10.cloned.1.call-done, bf16[1024,512]{1,0:T(8,128)(2,1)} %all-gather.20.cloned.1.call-done), kind=kOutput, calls=%fused_computation.4 | convolution fusion | flops 3222798336 | bytes 10485760 | tf_op jit(solution)/shard_map/tlk,tm->lkm/dot_general | solution.py:197
  (79 shorter events, 0.7 us)
Async XLA Ops:
  7.2 49.4 %copy-start = (bf16[3,512,1024]{2,1,0:T(8,128)(2,1)S(1)}, bf16[3,512,1024]{2,1,0:T(8,128)(2,1)}, u32[]{:S(2)}) copy-start(bf16[3,512,1024]{2,1,0:T(8,128)(2,1)} %param.15) | copy-start | bytes 9437188
  7.2 49.3 %all-gather.8.cloned.1.call-start = ((), (), s32[]{:S(2)}) async-start(), calls=%async_computation.5 | async-start | bytes 3538944 | tf_op jit(solution)/shard_map/all_gather | solution.py:10
  7.9 212.6 %all-reduce.8.cloned.1.call-start = ((), (), s32[]{:S(2)}) async-start(), calls=%async_computation.17 | async-start | bytes 16777216
  78.4 0.7 copy-start.26
  78.4 143.3 %copy-start.12 = (bf16[64,3,1024]{2,0,1:T(8,128)(2,1)S(1)}, bf16[64,3,1024]{2,0,1:T(8,128)(2,1)}, u32[]{:S(2)}) copy-start(bf16[64,3,1024]{2,0,1:T(8,128)(2,1)} %param.14) | copy-start | bytes 1179652
  78.5 205.7 %all-gather.10.cloned.1.call-start = ((), (), s32[]{:S(2)}) async-start(), calls=%async_computation.6 | async-start | bytes 6684672 | tf_op jit(solution)/shard_map/all_gather | solution.py:14
  222.7 105.5 %reduce-scatter.6.cloned.1.call-start = ((), (), s32[]{:S(2)}) async-start(), calls=%async_computation.7 | async-start | bytes 2359296 | tf_op jit(solution)/shard_map/reduce_scatter | solution.py:27
  292.6 0.7 copy-start.16
  292.6 0.7 copy-start.17
  292.6 0.9 copy-start.11
  292.6 73.6 %copy-start.21 = (bf16[1024,512]{1,0:T(8,128)(2,1)S(1)}, bf16[1024,512]{1,0:T(8,128)(2,1)}, u32[]{:S(2)}) copy-start(bf16[1024,512]{1,0:T(8,128)(2,1)} %param.23) | copy-start | bytes 3145732
  292.6 73.6 %all-gather.16.cloned.1.call-start = ((), (), s32[]{:S(2)}) async-start(), calls=%async_computation.12 | async-start | bytes 1179648 | tf_op jit(solution)/shard_map/all_gather | solution.py:10
  293.2 111.5 %all-gather.12.cloned.1.call-start = ((), (), s32[]{:S(2)}) async-start(), calls=%async_computation.8 | async-start | bytes 2359296 | tf_op jit(solution)/shard_map/all_gather | solution.py:10
  364.8 123.7 %reduce-scatter.12.cloned.1.call-start = ((), (), s32[]{:S(2)}) async-start(), calls=%async_computation.13 | async-start | bytes 2228224 | tf_op jit(solution)/shard_map/reduce_scatter | solution.py:18
  370.0 34.8 %copy-start.18 = (bf16[2,512,1024]{2,1,0:T(8,128)(2,1)S(1)}, bf16[2,512,1024]{2,1,0:T(8,128)(2,1)}, u32[]{:S(2)}) copy-start(bf16[2,512,1024]{2,1,0:T(8,128)(2,1)} %param.20) | copy-start | bytes 6291460
  370.0 191.5 %reduce-scatter.8.cloned.1.call-start = ((), (), s32[]{:S(2)}) async-start(), calls=%async_computation.9 | async-start | bytes 2228224 | tf_op jit(solution)/shard_map/reduce_scatter | solution.py:18
  404.8 6.8 copy-start.8
  410.1 0.7 copy-start.15
  410.1 1.6 copy-start.2
  410.1 2.3 copy-start.7
  410.1 249.3 %all-gather.18.cloned.1.call-start = ((), (), s32[]{:S(2)}) async-start(), calls=%async_computation.14 | async-start | bytes 2228224 | tf_op jit(solution)/shard_map/all_gather | solution.py:14
  413.1 148.5 %copy-start.14 = (pred[64,512]{1,0:T(8,128)(4,1)S(1)}, pred[64,512]{1,0:T(8,128)(4,1)}, u32[]{:S(2)}) copy-start(pred[64,512]{1,0:T(8,128)(4,1)} %compare_and_fusion) | copy-start | bytes 98308
  489.7 78.4 %copy-start.6 = (f32[8,64,512]{2,1,0:T(8,128)}, f32[8,64,512]{2,1,0:T(8,128)S(1)}, u32[]{:S(2)}) copy-start(f32[8,64,512]{2,1,0:T(8,128)S(1)} %convolution_bitcast_fusion.1) | copy-start | bytes 3145732
  568.8 3.2 copy-start.25
  568.8 95.9 %all-gather.14.cloned.1.call-start = ((), (), s32[]{:S(2)}) async-start(), calls=%async_computation.10 | async-start | bytes 2228224 | tf_op jit(solution)/shard_map/all_gather | solution.py:14
  571.9 140.7 %reduce-scatter.14.cloned.1.call-start = ((), (), s32[]{:S(2)}) async-start(), calls=%async_computation.15 | async-start | bytes 2359296 | tf_op jit(solution)/shard_map/reduce_scatter | solution.py:27
  572.0 5.1 copy-start.13
  572.0 5.1 copy-start.24
  659.4 3.4 copy-start.9
  659.4 3.4 copy-start.3
  664.6 1.2 copy-start.22
  664.6 89.3 %reduce-scatter.10.cloned.1.call-start = ((), (), s32[]{:S(2)}) async-start(), calls=%async_computation.11 | async-start | bytes 2359296 | tf_op jit(solution)/shard_map/reduce_scatter | solution.py:27
  670.0 42.6 %copy-start.4 = (f32[128,512]{1,0:T(8,128)S(1)}, f32[128,512]{1,0:T(8,128)}, u32[]{:S(2)}) copy-start(f32[128,512]{1,0:T(8,128)} %reduce-scatter.6.cloned.1.call-done) | copy-start | bytes 786436
  670.0 84.0 %copy-start.10 = (bf16[128,512]{1,0:T(8,128)(2,1)S(1)}, bf16[128,512]{1,0:T(8,128)(2,1)}, u32[]{:S(2)}) copy-start(bf16[128,512]{1,0:T(8,128)(2,1)} %param.25) | copy-start | bytes 393220
  670.0 85.8 %copy-start.5 = (bf16[1024,128]{1,0:T(8,128)(2,1)S(1)}, bf16[1024,128]{1,0:T(8,128)(2,1)}, u32[]{:S(2)}) copy-start(bf16[1024,128]{1,0:T(8,128)(2,1)} %get-tuple-element.6) | copy-start | bytes 786436
  670.0 121.9 %all-gather.20.cloned.1.call-start = ((), (), s32[]{:S(2)}) async-start(), calls=%async_computation.16 | async-start | bytes 1179648 | tf_op jit(solution)/shard_map/all_gather | solution.py:10
  755.8 2.9 copy-start.20
  755.8 2.9 copy-start.23
  758.7 2.3 copy-start.19
  791.9 8.3 %copy-start.1 = (bf16[3,512,1024]{2,1,0:T(8,128)(2,1)S(1)}, bf16[3,512,1024]{2,1,0:T(8,128)(2,1)}, u32[]{:S(2)}) copy-start(bf16[3,512,1024]{2,1,0:T(8,128)(2,1)} %param.15) | copy-start | bytes 9437188
Sparse Core Ops, SparseCore 0:
  9.7 46.8 all-gather.7
  78.6 141.8 all-reduce.7
  223.5 60.6 all-gather.9
  292.8 35.3 reduce-scatter.5
  329.8 36.3 all-gather.15
  368.4 36.3 all-gather.11
  408.9 75.9 reduce-scatter.11
  488.8 72.7 reduce-scatter.7
  568.9 47.0 all-gather.17
  618.8 44.9 all-gather.13
  666.9 45.6 reduce-scatter.13
  715.5 38.3 reduce-scatter.9
  756.2 35.5 all-gather.19
where the time goes:
time: 808 us; the launch traced here: 807 us
  waiting for transfers between devices  471 us (58%)
  blocking collectives  220 us (27%)
  matrix products  72.7 us (9%)
  local copies, waits for them, and re-layouts  20.4 us (3%)
  between operations  14.9 us (2%)
    psum x4, blocking collectives, totals_tensor(): return lax.psum(values, 'tensor')  220 us
    unnamed x14, waiting for transfers between devices  142 us
    all_gather x4, waiting for transfers between devices, gather_groups(): return lax.all_gather(values, ('group', 'seq'), axis=0, tiled=True)  112 us
    reduce_scatter x3, waiting for transfers between devices, partial_groups(): lax.psum_scatter(builder(jnp.int32(0), row_count * lax.axis_size(('group'...  84.1 us
    reduce_scatter x2, waiting for transfers between devices, partial_tensor(): lax.psum_scatter(builder(jnp.int32(0), row_count * lax.axis_size('tensor'...  71.9 us
    all_gather x3, waiting for transfers between devices, gather_tensor(): return lax.all_gather(values, 'tensor', axis=0, tiled=True)  61.4 us
  transfers between devices with their start and end apart: 13, of which 10 were waited for; matrix products, arithmetic and copies ran while one was open for 6% of the time, Pallas kernels for 0%

commit v1 on v0

--- a/solution.py
+++ b/solution.py
@@ -1,9 +1,332 @@
+import functools
+
 import jax
 import jax.numpy as jnp
 from jax import lax
+from jax.experimental import pallas as pl
+from jax.experimental.pallas import tpu as pltpu
 from jax.sharding import PartitionSpec as P
 
 epsilon = 1e-05
+F32 = jnp.float32
+BF16 = jnp.bfloat16
+NEAR = (1, 3, 2)
+VMEM_LIMIT = 60 * 2**20
+
+
+def rem(value, count):
+    return lax.rem(value, jnp.int32(count))
+
+
+def group_of(z):
+    return rem(z, 2) * 2 + lax.div(z, jnp.int32(2))
+
+
+class Place:
+    def __init__(self):
+        self.t = lax.axis_index("tensor")
+        seq = lax.axis_index("seq")
+        self.x, self.y = rem(self.t, 4), lax.div(self.t, jnp.int32(4))
+        self.z = lax.div(seq, jnp.int32(2)) * 2 + lax.axis_index("group")
+        self.c = rem(seq, 2)
+
+    def at(self, x=None, y=None, z=None, c=None):
+        x = self.x if x is None else x
+        y = self.y if y is None else y
+        z = self.z if z is None else z
+        c = self.c if c is None else c
+        return (rem(z, 2), y * 4 + x, lax.div(z, jnp.int32(2)) * 2 + c)
+
+    def to_x(self, d):
+        return self.at(x=rem(self.x + d, 4))
+
+    def to_y(self, d):
+        return self.at(y=rem(self.y + d, 4))
+
+    def to_z(self, d):
+        return self.at(z=rem(self.z + d, 4))
+
+    def sibling(self):
+        return self.at(c=1 - self.c)
+
+
+def greet(devices):
+    barrier = pltpu.get_barrier_semaphore()
+    for device in devices:
+        pl.semaphore_signal(barrier, inc=1, device_id=device, device_id_type=pl.DeviceIdType.MESH)
+    pl.semaphore_wait(barrier, len(devices))
+
+
+def remote(src, dst, send, recv, device):
+    return pltpu.make_async_remote_copy(
+        src_ref=src,
+        dst_ref=dst,
+        send_sem=send,
+        recv_sem=recv,
+        device_id=device,
+        device_id_type=pl.DeviceIdType.MESH,
+    )
+
+
+def rows(first, count):
+    return pl.ds(pl.multiple_of(first, count), count)
+
+
+def line_partners(place):
+    return (
+        [place.to_x(d) for d in NEAR]
+        + [place.to_y(d) for d in NEAR]
+        + [place.to_z(d) for d in NEAR]
+        + [place.sibling()]
+    )
+
+
+def features_kernel(
+    ctx, resid, wt, wj, joined, feats,
+    ca, sb, rx, ry, s0, s1, r2x, r2y, fa, js, jx, j2, jz,
+    s_z, r_z, s_c, r_c, s_x, r_x, s_y, r_y, s_2x, r_2x, s_2y, r_2y,
+    s_f1, r_f1, s_f2, r_f2, s_jx, r_jx, s_jz, r_jz, s_out,
+):
+    me = Place()
+    x, y, z, c = me.x, me.y, me.z, me.c
+    sib = me.sibling()
+    group = [group_of(rem(z + e, 4)) for e in range(4)]
+    half = rows(c * 128, 128)
+    mine = rows(x * 64, 64)
+    greet(line_partners(me))
+    sends = []
+
+    def send(src, dst, ss, rs, device):
+        copy = remote(src, dst, ss, rs, device)
+        copy.start()
+        sends.append(copy)
+
+    def arrived(dst, rs):
+        remote(dst, dst, s_c.at[0], rs, sib).wait_recv()
+
+    send(ctx, ca.at[group[0], :, half, :], s_c.at[0], r_c.at[0], sib)
+    for d in NEAR:
+        send(ctx, ca.at[group[0], :, half, :], s_z.at[d - 1], r_z.at[3 - d], me.to_z(d))
+    ca[group[0], :, half, :] = ctx[...]
+
+    def target(e):
+        def level(l, carry):
+            for j in range(4):
+                part = jnp.dot(
+                    ca[group[e], l], wt[l, :, j * 256 : (j + 1) * 256], preferred_element_type=F32
+                )
+                sb[j // 2, e, l, :, (j % 2) * 256 : (j % 2 + 1) * 256] = part.astype(BF16)
+            return carry
+
+        lax.fori_loop(0, 3, level, 0)
+        for d in NEAR:
+            to = rem(x + d, 4)
+            send(sb.at[0, e, :, rows(to * 64, 64), :], rx.at[e, 3 - d], s_x.at[e, d - 1], r_x.at[e, 3 - d], me.at(x=to))
+        slot = rem(y - group[e] + 4, 4)
+
+        @pl.when(slot != 0)
+        def _():
+            remote(sb.at[1, e], ry.at[slot - 1], s_y.at[e], r_y.at[slot - 1], me.at(y=group[e])).start()
+
+    def collect_x(e):
+        for d in NEAR:
+            arrived(rx.at[e, d - 1], r_x.at[e, d - 1])
+
+        def level(l, carry):
+            total = sb[0, e, l, mine, :].astype(F32)
+            for d in range(3):
+                total = total + rx[e, d, l].astype(F32)
+            s0[e, l] = total.astype(BF16)
+            return carry
+
+        lax.fori_loop(0, 3, level, 0)
+        slot = rem(y - group[e] + 4, 4)
+
+        @pl.when(slot != 0)
+        def _():
+            remote(s0.at[e], r2x.at[slot - 1], s_2x.at[e], r_2x.at[slot - 1], me.at(y=group[e])).start()
+
+    other = rows((1 - c) * 128, 128)
+
+    def context_in(e):
+        if e:
+            arrived(ca.at[group[e], :, half, :], r_z.at[e - 1])
+            send(ca.at[group[e], :, half, :], ca.at[group[e], :, half, :], s_c.at[e], r_c.at[e], sib)
+        arrived(ca.at[group[e], :, other, :], r_c.at[e])
+
+    for e in (0, 1, 3):
+        context_in(e)
+        target(e)
+    collect_x(0)
+    context_in(2)
+    target(2)
+    for e in (1, 3, 2):
+        collect_x(e)
+    own = rem(group_of(y) - z + 4, 4)
+    for d in NEAR:
+        arrived(ry.at[d - 1], r_y.at[d - 1])
+
+    def fold(i, carry):
+        l, part = lax.div(i, jnp.int32(4)), rows(rem(i, 4) * 64, 64)
+        total = sb[1, own, l, part, :].astype(F32)
+        for d in range(3):
+            total = total + ry[d, l, part, :].astype(F32)
+        s1[l, part, :] = total.astype(BF16)
+        return carry
+
+    lax.fori_loop(0, 12, fold, 0)
+    for d in NEAR:
+        to = rem(x + d, 4)
+        send(s1.at[:, rows(to * 64, 64), :], r2y.at[3 - d], s_2y.at[d - 1], r_2y.at[3 - d], me.at(x=to))
+    for d in NEAR:
+        arrived(r2x.at[d - 1], r_2x.at[d - 1])
+
+    def finish(h, part, got):
+        def level(l, carry):
+            total = part(l).astype(F32)
+            for d in range(3):
+                total = total + got[d, l].astype(F32)
+            fa[h, y, l, mine, :] = (resid[l, :, h * 512 : (h + 1) * 512].astype(F32) + total).astype(BF16)
+            return carry
+
+        lax.fori_loop(0, 3, level, 0)
+
+    def block(h, q, p):
+        return fa.at[h, q, :, rows(p * 64, 64), :]
+
+    def spread_x(h, q, p, ss, rs):
+        for d in NEAR:
+            send(block(h, q, p), block(h, q, p), ss(d - 1), rs(3 - d), me.to_x(d))
+
+    def spread_y(h, q, p, ss, rs):
+        for d in NEAR:
+            send(block(h, q, p), block(h, q, p), ss(d - 1), rs(3 - d), me.to_y(d))
+
+    finish(0, lambda l: s0[own, l], r2x)
+    spread_x(0, y, x, lambda i: s_f1.at[0, i], lambda i: r_f1.at[0, i])
+    spread_y(0, y, x, lambda i: s_f2.at[0, i, 0], lambda i: r_f2.at[0, i, 0])
+    for d in NEAR:
+        arrived(r2y.at[d - 1], r_2y.at[d - 1])
+    finish(1, lambda l: s1[l, mine, :], r2y)
+    spread_y(1, y, x, lambda i: s_f1.at[1, i], lambda i: r_f1.at[1, i])
+    spread_x(1, y, x, lambda i: s_f2.at[1, i, 0], lambda i: r_f2.at[1, i, 0])
+    for e in NEAR:
+        p, q = rem(x + e, 4), rem(y + e, 4)
+        arrived(block(0, y, p), r_f1.at[0, e - 1])
+        spread_y(0, y, p, lambda i: s_f2.at[0, i, e], lambda i: r_f2.at[0, i, e])
+        arrived(block(1, q, x), r_f1.at[1, e - 1])
+        spread_x(1, q, x, lambda i: s_f2.at[1, i, e], lambda i: r_f2.at[1, i, e])
+
+    def join(e):
+        q = rem(y + e, 4)
+        if e:
+            for p in range(4):
+                arrived(block(0, q, rem(x + p, 4)), r_f2.at[0, e - 1, p])
+        for p in NEAR:
+            arrived(block(1, q, rem(x + p, 4)), r_f2.at[1, p - 1, e])
+        for h in range(2):
+            pltpu.make_async_copy(fa.at[h, q], feats.at[h, q], s_out.at[h, e]).start()
+        for j in range(2):
+            columns = slice(j * 256, (j + 1) * 256)
+            total = jnp.zeros((256, 256), F32)
+            for l in range(3):
+                for h in range(2):
+                    total = total + jnp.dot(
+                        fa[h, q, l], wj[l, h * 512 : (h + 1) * 512, columns], preferred_element_type=F32
+                    )
+            js[e, :, columns] = total.astype(BF16)
+        send(js.at[e, other, :], jx.at[e], s_jx.at[e], r_jx.at[e], sib)
+
+    def pair(e):
+        q = rem(y + e, 4)
+        arrived(jx.at[e], r_jx.at[e])
+        j2[e] = (js[e, half, :].astype(F32) + jx[e].astype(F32)).astype(BF16)
+        to = group_of(q)
+        slot = rem(z - to + 4, 4)
+
+        @pl.when(slot != 0)
+        def _():
+            remote(j2.at[e], jz.at[slot - 1], s_jz.at[e], r_jz.at[slot - 1], me.at(z=to)).start()
+
+    join(0)
+    join(1)
+    pair(0)
+    join(3)
+    pair(1)
+    join(2)
+    pair(3)
+    pair(2)
+    for d in NEAR:
+        arrived(jz.at[d - 1], r_jz.at[d - 1])
+    kept = rem(group_of(z) - y + 4, 4)
+    total = j2[kept].astype(F32)
+    for d in range(3):
+        total = total + jz[d].astype(F32)
+    joined[...] = total
+
+    for copy in sends:
+        copy.wait_send()
+    for e in range(4):
+
+        @pl.when(rem(y - group[e] + 4, 4) != 0)
+        def _():
+            remote(sb.at[1, e], ry.at[0], s_y.at[e], r_y.at[0], sib).wait_send()
+            remote(s0.at[e], r2x.at[0], s_2x.at[e], r_2x.at[0], sib).wait_send()
+
+        @pl.when(group_of(rem(y + e, 4)) != z)
+        def _():
+            remote(j2.at[e], jz.at[0], s_jz.at[e], r_jz.at[0], sib).wait_send()
+
+        for h in range(2):
+            q = rem(y + e, 4)
+            pltpu.make_async_copy(fa.at[h, q], feats.at[h, q], s_out.at[h, e]).wait()
+
+
+def vmem(*shape, dtype=BF16):
+    return pltpu.VMEM(shape, dtype)
+
+
+def dma(*shape):
+    return pltpu.SemaphoreType.DMA(shape)
+
+
+IN_VMEM = pl.BlockSpec(memory_space=pltpu.VMEM)
+ANYWHERE = pl.BlockSpec(memory_space=pl.ANY)
+
+
+def features_call(ctx, resid, wt, wj):
+    return pl.pallas_call(
+        features_kernel,
+        name="features",
+        out_shape=(
+            jax.ShapeDtypeStruct((128, 512), F32),
+            jax.ShapeDtypeStruct((2, 4, 3, 256, 512), BF16),
+        ),
+        in_specs=[IN_VMEM] * 4,
+        out_specs=(IN_VMEM, ANYWHERE),
+        scratch_shapes=[
+            vmem(4, 3, 256, 512),
+            vmem(2, 4, 3, 256, 512),
+            vmem(4, 3, 3, 64, 512),
+            vmem(3, 3, 256, 512),
+            vmem(4, 3, 64, 512),
+            vmem(3, 256, 512),
+            vmem(3, 3, 64, 512),
+            vmem(3, 3, 64, 512),
+            vmem(2, 4, 3, 256, 512),
+            vmem(4, 256, 512),
+            vmem(4, 128, 512),
+            vmem(4, 128, 512),
+            vmem(3, 128, 512),
+            dma(3), dma(3), dma(4), dma(4), dma(4, 3), dma(4, 3), dma(4), dma(3),
+            dma(4), dma(3), dma(3), dma(3),
+            dma(2, 3), dma(2, 3), dma(2, 3, 4), dma(2, 3, 4), dma(4), dma(4), dma(4), dma(3), dma(2, 4),
+        ],
+        compiler_params=pltpu.CompilerParams(
+            collective_id=0, has_side_effects=True, vmem_limit_bytes=VMEM_LIMIT
+        ),
+        cost_estimate=pl.CostEstimate(flops=6500000000, bytes_accessed=14000000, transcendentals=0),
+    )(ctx, resid, wt, wj)
 
 
 def gather_groups(values):
@@ -62,21 +385,9 @@
     group_heads = query_w.shape[2] // head_dim
     seq_len = segment_ids.shape[1]
     score_scale = head_dim ** (-0.5)
-    context_all = gather_groups(context)
-
-    def target_term(first_row, row_count):
-        return jnp.einsum(
-            "tlk,lkm->tlm", context_all, target_out_w, preferred_element_type=jnp.float32
-        )
-
-    level_part = partial_tensor(target_term, tensor_rows)
-    features = (resid_in.astype(jnp.float32) + level_part).astype(jnp.bfloat16)
-    features_all = gather_tensor(features)
-
-    def join_term(first_row, row_count):
-        return jnp.einsum("tlk,lkm->tm", features_all, join_w, preferred_element_type=jnp.float32)
-
-    joined = partial_groups(join_term, group_rows)
+    joined, feats = features_call(
+        context.transpose(1, 0, 2), resid_in.transpose(1, 0, 2), target_out_w, join_w
+    )
     embed_float = embedded.astype(jnp.float32)
     joined_squares, embed_squares = totals_tensor(
         (jnp.sum(joined * joined, -1), jnp.sum(embed_float * embed_float, -1))
@@ -195,8 +506,12 @@
     )
     joined_grad_all = gather_groups(joined_grad.astype(jnp.bfloat16))
     grad_join = jnp.einsum(
-        "tlk,tm->lkm", features_all, joined_grad_all, preferred_element_type=jnp.float32
+        "hqltk,qtm->lhkm",
+        feats,
+        joined_grad_all.reshape(4, 256, -1),
+        preferred_element_type=jnp.float32,
     ).astype(jnp.bfloat16)
+    grad_join = grad_join.reshape(join_w.shape)
     return (draft_hidden, grad_join, grad_query, grad_key, grad_value, grad_out)
 
 

time: 808 us -> 633 us (0.78)
  waiting for transfers between devices: 471 us -> 186 us
  Pallas kernels: 0 us -> 134 us
  local copies, waits for them, and re-layouts: 20.4 us -> 5.95 us
  matrix products: 72.7 us -> 60.8 us
    unnamed x14 -> x9, waiting for transfers between devices: 142 us -> 0.81 us
    pallas_call x0 -> x1, Pallas kernels: none -> 134 us  [features_call(): pl.pallas_call(features_kernel, name='features', out_shape=(jax.ShapeDtyp...]
    all_gather x3 -> x2, waiting for transfers between devices: 61.4 us -> 0.02 us  [gather_tensor(): return lax.all_gather(values, 'tensor', axis=0, tiled=True)]
    all_gather x4 -> x3, waiting for transfers between devices: 112 us -> 65.3 us  [gather_groups(): return lax.all_gather(values, ('group', 'seq'), axis=0, tiled=True)]
    reduce_scatter x3 -> x2, waiting for transfers between devices: 84.1 us -> 50.6 us  [partial_groups(): lax.psum_scatter(builder(jnp.int32(0), row_count * lax.axis_size(('group'...]
    dot_general x3 -> x1, matrix products: 24.3 us -> 6.58 us  [local(): jnp.einsum('hqltk,qtm->lhkm', feats, joined_grad_all.reshape(4, 256, -1),...]
    convert_element_type x1, local copies, waits for them, and re-layouts: 14.4 us -> 2.05 us  [local(): grad_join = jnp.einsum('hqltk,qtm->lhkm', feats, joined_grad_all.reshape(...]
  transfers between devices with their start and end apart: 13 -> 9, of which waited for: 10 -> 5; matrix products, arithmetic and copies ran while one was open for 6% -> 9% of each run, Pallas kernels for 0% -> 21%
where the time goes in v1:
time: 633 us; the launch traced here: 632 us
  blocking collectives  221 us (35%)
  waiting for transfers between devices  186 us (29%)
  Pallas kernels  134 us (21%)
  matrix products  60.8 us (10%)
  between operations  14 us (2%)
  other arithmetic  9.56 us (2%)
    psum x4, blocking collectives, totals_tensor(): return lax.psum(values, 'tensor')  221 us
    pallas_call x1, Pallas kernels, features_call(): pl.pallas_call(features_kernel, name='features', out_shape=(jax.ShapeDtyp...  134 us
    reduce_scatter x2, waiting for transfers between devices, partial_tensor(): lax.psum_scatter(builder(jnp.int32(0), row_count * lax.axis_size('tensor'...  69.4 us
    all_gather x3, waiting for transfers between devices, gather_groups(): return lax.all_gather(values, ('group', 'seq'), axis=0, tiled=True)  65.3 us
    reduce_scatter x2, waiting for transfers between devices, partial_groups(): lax.psum_scatter(builder(jnp.int32(0), row_count * lax.axis_size(('group'...  50.6 us
  transfers between devices with their start and end apart: 9, of which 5 were waited for; matrix products, arithmetic and copies ran while one was open for 9% of the time, Pallas kernels for 21%

profile of v1, /device:TPU:1, one launch (start us, length us, event | category | flops | bytes accessed | tf_op | source)
XLA Modules:
  0.0 632.0 jit_solution(13162259596980405234)
XLA Ops:
  7.2 0.0 all-gather.10.cloned.1.call-start
  7.2 0.7 all-gather.10.cloned.1.call-update
  7.9 0.0 all-gather.6.cloned.1.call-start
  8.0 0.7 convert_element_type.91
  8.6 0.7 convert_element_type.89
  9.3 1.0 fusion.30
  10.4 133.6 %features.1 = (f32[128,512]{1,0:T(8,128)}, bf16[2,4,3,256,512]{4,3,2,1,0:T(8,128)(2,1)}) custom-call(bf16[3,128,512]{2,1,0:T(8,128)(2,1)} %bitcast.182, bf16[3,64,1024]{2,1,0:T(8,128)(2,1)} %bitcast.183, bf16[3,512,1024]{2,1,0:T(8,128)(2,1)} %wt.1, bf16[3,1024,512]{2,1,0:T(8,128)(2,1)} %wj.1), custom_call_target="tpu_custom_call" | custom-call | flops 6499999744 | bytes 14000000 | tf_op jit(solution)/shard_map/features/pallas_call | solution.py:298
  144.0 1.1 multiply_reduce_fusion.2
  145.1 36.2 %all-reduce.2 = (f32[128]{0:T(128)S(1)}, f32[128]{0:T(128)S(1)}) all-reduce(f32[128]{0:T(128)S(1)} %multiply_reduce_fusion.2, f32[128]{0:T(128)S(1)} %fusion.30), channel_id=1, replica_groups=mesh['group'=2,'tensor'=16,'seq'=4] {'tensor'}, use_global_device_ids=true, to_apply=%region_3.0 | all-reduce | flops 256 | bytes 2048 | tf_op jit(solution)/shard_map/psum | solution.py:359
  181.3 0.1 fusion.40
  181.4 1.0 fusion.37
  182.5 0.7 pad_maximum_fusion
  183.2 0.0 reduce-scatter.9.cloned.1.call-start
  183.3 0.0 all-gather.10.cloned.1.call-done
  183.3 3.8 convolution_convert_fusion
  187.2 0.0 reduce-scatter.9.cloned.1.call-update
  187.2 0.0 reduce-scatter.5.cloned.1.call-start
  187.2 38.8 %all-gather.6.cloned.1.call-done = bf16[1024,2,512]{2,0,1:T(8,128)(2,1)} async-done(((bf16[128,2,512]{2,0,1:T(8,128)(2,1)}), bf16[1024,2,512]{2,0,1:T(8,128)(2,1)}) %all-gather.6.cloned.1.call-update) | async-done | bytes 2097168 | tf_op jit(solution)/shard_map/all_gather | solution.py:333
  226.0 5.3 bitcast_convert_fusion.1
  231.3 0.0 all-gather.12.cloned.1.call-start
  231.4 0.6 copy-done.13
  232.0 0.1 dynamic_slice.13
  232.1 0.1 dynamic_slice.14
  232.1 0.7 compare_and_fusion
  232.8 0.1 copy-done.1
  232.9 1.5 convolution_bitcast_fusion.1
  234.4 1.5 convolution_bitcast_fusion.2
  235.9 75.7 %all-reduce.5 = (bf16[1024,128]{1,0:T(8,128)(2,1)S(1)}, bf16[1024,128]{1,0:T(8,128)(2,1)}) all-reduce(f32[1024,128]{1,0:T(8,128)} %convolution_bitcast_fusion.2, f32[1024,128]{1,0:T(8,128)} %convolution_bitcast_fusion.1), channel_id=1, replica_groups=mesh['group'=2,'tensor'=16,'seq'=4] {'tensor'}, use_global_device_ids=true, to_apply=%region_4.0 | all-reduce | flops 262144 | bytes 1572864 | tf_op jit(solution)/shard_map/psum | solution.py:359
  311.6 2.2 convolution_bitcast_fusion
  313.8 69.4 %reduce-scatter.5.cloned.1.call-done = bf16[64,1024]{1,0:T(8,128)(2,1)} async-done(((bf16[1024,1024]{1,0:T(8,128)(2,1)}), bf16[64,1024]{1,0:T(8,128)(2,1)}) %reduce-scatter.5.cloned.1.call-update) | async-done | bytes 131088 | tf_op jit(solution)/shard_map/reduce_scatter | solution.py:341
  383.2 2.4 fusion.81
  385.5 4.8 fusion.19
  390.3 0.7 copy.82
  391.0 0.0 all-gather.8.cloned.1.call-start
  391.1 2.1 fusion.18
  393.2 0.7 copy.83
  393.9 0.0 all-gather.8.cloned.1.call-update
  393.9 0.2 reduce-scatter.11.cloned.1.call-start
  394.2 0.8 broadcast_in_dim.12.clone
  395.0 5.7 fusion.17
  400.7 0.8 broadcast_in_dim.12.clone.1
  401.6 2.8 fusion.16
  404.4 75.8 %all-reduce.6 = (bf16[1024,128]{1,0:T(8,128)(2,1)}, bf16[1024,128]{1,0:T(8,128)(2,1)S(1)}) all-reduce(f32[1024,128]{1,0:T(8,128)} %fusion.17, f32[1024,128]{1,0:T(8,128)} %fusion.16), channel_id=1, replica_groups=mesh['group'=2,'tensor'=16,'seq'=4] {'tensor'}, use_global_device_ids=true, to_apply=%region_12.13 | all-reduce | flops 262144 | bytes 1572864 | tf_op jit(solution)/shard_map/psum | solution.py:359
  480.1 2.8 fusion.46
  483.0 3.4 fusion.20
  486.4 1.8 add_add_fusion
  488.2 0.0 reduce-scatter.7.cloned.1.call-start
  488.2 0.0 all-gather.8.cloned.1.call-done
  488.2 4.2 fusion.93
  492.4 0.0 all-gather.14.cloned.1.call-start
  492.5 45.0 %reduce-scatter.11.cloned.1.call-done = f32[128,512]{1,0:T(8,128)} async-done(((f32[1024,512]{1,0:T(8,128)}), f32[128,512]{1,0:T(8,128)}) %reduce-scatter.11.cloned.1.call-update) | async-done | bytes 262160 | tf_op jit(solution)/shard_map/reduce_scatter | solution.py:350
  537.4 1.1 multiply_reduce_fusion.1
  538.5 33.6 %psum.55 = f32[128]{0:T(128)} all-reduce(f32[128]{0:T(128)S(1)} %multiply_reduce_fusion.1), channel_id=1, replica_groups=mesh['group'=2,'tensor'=16,'seq'=4] {'tensor'}, use_global_device_ids=true, to_apply=%region_16.17 | all-reduce | flops 128 | bytes 1024 | tf_op jit(solution)/shard_map/psum | solution.py:359
  572.1 0.7 broadcast_multiply_fusion
  572.8 5.6 reduce-scatter.7.cloned.1.call-done
  578.4 1.8 subtract_convert_fusion
  580.2 0.0 all-gather.14.cloned.1.call-update
  580.3 2.6 convolution_convert_fusion.3
  582.8 1.5 convolution_convert_fusion.2
  584.3 2.3 convolution_convert_fusion.1
  586.6 3.7 fusion.5
  590.3 26.5 %all-gather.14.cloned.1.call-done = bf16[1024,512]{1,0:T(8,128)(2,1)} async-done(((bf16[128,512]{1,0:T(8,128)(2,1)}), bf16[1024,512]{1,0:T(8,128)(2,1)}) %all-gather.14.cloned.1.call-update) | async-done | bytes 1048592 | tf_op jit(solution)/shard_map/all_gather | solution.py:333
  616.8 6.6 %fusion.2 = bf16[3,2,512,512]{3,2,0,1:T(8,128)(2,1)S(1)} fusion(bf16[4,256,512,1,1]{2,1,4,0,3:T(8,128)(2,1)} %bitcast.181, bf16[2,4,3,256,512]{4,3,2,1,0:T(8,128)(2,1)} %get-tuple-element.9), kind=kOutput, calls=%fused_computation.4 | convolution fusion | flops 3222798336 | bytes 10485760 | tf_op jit(solution)/shard_map/hqltk,qtm->lhkm/dot_general | solution.py:508
  623.4 2.1 copy.34
  (47 shorter events, 0.2 us)
Async XLA Ops:
  7.2 176.1 %copy-start = (bf16[1024,512]{1,0:T(8,128)(2,1)S(1)}, bf16[1024,512]{1,0:T(8,128)(2,1)}, u32[]{:S(2)}) copy-start(bf16[1024,512]{1,0:T(8,128)(2,1)} %param.23) | copy-start | bytes 3145732
  7.2 176.1 %all-gather.10.cloned.1.call-start = ((), (), s32[]{:S(2)}) async-start(), calls=%async_computation.8 | async-start | bytes 1179648 | tf_op jit(solution)/shard_map/all_gather | solution.py:333
  7.9 218.1 %all-gather.6.cloned.1.call-start = ((), (), s32[]{:S(2)}) async-start(), calls=%async_computation.4 | async-start | bytes 2359296 | tf_op jit(solution)/shard_map/all_gather | solution.py:333
  10.3 171.0 %copy-start.10 = (bf16[128,512]{1,0:T(8,128)(2,1)S(1)}, bf16[128,512]{1,0:T(8,128)(2,1)}, u32[]{:S(2)}) copy-start(bf16[128,512]{1,0:T(8,128)(2,1)} %param.16) | copy-start | bytes 393220
  183.2 128.4 %reduce-scatter.9.cloned.1.call-start = ((), (), s32[]{:S(2)}) async-start(), calls=%async_computation.9 | async-start | bytes 2228224 | tf_op jit(solution)/shard_map/reduce_scatter | solution.py:341
  187.1 38.8 %copy-start.14 = (bf16[2,512,1024]{2,1,0:T(8,128)(2,1)S(1)}, bf16[2,512,1024]{2,1,0:T(8,128)(2,1)}, u32[]{:S(2)}) copy-start(bf16[2,512,1024]{2,1,0:T(8,128)(2,1)} %param.20) | copy-start | bytes 6291460
  187.2 196.0 %reduce-scatter.5.cloned.1.call-start = ((), (), s32[]{:S(2)}) async-start(), calls=%async_computation.5 | async-start | bytes 2228224 | tf_op jit(solution)/shard_map/reduce_scatter | solution.py:341
  226.0 6.8 %copy-start.6 = (bf16[2,512,128]{2,1,0:T(8,128)(2,1)S(1)}, bf16[2,512,128]{2,1,0:T(8,128)(2,1)}, u32[]{:S(2)}) copy-start(bf16[2,512,128]{2,1,0:T(8,128)(2,1)} %param.21) | copy-start | bytes 786436
  231.3 0.7 copy-start.13
  231.3 1.6 copy-start.1
  231.3 251.7 %all-gather.12.cloned.1.call-start = ((), (), s32[]{:S(2)}) async-start(), calls=%async_computation.10 | async-start | bytes 2228224 | tf_op jit(solution)/shard_map/all_gather | solution.py:337
  232.0 2.4 copy-start.7
  234.4 148.8 %copy-start.12 = (pred[64,512]{1,0:T(8,128)(4,1)S(1)}, pred[64,512]{1,0:T(8,128)(4,1)}, u32[]{:S(2)}) copy-start(pred[64,512]{1,0:T(8,128)(4,1)} %compare_and_fusion) | copy-start | bytes 98308
  391.0 97.2 %all-gather.8.cloned.1.call-start = ((), (), s32[]{:S(2)}) async-start(), calls=%async_computation.6 | async-start | bytes 2228224 | tf_op jit(solution)/shard_map/all_gather | solution.py:337
  393.9 143.5 %reduce-scatter.11.cloned.1.call-start = ((), (), s32[]{:S(2)}) async-start(), calls=%async_computation.11 | async-start | bytes 2359296 | tf_op jit(solution)/shard_map/reduce_scatter | solution.py:350
  395.0 6.6 %copy-start.11 = (bf16[64,1024]{1,0:T(8,128)(2,1)S(1)}, bf16[64,1024]{1,0:T(8,128)(2,1)}, u32[]{:S(2)}) copy-start(bf16[64,1024]{1,0:T(8,128)(2,1)} %reduce-scatter.9.cloned.1.call-done) | copy-start | bytes 393220
  395.0 6.6 %copy-start.18 = (bf16[1024,128]{1,0:T(8,128)(2,1)S(1)}, bf16[1024,128]{1,0:T(8,128)(2,1)}, u32[]{:S(2)}) copy-start(bf16[1024,128]{1,0:T(8,128)(2,1)} %get-tuple-element.13) | copy-start | bytes 786436
  480.1 6.2 copy-start.4
  483.0 3.4 copy-start.2
  483.0 3.4 copy-start.8
  488.2 90.2 %reduce-scatter.7.cloned.1.call-start = ((), (), s32[]{:S(2)}) async-start(), calls=%async_computation.7 | async-start | bytes 2359296 | tf_op jit(solution)/shard_map/reduce_scatter | solution.py:350
  492.4 45.0 %copy-start.3 = (f32[128,512]{1,0:T(8,128)S(1)}, f32[128,512]{1,0:T(8,128)}, u32[]{:S(2)}) copy-start(f32[128,512]{1,0:T(8,128)} %get-tuple-element.8) | copy-start | bytes 786436
  492.4 86.0 %copy-start.9 = (bf16[128,512]{1,0:T(8,128)(2,1)S(1)}, bf16[128,512]{1,0:T(8,128)(2,1)}, u32[]{:S(2)}) copy-start(bf16[128,512]{1,0:T(8,128)(2,1)} %param.25) | copy-start | bytes 393220
  492.4 124.4 %all-gather.14.cloned.1.call-start = ((), (), s32[]{:S(2)}) async-start(), calls=%async_computation.12 | async-start | bytes 1179648 | tf_op jit(solution)/shard_map/all_gather | solution.py:333
  580.2 2.6 copy-start.5
  580.2 4.1 copy-start.16
  580.3 4.0 copy-start.17
  584.3 2.3 copy-start.15
Sparse Core Ops, SparseCore 0:
  9.7 45.0 all-gather.9
  183.4 42.5 all-gather.5
  229.8 75.7 reduce-scatter.8
  309.7 73.4 reduce-scatter.4
  391.2 47.0 all-gather.11
  440.9 46.7 all-gather.7
  490.7 46.7 reduce-scatter.10
  540.4 37.9 reduce-scatter.6
  580.6 36.1 all-gather.13

commit v2 on v1

--- a/solution.py
+++ b/solution.py
@@ -81,11 +81,251 @@
     )
 
 
+def vmem(*shape, dtype=BF16):
+    return pltpu.VMEM(shape, dtype)
+
+
+def dma(*shape):
+    return pltpu.SemaphoreType.DMA(shape)
+
+
+IN_VMEM = pl.BlockSpec(memory_space=pltpu.VMEM)
+ANYWHERE = pl.BlockSpec(memory_space=pl.ANY)
+
+
+def nt(a, b):
+    return lax.dot_general(a, b, (((1,), (1,)), ((), ())), preferred_element_type=F32)
+
+
+def tn(a, b):
+    return lax.dot_general(a, b, (((0,), (0,)), ((), ())), preferred_element_type=F32)
+
+
+def dot(a, b):
+    return jnp.dot(a, b, preferred_element_type=F32)
+
+
+class Mover:
+    def __init__(self, me, dummy):
+        self.me, self.dummy, self.sends, self.guarded = me, dummy, [], []
+
+    def send(self, src, dst, ss, rs, device, when=None):
+        copy = remote(src, dst, ss, rs, device)
+        if when is None:
+            copy.start()
+            self.sends.append(copy)
+        else:
+            pl.when(when)(copy.start)
+            self.guarded.append((when, src, ss))
+
+    def arrived(self, dst, rs):
+        remote(dst, dst, self.dummy, rs, self.me.sibling()).wait_recv()
+
+    def drain(self):
+        for copy in self.sends:
+            copy.wait_send()
+        for when, src, ss in self.guarded:
+            pl.when(when)(remote(src, src, ss, self.dummy, self.me.sibling()).wait_send)
+
+
+class GatherG:
+    def __init__(self, mv, block, s_z, r_z, s_c, r_c):
+        me = mv.me
+        self.mv, self.block, self.sems = mv, block, (s_z, r_z, s_c, r_c)
+        self.group = [group_of(rem(me.z + e, 4)) for e in range(4)]
+
+    def to_sibling(self, e, src=None):
+        me, (_, _, s_c, r_c) = self.mv.me, self.sems
+        place = self.block(self.group[e], me.c)
+        self.mv.send(place if src is None else src, place, s_c.at[e], r_c.at[e], me.sibling())
+
+    def along_z(self, src=None):
+        me, (s_z, r_z, _, _) = self.mv.me, self.sems
+        place = self.block(self.group[0], me.c)
+        for d in NEAR:
+            self.mv.send(place if src is None else src, place, s_z.at[d - 1], r_z.at[3 - d], me.to_z(d))
+
+    def forward(self, e):
+        me, (_, r_z, _, _) = self.mv.me, self.sems
+        self.mv.arrived(self.block(self.group[e], me.c), r_z.at[e - 1])
+        self.to_sibling(e)
+
+    def whole(self, e):
+        me, (_, _, _, r_c) = self.mv.me, self.sems
+        self.mv.arrived(self.block(self.group[e], 1 - me.c), r_c.at[e])
+
+
+class GatherT:
+    def __init__(self, mv, block, s_1, r_1, s_2, r_2):
+        self.mv, self.block, self.sems = mv, block, (s_1, r_1, s_2, r_2)
+
+    def spread(self, along_x, h, q, p, ss, rs):
+        me = self.mv.me
+        for d in NEAR:
+            to = me.to_x(d) if along_x else me.to_y(d)
+            self.mv.send(self.block(h, q, p), self.block(h, q, p), ss(d - 1), rs(3 - d), to)
+
+    def start(self, h):
+        me, (s_1, r_1, s_2, r_2) = self.mv.me, self.sems
+        self.spread(h == 0, h, me.y, me.x, lambda i: s_1.at[h, i], lambda i: r_1.at[h, i])
+        self.spread(h == 1, h, me.y, me.x, lambda i: s_2.at[h, i, 0], lambda i: r_2.at[h, i, 0])
+
+    def forward(self):
+        me, (s_1, r_1, s_2, r_2) = self.mv.me, self.sems
+        for e in NEAR:
+            p, q = rem(me.x + e, 4), rem(me.y + e, 4)
+            self.mv.arrived(self.block(0, me.y, p), r_1.at[0, e - 1])
+            self.spread(False, 0, me.y, p, lambda i: s_2.at[0, i, e], lambda i: r_2.at[0, i, e])
+            self.mv.arrived(self.block(1, q, me.x), r_1.at[1, e - 1])
+            self.spread(True, 1, q, me.x, lambda i: s_2.at[1, i, e], lambda i: r_2.at[1, i, e])
+
+    def group(self, e):
+        me, (_, _, _, r_2) = self.mv.me, self.sems
+        q = rem(me.y + e, 4)
+        if e:
+            for p in range(4):
+                self.mv.arrived(self.block(0, q, rem(me.x + p, 4)), r_2.at[0, e - 1, p])
+        for p in NEAR:
+            self.mv.arrived(self.block(1, q, rem(me.x + p, 4)), r_2.at[1, p - 1, e])
+        return q
+
+
+class SumG:
+    def __init__(self, mv, js, jx, j2, jz, s_x, r_x, s_z, r_z):
+        self.mv, self.refs, self.sems = mv, (js, jx, j2, jz), (s_x, r_x, s_z, r_z)
+
+    def swap(self, e):
+        (js, jx, _, _), (s_x, r_x, _, _), me = self.refs, self.sems, self.mv.me
+        self.mv.send(js.at[e, rows((1 - me.c) * 128, 128), :], jx.at[e], s_x.at[e], r_x.at[e], me.sibling())
+
+    def pair(self, e):
+        (js, jx, j2, jz), (_, r_x, s_z, r_z), me = self.refs, self.sems, self.mv.me
+        self.mv.arrived(jx.at[e], r_x.at[e])
+        j2[e] = (js[e, rows(me.c * 128, 128), :].astype(F32) + jx[e].astype(F32)).astype(BF16)
+        to = group_of(rem(me.y + e, 4))
+        slot = rem(me.z - to + 4, 4)
+        at = jnp.maximum(slot - 1, 0)
+        self.mv.send(j2.at[e], jz.at[at], s_z.at[e], r_z.at[at], me.at(z=to), when=slot != 0)
+
+    def total(self):
+        (_, _, j2, jz), (_, _, _, r_z), me = self.refs, self.sems, self.mv.me
+        for d in NEAR:
+            self.mv.arrived(jz.at[d - 1], r_z.at[d - 1])
+        total = j2[rem(group_of(me.z) - me.y + 4, 4)].astype(F32)
+        for d in range(3):
+            total = total + jz[d].astype(F32)
+        return total
+
+    @staticmethod
+    def scratch():
+        return [vmem(4, 256, 512), vmem(4, 128, 512), vmem(4, 128, 512), vmem(3, 128, 512), dma(4), dma(4), dma(4), dma(3)]
+
+
+class SumT:
+    def __init__(self, mv, ps, rx, ry, s0, s1, r2x, r2y, *sems):
+        self.mv, self.ps, self.rx, self.ry, self.s0, self.s1, self.r2x, self.r2y = mv, ps, rx, ry, s0, s1, r2x, r2y
+        self.sems = sems
+
+    def issue(self, e):
+        mv, me = self.mv, self.mv.me
+        s_x, r_x, s_y, r_y = self.sems[:4]
+        for d in NEAR:
+            to = rem(me.x + d, 4)
+            mv.send(self.ps.at[0, e, rows(to * 64, 64), :], self.rx.at[e, 3 - d], s_x.at[e, d - 1], r_x.at[e, 3 - d], me.at(x=to))
+        if e:
+            mv.send(self.ps.at[1, e], self.ry.at[3 - e], s_y.at[e], r_y.at[3 - e], me.to_y(e))
+
+    def collect_x(self, e):
+        mv, me = self.mv, self.mv.me
+        r_x, s_2x, r_2x = self.sems[1], self.sems[4], self.sems[5]
+        for d in NEAR:
+            mv.arrived(self.rx.at[e, d - 1], r_x.at[e, d - 1])
+        total = self.ps[0, e, rows(me.x * 64, 64), :].astype(F32)
+        for d in range(3):
+            total = total + self.rx[e, d].astype(F32)
+        self.s0[e] = total.astype(BF16)
+        if e:
+            mv.send(self.s0.at[e], self.r2x.at[3 - e], s_2x.at[e], r_2x.at[3 - e], me.to_y(e))
+
+    def fold(self):
+        mv, me = self.mv, self.mv.me
+        r_y, s_2y, r_2y = self.sems[3], self.sems[6], self.sems[7]
+        for d in NEAR:
+            mv.arrived(self.ry.at[d - 1], r_y.at[d - 1])
+        for d in (2, 1, 3, 0):
+            to = rem(me.x + d, 4)
+            part = rows(to * 64, 64)
+            total = self.ps[1, 0, part, :].astype(F32)
+            for i in range(3):
+                total = total + self.ry[i, part, :].astype(F32)
+            self.s1[part, :] = total.astype(BF16)
+            if d:
+                mv.send(self.s1.at[part, :], self.r2y.at[3 - d], s_2y.at[d - 1], r_2y.at[3 - d], me.at(x=to))
+
+    def finish(self, h):
+        mv, me = self.mv, self.mv.me
+        got, sem = ((self.r2x, self.sems[5]), (self.r2y, self.sems[7]))[h]
+        for d in NEAR:
+            mv.arrived(got.at[d - 1], sem.at[d - 1])
+        total = (self.s0[0] if h == 0 else self.s1[rows(me.x * 64, 64), :]).astype(F32)
+        for d in range(3):
+            total = total + got[d].astype(F32)
+        return total.astype(BF16)
+
+    @staticmethod
+    def scratch(w):
+        return [
+            vmem(2, 4, 256, w), vmem(4, 3, 64, w), vmem(3, 256, w), vmem(4, 64, w), vmem(256, w), vmem(3, 64, w), vmem(3, 64, w),
+            dma(4, 3), dma(4, 3), dma(4), dma(3), dma(4), dma(3), dma(3), dma(3),
+        ]
+
+
+def lanes(column):
+    return jnp.broadcast_to(column, (128, 128)).T[0:8, :]
+
+
+def column(row):
+    return jnp.broadcast_to(row, (128, 128)).T[:, 0:1]
+
+
+class StatsT:
+    def __init__(self, mv, tiles, s_t, r_t):
+        self.mv, self.tiles, self.s_t, self.r_t = mv, tiles, s_t, r_t
+
+    def start(self, tile):
+        me = self.mv.me
+        self.tiles[0] = tile
+        for d in range(1, 16):
+            dx, dy = d % 4, d // 4
+            back = (4 - dx) % 4 + 4 * ((4 - dy) % 4)
+            to = me.at(x=rem(me.x + dx, 4), y=rem(me.y + dy, 4))
+            self.mv.send(self.tiles.at[0], self.tiles.at[back], self.s_t.at[d], self.r_t.at[back], to)
+
+    def total(self):
+        for d in range(1, 16):
+            self.mv.arrived(self.tiles.at[d], self.r_t.at[d])
+        total = self.tiles[0]
+        for d in range(1, 16):
+            total = total + self.tiles[d]
+        return total
+
+    @staticmethod
+    def scratch():
+        return [pltpu.VMEM((16, 8, 128), F32), dma(16), dma(16)]
+
+
+def take(refs, count):
+    out = refs[:count]
+    del refs[:count]
+    return out
+
+
 def features_kernel(
-    ctx, resid, wt, wj, joined, feats,
-    ca, sb, rx, ry, s0, s1, r2x, r2y, fa, js, jx, j2, jz,
+    ctx, resid, wt, wj, early, joined, feats, early_all,
+    ca, sb, rx, ry, s0, s1, r2x, r2y, fa, js, jx, j2, jz, ea,
     s_z, r_z, s_c, r_c, s_x, r_x, s_y, r_y, s_2x, r_2x, s_2y, r_2y,
     s_f1, r_f1, s_f2, r_f2, s_jx, r_jx, s_jz, r_jz, s_out,
+    s_ez, r_ez, s_ec, r_ec, s_early,
 ):
     me = Place()
     x, y, z, c = me.x, me.y, me.z, me.c
@@ -147,6 +387,8 @@
             remote(s0.at[e], r2x.at[slot - 1], s_2x.at[e], r_2x.at[slot - 1], me.at(y=group[e])).start()
 
     other = rows((1 - c) * 128, 128)
+    mv = Mover(me, s_c.at[0])
+    begin = GatherG(mv, lambda q, core: ea.at[:, q, rows(core * 128, 128), :], s_ez, r_ez, s_ec, r_ec)
 
     def context_in(e):
         if e:
@@ -157,11 +399,16 @@
     for e in (0, 1, 3):
         context_in(e)
         target(e)
+    ea[:, group[0], half, :] = early[...]
+    begin.to_sibling(0, early)
+    begin.along_z(early)
     collect_x(0)
     context_in(2)
     target(2)
     for e in (1, 3, 2):
         collect_x(e)
+    for e in NEAR:
+        begin.forward(e)
     own = rem(group_of(y) - z + 4, 4)
     for d in NEAR:
         arrived(ry.at[d - 1], r_y.at[d - 1])
@@ -180,6 +427,11 @@
         send(s1.at[:, rows(to * 64, 64), :], r2y.at[3 - d], s_2y.at[d - 1], r_2y.at[3 - d], me.at(x=to))
     for d in NEAR:
         arrived(r2x.at[d - 1], r_2x.at[d - 1])
+
+    for e in range(4):
+        begin.whole(e)
+    early_out = pltpu.make_async_copy(ea, early_all, s_early.at[0])
+    early_out.start()
 
     def finish(h, part, got):
         def level(l, carry):
@@ -264,6 +516,8 @@
         total = total + jz[d].astype(F32)
     joined[...] = total
 
+    mv.drain()
+    early_out.wait()
     for copy in sends:
         copy.wait_send()
     for e in range(4):
@@ -282,28 +536,17 @@
             pltpu.make_async_copy(fa.at[h, q], feats.at[h, q], s_out.at[h, e]).wait()
 
 
-def vmem(*shape, dtype=BF16):
-    return pltpu.VMEM(shape, dtype)
-
-
-def dma(*shape):
-    return pltpu.SemaphoreType.DMA(shape)
-
-
-IN_VMEM = pl.BlockSpec(memory_space=pltpu.VMEM)
-ANYWHERE = pl.BlockSpec(memory_space=pl.ANY)
-
-
-def features_call(ctx, resid, wt, wj):
+def features_call(ctx, resid, wt, wj, early):
     return pl.pallas_call(
         features_kernel,
         name="features",
         out_shape=(
             jax.ShapeDtypeStruct((128, 512), F32),
             jax.ShapeDtypeStruct((2, 4, 3, 256, 512), BF16),
+            jax.ShapeDtypeStruct((2, 4, 256, 512), BF16),
         ),
-        in_specs=[IN_VMEM] * 4,
-        out_specs=(IN_VMEM, ANYWHERE),
+        in_specs=[IN_VMEM] * 5,
+        out_specs=(IN_VMEM, ANYWHERE, ANYWHERE),
         scratch_shapes=[
             vmem(4, 3, 256, 512),
             vmem(2, 4, 3, 256, 512),
@@ -318,45 +561,300 @@
             vmem(4, 128, 512),
             vmem(4, 128, 512),
             vmem(3, 128, 512),
+            vmem(2, 4, 256, 512),
             dma(3), dma(3), dma(4), dma(4), dma(4, 3), dma(4, 3), dma(4), dma(3),
             dma(4), dma(3), dma(3), dma(3),
             dma(2, 3), dma(2, 3), dma(2, 3, 4), dma(2, 3, 4), dma(4), dma(4), dma(4), dma(3), dma(2, 4),
+            dma(3), dma(3), dma(4), dma(4), dma(1),
         ],
         compiler_params=pltpu.CompilerParams(
             collective_id=0, has_side_effects=True, vmem_limit_bytes=VMEM_LIMIT
         ),
-        cost_estimate=pl.CostEstimate(flops=6500000000, bytes_accessed=14000000, transcendentals=0),
-    )(ctx, resid, wt, wj)
-
-
-def gather_groups(values):
-    return lax.all_gather(values, ("group", "seq"), axis=0, tiled=True)
-
-
-def gather_tensor(values):
-    return lax.all_gather(values, "tensor", axis=0, tiled=True)
-
-
-def partial_tensor(builder, row_count):
-    return lax.psum_scatter(
-        builder(jnp.int32(0), row_count * lax.axis_size("tensor")).astype(jnp.bfloat16),
-        "tensor",
-        scatter_dimension=0,
-        tiled=True,
-    ).astype(jnp.float32)
-
-
-def partial_groups(builder, row_count):
-    return lax.psum_scatter(
-        builder(jnp.int32(0), row_count * lax.axis_size(("group", "seq"))),
-        ("group", "seq"),
-        scatter_dimension=0,
-        tiled=True,
+        cost_estimate=pl.CostEstimate(flops=6500000000, bytes_accessed=16000000, transcendentals=0),
+    )(ctx, resid, wt, wj, early)
+
+
+def draft_kernel(*refs):
+    refs = list(refs)
+    joined, early, own_early, wq, wk, wv, wo, gains, mask = take(refs, 9)
+    draft, xn_out, gq_out, at_out, jg_out = take(refs, 5)
+    xa, xn, rt, qh, gh, kw, vw, kg, kgot, gq, at, jg, pf = take(refs, 13)
+    s_loc, s_rt, r_rt, s_kv, r_kv, s_kg, r_kg = take(refs, 7)
+    me = Place()
+    x, y, z, c, t = me.x, me.y, me.z, me.c, me.t
+    mv = Mover(me, s_loc.at[0])
+    mine, half = rows(x * 64, 64), rows(c * 128, 128)
+    hidden_rows = GatherG(mv, lambda q, core: xa.at[q, rows(core * 128, 128), :], *take(refs, 4))
+    grad_rows = GatherG(mv, lambda q, core: jg.at[q, rows(core * 128, 128), :], *take(refs, 4))
+    stats = StatsT(mv, *take(refs, 3))
+    inner = StatsT(mv, *take(refs, 3))
+    back = SumT(mv, *take(refs, 15))
+    qkv = SumT(mv, *take(refs, 15))
+    hidden = SumG(mv, *take(refs, 8))
+    output = SumG(mv, *take(refs, 8))
+    ends = GatherT(mv, lambda h, q, p: gq.at[h, q, rows(p * 64, 64), :], *take(refs, 4))
+    attends = GatherT(mv, lambda h, q, p: at.at[h, q, rows(p * 64, 64), :], *take(refs, 4))
+    assert not refs
+    outs = []
+
+    def local_out(src, dst, i):
+        copy = pltpu.make_async_copy(src, dst, s_loc.at[1 + i])
+        copy.start()
+        outs.append(copy)
+
+    plane = [
+        me.at(x=rem(x + d % 4, 4), y=rem(y + d // 4, 4)) for d in range(1, 16)
+    ]
+    line = [me.at(z=rem(z + d % 4, 4), c=rem(c + d // 4, 2)) for d in range(1, 8)]
+    greet(plane + line)
+
+    q0 = group_of(z)
+    value = joined[...]
+    xa[q0, half, :] = value.astype(BF16)
+    hidden_rows.to_sibling(0)
+    hidden_rows.along_z()
+    first = lax.broadcasted_iota(jnp.int32, (8, 128), 0) == 0
+    embed_own = own_early[0].astype(F32)
+    stats.start(
+        jnp.where(
+            first,
+            lanes(jnp.sum(value * value, -1, keepdims=True)),
+            lanes(jnp.sum(embed_own * embed_own, -1, keepdims=True)),
+        )
     )
 
-
-def totals_tensor(values):
-    return lax.psum(values, "tensor")
+    def back_part(e):
+        q = rem(y + e, 4)
+        for j in range(4):
+            part = nt(early[1, q], wo[j * 256 : (j + 1) * 256, :])
+            back.ps[j // 2, e, :, (j % 2) * 256 : (j % 2 + 1) * 256] = part.astype(BF16)
+        back.issue(e)
+
+    back_part(2)
+    back_part(1)
+    for e in NEAR:
+        hidden_rows.forward(e)
+    sums = stats.total()
+    rate = lax.rsqrt(sums / 8192.0 + epsilon)
+    rt[2 * q0 + c] = rate
+    for d in range(1, 8):
+        dz, dc = d % 4, d // 4
+        back_at = (4 - dz) % 4 + 4 * dc
+        mv.send(rt.at[2 * q0 + c], rt.at[2 * q0 + c], s_rt.at[d], r_rt.at[back_at], line[d - 1])
+    back_part(3)
+    back_part(0)
+    for e in range(4):
+        hidden_rows.whole(e)
+    for d in range(1, 8):
+        there = 2 * group_of(rem(z + d % 4, 4)) + rem(c + d // 4, 2)
+        mv.arrived(rt.at[there], r_rt.at[d])
+    gain_e = gains[0:1, :].astype(F32)
+    gain_j = gains[1:2, :].astype(F32)
+
+    def qkv_part(e):
+        q = rem(y + e, 4)
+        for i in range(2):
+            part = slice(i * 128, (i + 1) * 128)
+            rates = rt[2 * q + i]
+            xn[0, q, part, :] = (early[0, q, part, :].astype(F32) * column(rates[1:2, :]) * gain_e).astype(BF16)
+            xn[1, q, part, :] = (xa[q, part, :].astype(F32) * column(rates[0:1, :]) * gain_j).astype(BF16)
+
+        def both(w, columns):
+            return (dot(xn[0, q], w[0, :, columns]) + dot(xn[1, q], w[1, :, columns])).astype(BF16)
+
+        for h, first_column, at_column, width in (
+            (0, 0, 0, 256), (0, 256, 256, 256), (0, 512, 512, 128), (1, 640, 0, 128), (1, 768, 128, 256),
+        ):
+            qkv.ps[h, e, :, at_column : at_column + width] = both(wq, slice(first_column, first_column + width))
+        qkv.ps[1, e, :, 384:512] = both(wk, slice(0, 128))
+        qkv.ps[1, e, :, 512:640] = both(wv, slice(0, 128))
+        qkv.issue(e)
+        for i in range(2):
+            local_out(xn.at[i, q], xn_out.at[i, q], 2 * e + i)
+
+    for e in (2, 1, 3, 0):
+        qkv_part(e)
+    for e in (2, 1, 3, 0):
+        back.collect_x(e)
+    back.fold()
+    for e in (2, 1, 3, 0):
+        qkv.collect_x(e)
+    qkv.fold()
+    for h in range(2):
+        got = back.finish(h)
+        for i in range(4):
+            gh[(4 * h + i) * 64 : (4 * h + i + 1) * 64, :] = got[:, i * 128 : (i + 1) * 128]
+
+    got = qkv.finish(1)
+    kw[0:64, :] = jnp.zeros((64, 128), BF16)
+    vw[0:64, :] = jnp.zeros((64, 128), BF16)
+    kw[192:256, :] = got[:, 384:512]
+    vw[192:256, :] = got[:, 512:640]
+    for i in range(1, 3):
+        after = rem(t + i, 16)
+        to = me.at(x=rem(after, 4), y=lax.div(after, jnp.int32(4)))
+        place = slice(192 - 64 * i, 256 - 64 * i)
+        mv.send(kw.at[192:256, :], kw.at[place, :], s_kv.at[0, i - 1], r_kv.at[0, i - 1], to)
+        mv.send(vw.at[192:256, :], vw.at[place, :], s_kv.at[1, i - 1], r_kv.at[1, i - 1], to)
+    for i in range(3):
+        qh[(5 + i) * 64 : (6 + i) * 64, :] = got[:, i * 128 : (i + 1) * 128]
+    got = qkv.finish(0)
+    for i in range(5):
+        qh[i * 64 : (i + 1) * 64, :] = got[:, i * 128 : (i + 1) * 128]
+    for i in range(1, 3):
+        place = slice(192 - 64 * i, 256 - 64 * i)
+        mv.arrived(kw.at[place, :], r_kv.at[0, i - 1])
+        mv.arrived(vw.at[place, :], r_kv.at[1, i - 1])
+
+    scale = 128.0**-0.5
+    allowed = jnp.concatenate([mask[...]] * 4, axis=0) > 0.5
+    for i in range(2):
+        part = slice(i * 256, (i + 1) * 256)
+        scores = jnp.where(allowed, nt(qh[part, :], kw[...]) * scale, -1e30)
+        powers = jnp.exp(scores - jnp.max(scores, -1, keepdims=True))
+        probs = powers / jnp.sum(powers, -1, keepdims=True)
+        low = probs.astype(BF16)
+        attended = dot(low, vw[...]).astype(BF16)
+        for j in range(4):
+            at[i, y, mine, j * 128 : (j + 1) * 128] = attended[j * 64 : (j + 1) * 64, :]
+        value_grad = tn(low, gh[part, :])
+        probs_grad = nt(gh[part, :], vw[...])
+        score_grad = probs * (probs_grad - jnp.sum(probs_grad * probs, -1, keepdims=True)) * scale
+        score_grad = score_grad.astype(BF16)
+        query_grad = dot(score_grad, kw[...]).astype(BF16)
+        for j in range(4):
+            head = 4 * i + j
+            h, at_head = (0, head) if head < 5 else (1, head - 5)
+            gq[h, y, mine, at_head * 128 : (at_head + 1) * 128] = query_grad[j * 64 : (j + 1) * 64, :]
+        key_grad = tn(score_grad, qh[part, :])
+        if i == 0:
+            kg[0, :, :] = key_grad
+            kg[1, :, :] = value_grad
+        else:
+            kg[0, :, :] = kg[0, :, :] + key_grad
+            kg[1, :, :] = kg[1, :, :] + value_grad
+    for i in range(1, 3):
+        before = rem(t + 16 - i, 16)
+        to = me.at(x=rem(before, 4), y=lax.div(before, jnp.int32(4)))
+        mv.send(kg.at[:, 192 - 64 * i : 256 - 64 * i, :], kgot.at[i - 1], s_kg.at[i - 1], r_kg.at[i - 1], to)
+    ends.start(0)
+    for i in range(2):
+        mv.arrived(kgot.at[i], r_kg.at[i])
+    for i in range(2):
+        total = kg[i, 192:256, :] + kgot[0, i] + kgot[1, i]
+        gq[1, y, mine, 384 + 128 * i : 512 + 128 * i] = total.astype(BF16)
+    ends.start(1)
+    ends.forward()
+    attends.start(0)
+    attends.start(1)
+
+    def hidden_part(e):
+        q = ends.group(e)
+        for j in range(2):
+            columns = slice(j * 256, (j + 1) * 256)
+            total = nt(gq[0, q], wq[1, columns, 0:640])
+            total = total + nt(gq[1, q, :, 0:384], wq[1, columns, 640:1024])
+            total = total + nt(gq[1, q, :, 384:512], wk[1, columns, :])
+            total = total + nt(gq[1, q, :, 512:640], wv[1, columns, :])
+            hidden.refs[0][e, :, columns] = total.astype(BF16)
+        hidden.swap(e)
+        for h in range(2):
+            local_out(gq.at[h, q], gq_out.at[h, q], 8 + 2 * e + h)
+
+    hidden_part(0)
+    hidden_part(1)
+    hidden.pair(0)
+    attends.forward()
+    hidden_part(3)
+    hidden.pair(1)
+    hidden_part(2)
+    hidden.pair(3)
+    hidden.pair(2)
+    hidden_grad = hidden.total()
+    scaled = hidden_grad * gain_j
+    value = joined[...]
+    inner.start(lanes(jnp.sum(scaled * value, -1, keepdims=True)))
+    pf[...] = scaled
+
+    def output_part(e):
+        q = attends.group(e)
+        for j in range(2):
+            columns = slice(j * 256, (j + 1) * 256)
+            total = dot(at[0, q], wo[0:512, columns]) + dot(at[1, q], wo[512:1024, columns])
+            output.refs[0][e, :, columns] = total.astype(BF16)
+        output.swap(e)
+        for h in range(2):
+            local_out(at.at[h, q], at_out.at[h, q], 16 + 2 * e + h)
+
+    output_part(0)
+    output_part(1)
+    mean = column((inner.total() / 8192.0)[0:1, :])
+    rate = column(rt[2 * q0 + c][0:1, :])
+    value = joined[...]
+    own_grad = own_early[1].astype(F32) + rate * pf[...] - value * (rate * rate * rate) * mean
+    jg[q0, half, :] = own_grad.astype(BF16)
+    grad_rows.to_sibling(0)
+    grad_rows.along_z()
+    output.pair(0)
+    output_part(3)
+    output.pair(1)
+    output_part(2)
+    output.pair(3)
+    for e in NEAR:
+        grad_rows.forward(e)
+    output.pair(2)
+    draft[...] = (value + output.total()).astype(BF16)
+    for e in range(4):
+        grad_rows.whole(e)
+    local_out(jg, jg_out, 24)
+    mv.drain()
+    for copy in outs:
+        copy.wait()
+
+
+def draft_call(*args):
+    def gather_g():
+        return [dma(3), dma(3), dma(4), dma(4)]
+
+    def gather_t():
+        return [dma(2, 3), dma(2, 3), dma(2, 3, 4), dma(2, 3, 4)]
+
+    return pl.pallas_call(
+        draft_kernel,
+        name="draft",
+        out_shape=(
+            jax.ShapeDtypeStruct((128, 512), BF16),
+            jax.ShapeDtypeStruct((2, 4, 256, 512), BF16),
+            jax.ShapeDtypeStruct((2, 4, 256, 640), BF16),
+            jax.ShapeDtypeStruct((2, 4, 256, 512), BF16),
+            jax.ShapeDtypeStruct((4, 256, 512), BF16),
+        ),
+        in_specs=[IN_VMEM] * 9,
+        out_specs=(IN_VMEM, ANYWHERE, ANYWHERE, ANYWHERE, ANYWHERE),
+        scratch_shapes=[
+            vmem(4, 256, 512),
+            vmem(2, 4, 256, 512),
+            vmem(8, 8, 128, dtype=F32),
+            vmem(512, 128),
+            vmem(512, 128),
+            vmem(256, 128),
+            vmem(256, 128),
+            vmem(2, 256, 128, dtype=F32),
+            vmem(2, 2, 64, 128, dtype=F32),
+            vmem(2, 4, 256, 640),
+            vmem(2, 4, 256, 512),
+            vmem(4, 256, 512),
+            vmem(128, 512, dtype=F32),
+            dma(26), dma(8), dma(8), dma(2, 2), dma(2, 2), dma(2), dma(2),
+            *gather_g(), *gather_g(), *StatsT.scratch(), *StatsT.scratch(),
+            *SumT.scratch(512), *SumT.scratch(640), *SumG.scratch(), *SumG.scratch(),
+            *gather_t(), *gather_t(),
+        ],
+        compiler_params=pltpu.CompilerParams(
+            collective_id=1, has_side_effects=True, vmem_limit_bytes=VMEM_LIMIT
+        ),
+        cost_estimate=pl.CostEstimate(flops=7000000000, bytes_accessed=16000000, transcendentals=0),
+    )(*args)
 
 
 def local(
@@ -374,144 +872,35 @@
     segment_ids,
     grad_hidden,
 ):
-    tensor_count = lax.axis_size("tensor")
-    group_count = lax.axis_size(("group", "seq"))
-    tensor_index = lax.axis_index("tensor")
-    group_rows = embedded.shape[0]
-    token_count = group_rows * group_count
-    tensor_rows = token_count // tensor_count
-    model_width = embedded.shape[1] * tensor_count
-    head_dim = key_w.shape[2]
-    group_heads = query_w.shape[2] // head_dim
-    seq_len = segment_ids.shape[1]
-    score_scale = head_dim ** (-0.5)
-    joined, feats = features_call(
-        context.transpose(1, 0, 2), resid_in.transpose(1, 0, 2), target_out_w, join_w
+    early = jnp.stack([embedded, grad_hidden])
+    first_query = lax.axis_index("tensor") * 64
+    seq_start = first_query // 512 * 512
+    segments = jnp.pad(segment_ids.reshape(-1), (192, 0))
+    key_segment = lax.dynamic_slice_in_dim(segments, first_query, 256, 0)
+    query_segment = lax.dynamic_slice_in_dim(segments, first_query + 192, 64, 0)
+    key_pos = first_query - 192 + jnp.arange(256, dtype=jnp.int32)
+    query_pos = first_query + jnp.arange(64, dtype=jnp.int32)
+    mask = (
+        (query_segment[:, None] == key_segment[None, :])
+        & (key_pos[None, :] <= query_pos[:, None])
+        & (key_pos[None, :] >= seq_start)
+    ).astype(F32)
+    joined, feats, early_all = features_call(
+        context.transpose(1, 0, 2), resid_in.transpose(1, 0, 2), target_out_w, join_w, early
     )
-    embed_float = embedded.astype(jnp.float32)
-    joined_squares, embed_squares = totals_tensor(
-        (jnp.sum(joined * joined, -1), jnp.sum(embed_float * embed_float, -1))
+    draft_hidden, inputs, ends, attended, joined_grad = draft_call(
+        joined, early_all, early, query_w, key_w, value_w, out_w, jnp.stack([embed_gain, joined_gain]), mask
     )
-    joined_rate = lax.rsqrt(joined_squares / model_width + epsilon)[:, None]
-    embed_rate = lax.rsqrt(embed_squares / model_width + epsilon)[:, None]
-    joined_scale = joined_gain.astype(jnp.float32)
-    hidden_norm = (joined * joined_rate * joined_scale).astype(jnp.bfloat16)
-    embed_norm = (embed_float * embed_rate * embed_gain.astype(jnp.float32)).astype(jnp.bfloat16)
-    inputs_all = gather_groups(jnp.stack([embed_norm, hidden_norm], 1))
-
-    def query_term(first_row, row_count):
-        return jnp.einsum("thk,hkm->tm", inputs_all, query_w, preferred_element_type=jnp.float32)
-
-    query = partial_tensor(query_term, tensor_rows).astype(jnp.bfloat16)
-    key_part = jnp.einsum("thk,hkm->tm", inputs_all, key_w, preferred_element_type=jnp.float32)
-    value_part = jnp.einsum("thk,hkm->tm", inputs_all, value_w, preferred_element_type=jnp.float32)
-    key_sum, value_sum = totals_tensor((key_part, value_part))
-    key_full = key_sum.astype(jnp.bfloat16)
-    value_full = value_sum.astype(jnp.bfloat16)
-    first_query = tensor_index * tensor_rows
-    seq_start = first_query // seq_len * seq_len
-    flat_segments = segment_ids.reshape(-1)
-    query_segment = lax.dynamic_slice_in_dim(flat_segments, first_query, tensor_rows, 0)
-    key_segment = lax.dynamic_slice_in_dim(flat_segments, seq_start, seq_len, 0)
-    query_pos = first_query + jnp.arange(tensor_rows, dtype=jnp.int32)
-    key_pos = seq_start + jnp.arange(seq_len, dtype=jnp.int32)
-    allowed = (query_segment[:, None] == key_segment[None, :]) & (
-        key_pos[None, :] <= query_pos[:, None]
-    )
-    keys_local = lax.dynamic_slice_in_dim(key_full, seq_start, seq_len, 0)
-    values_local = lax.dynamic_slice_in_dim(value_full, seq_start, seq_len, 0)
-    query_heads = query.reshape(tensor_rows, group_heads, head_dim)
-    scores = (
-        jnp.einsum("igd,jd->gij", query_heads, keys_local, preferred_element_type=jnp.float32)
-        * score_scale
-    )
-    scores = jnp.where(allowed[None], scores, -1e30)
-    probs = jax.nn.softmax(scores, axis=-1)
-    probs_low = probs.astype(jnp.bfloat16)
-    attended = jnp.einsum(
-        "gij,jd->igd", probs_low, values_local, preferred_element_type=jnp.float32
-    )
-    attended = attended.reshape(tensor_rows, group_heads * head_dim).astype(jnp.bfloat16)
-    attended_all = gather_tensor(attended)
-
-    def output_term(first_row, row_count):
-        return jnp.dot(attended_all, out_w, preferred_element_type=jnp.float32)
-
-    attn_sum = partial_groups(output_term, group_rows)
-    draft_hidden = (joined + attn_sum).astype(jnp.bfloat16)
-    cotangent_all = gather_groups(grad_hidden)
-    grad_out = jnp.einsum(
-        "tm,tn->mn", attended_all, cotangent_all, preferred_element_type=jnp.float32
-    ).astype(jnp.bfloat16)
-
-    def back_term(first_row, row_count):
-        return jnp.einsum("tn,mn->tm", cotangent_all, out_w, preferred_element_type=jnp.float32)
-
-    attended_grad = partial_tensor(back_term, tensor_rows).astype(jnp.bfloat16)
-    grad_heads = attended_grad.reshape(tensor_rows, group_heads, head_dim)
-    probs_grad = jnp.einsum(
-        "igd,jd->gij", grad_heads, values_local, preferred_element_type=jnp.float32
-    )
-    score_grad = (
-        probs * (probs_grad - jnp.sum(probs_grad * probs, -1, keepdims=True)) * score_scale
-    ).astype(jnp.bfloat16)
-    query_grad = jnp.einsum(
-        "gij,jd->igd", score_grad, keys_local, preferred_element_type=jnp.float32
-    )
-    query_grad = query_grad.reshape(tensor_rows, group_heads * head_dim).astype(jnp.bfloat16)
-    key_local = jnp.einsum(
-        "gij,igd->jd", score_grad, query_heads, preferred_element_type=jnp.float32
-    )
-    value_local = jnp.einsum(
-        "gij,igd->jd", probs_low, grad_heads, preferred_element_type=jnp.float32
-    )
-    zeros_full = jnp.zeros((token_count, head_dim), jnp.float32)
-    key_grad_sum, value_grad_sum = totals_tensor(
-        (
-            lax.dynamic_update_slice_in_dim(zeros_full, key_local, seq_start, 0),
-            lax.dynamic_update_slice_in_dim(zeros_full, value_local, seq_start, 0),
-        )
-    )
-    key_grad = key_grad_sum.astype(jnp.bfloat16)
-    value_grad = value_grad_sum.astype(jnp.bfloat16)
-    query_grad_all = gather_tensor(query_grad)
-    grad_query = jnp.einsum(
-        "thk,tm->hkm", inputs_all, query_grad_all, preferred_element_type=jnp.float32
-    ).astype(jnp.bfloat16)
-    grad_key = jnp.einsum(
-        "thk,tm->hkm", inputs_all, key_grad, preferred_element_type=jnp.float32
-    ).astype(jnp.bfloat16)
-    grad_value = jnp.einsum(
-        "thk,tm->hkm", inputs_all, value_grad, preferred_element_type=jnp.float32
-    ).astype(jnp.bfloat16)
-
-    def input_term(first_row, row_count):
-        running = jnp.einsum(
-            "tm,km->tk", query_grad_all, query_w[1], preferred_element_type=jnp.float32
-        )
-        running = running + jnp.einsum(
-            "tm,km->tk", key_grad, key_w[1], preferred_element_type=jnp.float32
-        )
-        return running + jnp.einsum(
-            "tm,km->tk", value_grad, value_w[1], preferred_element_type=jnp.float32
-        )
-
-    hidden_grad = partial_groups(input_term, group_rows)
-    scaled_grad = hidden_grad * joined_scale
-    inner_sum = totals_tensor(jnp.sum(scaled_grad * joined, -1))
-    joined_grad = (
-        grad_hidden.astype(jnp.float32)
-        + joined_rate * scaled_grad
-        - joined * (joined_rate * joined_rate * joined_rate) * (inner_sum / model_width)[:, None]
-    )
-    joined_grad_all = gather_groups(joined_grad.astype(jnp.bfloat16))
-    grad_join = jnp.einsum(
-        "hqltk,qtm->lhkm",
-        feats,
-        joined_grad_all.reshape(4, 256, -1),
-        preferred_element_type=jnp.float32,
-    ).astype(jnp.bfloat16)
-    grad_join = grad_join.reshape(join_w.shape)
+
+    def over_tokens(spec, left, right):
+        return jnp.einsum(spec, left, right, preferred_element_type=F32).astype(BF16)
+
+    query_grad = jnp.concatenate([ends[0], ends[1, :, :, 0:384]], -1)
+    grad_query = over_tokens("hqtk,qtm->hkm", inputs, query_grad)
+    grad_key = over_tokens("hqtk,qtm->hkm", inputs, ends[1, :, :, 384:512])
+    grad_value = over_tokens("hqtk,qtm->hkm", inputs, ends[1, :, :, 512:640])
+    grad_out = over_tokens("hqtk,qtm->hkm", attended, early_all[1]).reshape(out_w.shape)
+    grad_join = over_tokens("hqltk,qtm->lhkm", feats, joined_grad).reshape(join_w.shape)
     return (draft_hidden, grad_join, grad_query, grad_key, grad_value, grad_out)
 
 

time: 633 us -> 276 us (0.44)
  blocking collectives: 221 us -> 0 us
  waiting for transfers between devices: 186 us -> 0 us
  Pallas kernels: 134 us -> 249 us
  matrix products: 60.8 us -> 15.6 us
  between operations: 14 us -> 0.75 us
  other arithmetic: 9.56 us -> 3.17 us
    psum x4 -> x0, blocking collectives: 221 us -> none  [totals_tensor(): return lax.psum(values, 'tensor')]
    pallas_call x0 -> x1, Pallas kernels: none -> 121 us  [draft_call(): pl.pallas_call(draft_kernel, name='draft', out_shape=(jax.ShapeDtypeStruc...]
    reduce_scatter x4 -> x0, waiting for transfers between devices: 120 us -> none  [the longest x2 69.4 us: partial_tensor(): lax.psum_scatter(builder(jnp.int32(0), row_count * lax.axis_size('tensor'...]
    all_gather x5 -> x0, waiting for transfers between devices: 65.4 us -> none  [the longest x3 65.3 us: gather_groups(): return lax.all_gather(values, ('group', 'seq'), axis=0, tiled=True)]
    dot_general x18 -> x5, matrix products: 58.4 us -> 15.6 us  [over_tokens(): jnp.einsum(spec, left, right, preferred_element_type=F32).astype(BF16)]
  transfers between devices with their start and end apart: 9 -> 0, of which waited for: 5 -> 0; matrix products, arithmetic and copies ran while one was open for 9% -> 0% of each run, Pallas kernels for 21% -> 0%
where the time goes in v2:
time: 276 us; the launch traced here: 275 us
  Pallas kernels  249 us (90%)
  matrix products  15.6 us (6%)
  local copies, waits for them, and re-layouts  6.42 us (2%)
  other arithmetic  3.17 us (1%)
    pallas_call x1, Pallas kernels, features_call(): pl.pallas_call(features_kernel, name='features', out_shape=(jax.ShapeDtyp...  128 us
    pallas_call x1, Pallas kernels, draft_call(): pl.pallas_call(draft_kernel, name='draft', out_shape=(jax.ShapeDtypeStruc...  121 us
    dot_general x5, matrix products, over_tokens(): jnp.einsum(spec, left, right, preferred_element_type=F32).astype(BF16)  15.6 us

profile of v2, /device:TPU:1, one launch (start us, length us, event | category | flops | bytes accessed | tf_op | source)
XLA Modules:
  0.0 274.6 jit_solution(233831055602815301)
XLA Ops:
  0.7 0.7 stack.21
  1.3 0.7 stack.22
  2.0 0.6 pad_maximum_fusion.1.refs_7_
  2.6 0.7 copy.42
  3.3 0.1 pad_dynamic-slice_fusion.1
  3.4 0.1 pad_dynamic-slice_fusion
  3.5 0.7 and_convert_fusion.refs_8_
  4.2 1.7 pad_maximum_fusion.early.refs_2_
  5.9 128.2 %features.1 = (f32[128,512]{1,0:T(8,128)}, bf16[2,4,3,256,512]{4,3,2,1,0:T(8,128)(2,1)}, bf16[2,4,256,512]{3,2,1,0:T(8,128)(2,1)}) custom-call(bf16[3,128,512]{2,1,0:T(8,128)(2,1)} %bitcast.70, bf16[3,64,1024]{2,1,0:T(8,128)(2,1)} %bitcast.71, bf16[3,512,1024]{2,1,0:T(8,128)(2,1)} %wt.1, bf16[3,1024,512]{2,1,0:T(8,128)(2,1)} %wj.1, ...), custom_call_target="tpu_custom_call" | custom-call | flops 6499999744 | bytes 16000000 | tf_op jit(solution)/shard_map/features/pallas_call | solution.py:540
  134.1 0.0 copy-start.3
  134.1 120.5 %draft.1 = (bf16[128,512]{1,0:T(8,128)(2,1)}, bf16[2,4,256,512]{3,2,1,0:T(8,128)(2,1)}, bf16[2,4,256,640]{3,2,1,0:T(8,128)(2,1)}, bf16[2,4,256,512]{3,2,1,0:T(8,128)(2,1)}, bf16[4,256,512]{2,1,0:T(8,128)(2,1)}) custom-call(f32[128,512]{1,0:T(8,128)} %get-tuple-element.14.refs_0_, bf16[2,4,256,512]{3,2,1,0:T(8,128)(2,1)} %get-tuple-element.15.refs_1_, ...), custom_call_target="tpu_custom_call" | custom-call | flops 7000000000 | bytes 16000000 | tf_op jit(solution)/shard_map/draft/pallas_call | solution.py:822
  254.6 0.0 copy-done.3
  254.6 0.0 copy-start.4
  254.6 4.0 %bitcast_convert_fusion.2 = bf16[2,512,512]{2,1,0:T(8,128)(2,1)} fusion(bf16[2,4,256,512]{3,2,1,0:T(8,128)(2,1)} %get-tuple-element.21, bf16[2,4,256,512]{3,2,1,0:T(8,128)(2,1)S(1)} %copy-done.3), kind=kOutput, calls=%fused_computation.6 | convolution fusion | flops 1074266112 | bytes 4194304 | tf_op jit(solution)/shard_map/hqtk,qtm->hkm/dot_general | solution.py:896
  258.6 0.0 copy-done.4
  258.6 5.0 %fusion = bf16[3,2,512,512]{3,2,0,1:T(8,128)(2,1)S(1)} fusion(bf16[2,4,3,256,512]{4,3,2,1,0:T(8,128)(2,1)S(1)} %copy-done.4, bf16[4,256,512]{2,1,0:T(8,128)(2,1)} %get-tuple-element.17), kind=kOutput, calls=%fused_computation.2 | convolution fusion | flops 3222798336 | bytes 10485760 | tf_op jit(solution)/shard_map/hqltk,qtm->lhkm/dot_general | solution.py:896
  263.6 0.0 copy-start
  263.6 0.0 copy-start.2
  263.6 2.1 copy.25
  265.7 0.6 copy-done
  266.2 0.9 copy-done.2
  267.1 1.5 fusion.4
  268.6 1.5 fusion.3
  270.0 0.1 slice_bitcast_fusion.1
  270.1 0.1 slice_bitcast_fusion
  270.2 0.0 copy-start.1
  270.2 3.7 %bitcast_convert_fusion.1 = bf16[2,512,1024]{2,1,0:T(8,128)(2,1)} fusion(bf16[2,4,256,512]{3,2,1,0:T(8,128)(2,1)S(1)} %copy-done.2, bf16[4,256,384]{2,1,0:T(8,128)(2,1)S(1)} %slice_bitcast_fusion.1, bf16[4,256,640]{2,1,0:T(8,128)(2,1)S(1)} %slice_bitcast_fusion), kind=kOutput, calls=%fused_computation.1 | convolution fusion | flops 2152726528 | bytes 6291456 | tf_op jit(solution)/shard_map/hqtk,qtm->hkm/dot_general | solution.py:896
  274.0 0.0 copy-done.1
  274.0 0.7 copy.44
  (1 shorter events, 0.0 us)
Async XLA Ops:
  134.1 120.5 %copy-start.3 = (bf16[2,4,256,512]{3,2,1,0:T(8,128)(2,1)S(1)}, bf16[2,4,256,512]{3,2,1,0:T(8,128)(2,1)}, u32[]{:S(2)}) copy-start(bf16[2,4,256,512]{3,2,1,0:T(8,128)(2,1)} %get-tuple-element.15.refs_1_) | copy-start | bytes 6291460
  254.6 4.0 %copy-start.4 = (bf16[2,4,3,256,512]{4,3,2,1,0:T(8,128)(2,1)S(1)}, bf16[2,4,3,256,512]{4,3,2,1,0:T(8,128)(2,1)}, u32[]{:S(2)}) copy-start(bf16[2,4,3,256,512]{4,3,2,1,0:T(8,128)(2,1)} %get-tuple-element.18) | copy-start | bytes 18874372
  263.6 2.6 copy-start
  263.6 3.5 %copy-start.2 = (bf16[2,4,256,512]{3,2,1,0:T(8,128)(2,1)S(1)}, bf16[2,4,256,512]{3,2,1,0:T(8,128)(2,1)}, u32[]{:S(2)}) copy-start(bf16[2,4,256,512]{3,2,1,0:T(8,128)(2,1)} %get-tuple-element.19) | copy-start | bytes 6291460
  270.2 3.7 %copy-start.1 = (bf16[128,512]{1,0:T(8,128)(2,1)S(1)}, bf16[128,512]{1,0:T(8,128)(2,1)}, u32[]{:S(2)}) copy-start(bf16[128,512]{1,0:T(8,128)(2,1)} %get-tuple-element.32) | copy-start | bytes 393220

commit v3 on v2

v3 whole, which is shorter than its diff:
```python
import jax
import jax.numpy as jnp
from jax import lax
from jax.experimental import pallas as pl
from jax.experimental.pallas import tpu as pltpu
from jax.sharding import PartitionSpec as P

epsilon = 1e-05
F32 = jnp.float32
BF16 = jnp.bfloat16
NEAR = (1, 3, 2)
VMEM_LIMIT = 62 * 2**20


def rem(value, count):
    return lax.rem(value, jnp.int32(count))


def group_of(z):
    return rem(z, 2) * 2 + lax.div(z, jnp.int32(2))


class Place:
    def __init__(self):
        self.t = lax.axis_index("tensor")
        seq = lax.axis_index("seq")
        self.x, self.y = rem(self.t, 4), lax.div(self.t, jnp.int32(4))
        self.z = lax.div(seq, jnp.int32(2)) * 2 + lax.axis_index("group")
        self.c = rem(seq, 2)

    def at(self, x=None, y=None, z=None, c=None):
        x = self.x if x is None else x
        y = self.y if y is None else y
        z = self.z if z is None else z
        c = self.c if c is None else c
        return (rem(z, 2), y * 4 + x, lax.div(z, jnp.int32(2)) * 2 + c)

    def to_x(self, d):
        return self.at(x=rem(self.x + d, 4))

    def to_y(self, d):
        return self.at(y=rem(self.y + d, 4))

    def to_z(self, d):
        return self.at(z=rem(self.z + d, 4))

    def sibling(self):
        return self.at(c=1 - self.c)


def greet(devices):
    barrier = pltpu.get_barrier_semaphore()
    for device in devices:
        pl.semaphore_signal(barrier, inc=1, device_id=device, device_id_type=pl.DeviceIdType.MESH)
    pl.semaphore_wait(barrier, len(devices))


def remote(src, dst, send, recv, device):
    return pltpu.make_async_remote_copy(
        src_ref=src,
        dst_ref=dst,
        send_sem=send,
        recv_sem=recv,
        device_id=device,
        device_id_type=pl.DeviceIdType.MESH,
    )


def rows(first, count):
    return pl.ds(pl.multiple_of(first, count), count)


def vmem(*shape, dtype=BF16):
    return pltpu.VMEM(shape, dtype)


def dma(*shape):
    return pltpu.SemaphoreType.DMA(shape)


IN_VMEM = pl.BlockSpec(memory_space=pltpu.VMEM)
ANYWHERE = pl.BlockSpec(memory_space=pl.ANY)


def nt(a, b):
    return lax.dot_general(a, b, (((1,), (1,)), ((), ())), preferred_element_type=F32)


def tn(a, b):
    return lax.dot_general(a, b, (((0,), (0,)), ((), ())), preferred_element_type=F32)


def dot(a, b):
    return jnp.dot(a, b, preferred_element_type=F32)


class Mover:
    def __init__(self, me, dummy):
        self.me, self.dummy, self.open = me, dummy, {}

    def send(self, src, dst, ss, rs, device, when=None, tag="end"):
        copy = remote(src, dst, ss, rs, device)
        if when is None:
            copy.start()
        else:
            pl.when(when)(copy.start)
        self.open.setdefault(tag, []).append((when, src, ss))

    def arrived(self, dst, rs):
        remote(dst, dst, self.dummy, rs, self.me.sibling()).wait_recv()

    def settle(self, tag):
        for when, src, ss in self.open.pop(tag, []):
            wait = remote(src, src, ss, self.dummy, self.me.sibling()).wait_send
            if when is None:
                wait()
            else:
                pl.when(when)(wait)

    def drain(self):
        for tag in list(self.open):
            self.settle(tag)


class GatherG:
    def __init__(self, mv, tag, block, s_z, r_z, s_c, r_c):
        me = mv.me
        self.mv, self.tag, self.block, self.sems = mv, tag, block, (s_z, r_z, s_c, r_c)
        self.group = [group_of(rem(me.z + e, 4)) for e in range(4)]

    def to_sibling(self, e, src=None):
        me, (_, _, s_c, r_c) = self.mv.me, self.sems
        place = self.block(self.group[e], me.c)
        self.mv.send(place if src is None else src, place, s_c.at[e], r_c.at[e], me.sibling(), tag=self.tag)

    def along_z(self, src=None):
        me, (s_z, r_z, _, _) = self.mv.me, self.sems
        place = self.block(self.group[0], me.c)
        for d in NEAR:
            self.mv.send(place if src is None else src, place, s_z.at[d - 1], r_z.at[3 - d], me.to_z(d), tag=self.tag)

    def forward(self, e):
        me, (_, r_z, _, _) = self.mv.me, self.sems
        self.mv.arrived(self.block(self.group[e], me.c), r_z.at[e - 1])
        self.to_sibling(e)

    def whole(self, e):
        me, (_, _, _, r_c) = self.mv.me, self.sems
        self.mv.arrived(self.block(self.group[e], 1 - me.c), r_c.at[e])


class GatherT:
    def __init__(self, mv, block, s_1, r_1, s_2, r_2):
        self.mv, self.rows_of, self.sems = mv, block, (s_1, r_1, s_2, r_2)

    def block(self, h, a, b, lo=0, count=64):
        me = self.mv.me
        p, q = (a, b) if h == 0 else (b, a)
        return self.rows_of(h, rem(me.y + q, 4), rem(me.x + p, 4), lo, count)

    def move(self, first_axis, h, part, ss, rs, i):
        me, step = self.mv.me, 1 if i % 2 == 0 else 3
        to = me.to_x(step) if first_axis == (h == 0) else me.to_y(step)
        self.mv.send(part, part, ss, rs, to)

    def to_second(self, h, a):
        s_2, r_2 = self.sems[2:]
        for i in range(2):
            self.move(False, h, self.block(h, a, 0), s_2.at[h, a, i], r_2.at[h, a, i], i)

    def start(self, h):
        s_1, r_1 = self.sems[:2]
        for i in range(2):
            self.move(True, h, self.block(h, 0, 0), s_1.at[h, i], r_1.at[h, i], i)
        self.to_second(h, 0)

    def first(self, h):
        s_1, r_1 = self.sems[:2]
        for i, a in ((0, 3), (1, 1)):
            self.mv.arrived(self.block(h, a, 0), r_1.at[h, i])
            self.move(True, h, self.block(h, a, 0, 32 * i, 32), s_1.at[h, 2 + i], r_1.at[h, 2 + i], i)
            self.to_second(h, a)

    def far(self, h):
        for i in range(2):
            self.mv.arrived(self.block(h, 2, 0, 32 * i, 32), self.sems[1].at[h, 2 + i])
        self.to_second(h, 2)

    def relay(self, h, a):
        s_2, r_2 = self.sems[2:]
        for i, b in ((0, 3), (1, 1)):
            self.mv.arrived(self.block(h, a, b), r_2.at[h, a, i])
            self.move(False, h, self.block(h, a, b, 32 * i, 32), s_2.at[h, a, 2 + i], r_2.at[h, a, 2 + i], i)

    def last(self, h, a):
        for i in range(2):
            self.mv.arrived(self.block(h, a, 2, 32 * i, 32), self.sems[3].at[h, a, 2 + i])

    def middle(self):
        for h in range(2):
            self.first(h)
        for h in range(2):
            self.relay(h, 0)
        for h in range(2):
            self.far(h)
        for a in (3, 1):
            for h in range(2):
                self.relay(h, a)

    def end(self):
        for h in range(2):
            self.relay(h, 2)

    def group(self, e):
        if e == 2:
            for a in range(4):
                self.last(0, a)
        self.last(1, e)
        return rem(self.mv.me.y + e, 4)

    @staticmethod
    def scratch():
        return [dma(2, 4), dma(2, 4), dma(2, 4, 4), dma(2, 4, 4)]


class SumG:
    def __init__(self, mv, js, jx, j2, jz, s_x, r_x, s_z, r_z):
        self.mv, self.refs, self.sems = mv, (js, jx, j2, jz), (s_x, r_x, s_z, r_z)

    def swap(self, e):
        (js, jx, _, _), (s_x, r_x, _, _), me = self.refs, self.sems, self.mv.me
        self.mv.send(js.at[e, rows((1 - me.c) * 128, 128), :], jx.at[e], s_x.at[e], r_x.at[e], me.sibling(), tag=self)

    def pair(self, e):
        (js, jx, j2, jz), (_, r_x, s_z, r_z), me = self.refs, self.sems, self.mv.me
        self.mv.arrived(jx.at[e], r_x.at[e])
        j2[e] = (js[e, rows(me.c * 128, 128), :].astype(F32) + jx[e].astype(F32)).astype(BF16)
        to = group_of(rem(me.y + e, 4))
        slot = rem(me.z - to + 4, 4)
        at = jnp.maximum(slot - 1, 0)
        self.mv.send(j2.at[e], jz.at[at], s_z.at[e], r_z.at[at], me.at(z=to), when=slot != 0, tag=self)

    def total(self):
        (_, _, j2, jz), (_, _, _, r_z), me = self.refs, self.sems, self.mv.me
        for d in NEAR:
            self.mv.arrived(jz.at[d - 1], r_z.at[d - 1])
        total = j2[rem(group_of(me.z) - me.y + 4, 4)].astype(F32)
        for d in range(3):
            total = total + jz[d].astype(F32)
        return total

    @staticmethod
    def scratch():
        return [vmem(4, 256, 512), vmem(4, 128, 512), vmem(4, 128, 512), vmem(3, 128, 512), dma(4), dma(4), dma(4), dma(3)]


class SumT:
    def __init__(self, mv, ps, rx, ry, s0, s1, r2x, r2y, *sems):
        self.mv, self.ps, self.rx, self.ry, self.s0, self.s1, self.r2x, self.r2y = mv, ps, rx, ry, s0, s1, r2x, r2y
        self.sems = sems

    def issue(self, e):
        mv, me = self.mv, self.mv.me
        s_x, r_x, s_y, r_y = self.sems[:4]
        for d in NEAR:
            to = rem(me.x + d, 4)
            mv.send(self.ps.at[0, e, rows(to * 64, 64), :], self.rx.at[e, 3 - d], s_x.at[e, d - 1], r_x.at[e, 3 - d], me.at(x=to), tag=self)
        if e:
            mv.send(self.ps.at[1, e], self.ry.at[3 - e], s_y.at[e], r_y.at[3 - e], me.to_y(e), tag=self)

    def collect_x(self, e):
        mv, me = self.mv, self.mv.me
        r_x, s_2x, r_2x = self.sems[1], self.sems[4], self.sems[5]
        for d in NEAR:
            mv.arrived(self.rx.at[e, d - 1], r_x.at[e, d - 1])
        total = self.ps[0, e, rows(me.x * 64, 64), :].astype(F32)
        for d in range(3):
            total = total + self.rx[e, d].astype(F32)
        self.s0[e] = total.astype(BF16)
        if e:
            mv.send(self.s0.at[e], self.r2x.at[3 - e], s_2x.at[e], r_2x.at[3 - e], me.to_y(e))

    def fold(self):
        mv, me = self.mv, self.mv.me
        r_y, s_2y, r_2y = self.sems[3], self.sems[6], self.sems[7]
        for d in NEAR:
            mv.arrived(self.ry.at[d - 1], r_y.at[d - 1])
        for d in (2, 1, 3, 0):
            to = rem(me.x + d, 4)
            part = rows(to * 64, 64)
            total = self.ps[1, 0, part, :].astype(F32)
            for i in range(3):
                total = total + self.ry[i, part, :].astype(F32)
            self.s1[part, :] = total.astype(BF16)
            if d:
                mv.send(self.s1.at[part, :], self.r2y.at[3 - d], s_2y.at[d - 1], r_2y.at[3 - d], me.at(x=to))

    def finish(self, h):
        mv, me = self.mv, self.mv.me
        got, sem = ((self.r2x, self.sems[5]), (self.r2y, self.sems[7]))[h]
        for d in NEAR:
            mv.arrived(got.at[d - 1], sem.at[d - 1])
        total = (self.s0[0] if h == 0 else self.s1[rows(me.x * 64, 64), :]).astype(F32)
        for d in range(3):
            total = total + got[d].astype(F32)
        return total.astype(BF16)

    @staticmethod
    def scratch(w):
        return [
            vmem(4, 3, 64, w), vmem(3, 256, w), vmem(4, 64, w), vmem(256, w), vmem(3, 64, w), vmem(3, 64, w),
            dma(4, 3), dma(4, 3), dma(4), dma(3), dma(4), dma(3), dma(3), dma(3),
        ]


def lanes(column):
    return jnp.broadcast_to(column, (128, 128)).T[0:8, :]


def column(row):
    return jnp.broadcast_to(row, (128, 128)).T[:, 0:1]


class TilesG:
    def __init__(self, mv, line, tiles, s_t, r_t):
        self.mv, self.line, self.tiles, self.s_t, self.r_t = mv, line, tiles, s_t, r_t

    def place(self, e, core):
        me = self.mv.me
        return self.tiles.at[2 * group_of(rem(me.z + e, 4)) + rem(me.c + core, 2)]

    def start(self, tile):
        me = self.mv.me
        self.tiles[2 * group_of(me.z) + me.c] = tile
        for d in range(1, 8):
            back = (4 - d % 4) % 4 + 4 * (d // 4)
            self.mv.send(self.place(0, 0), self.place(0, 0), self.s_t.at[d], self.r_t.at[back], self.line[d - 1])

    def whole(self):
        for d in range(1, 8):
            self.mv.arrived(self.place(d % 4, d // 4), self.r_t.at[d])

    def column(self, q, i):
        return column(self.tiles[2 * q + i][0:1, :])

    @staticmethod
    def scratch():
        return [pltpu.VMEM((8, 8, 128), F32), dma(8), dma(8)]


class StatsT:
    def __init__(self, mv, tiles, s_t, r_t):
        self.mv, self.tiles, self.s_t, self.r_t = mv, tiles, s_t, r_t

    def start(self, tile):
        me = self.mv.me
        self.tiles[0] = tile
        for d in range(1, 16):
            dx, dy = d % 4, d // 4
            back = (4 - dx) % 4 + 4 * ((4 - dy) % 4)
            to = me.at(x=rem(me.x + dx, 4), y=rem(me.y + dy, 4))
            self.mv.send(self.tiles.at[0], self.tiles.at[back], self.s_t.at[d], self.r_t.at[back], to)

    def total(self):
        for d in range(1, 16):
            self.mv.arrived(self.tiles.at[d], self.r_t.at[d])
        total = self.tiles[0]
        for d in range(1, 16):
            total = total + self.tiles[d]
        return total

    @staticmethod
    def scratch():
        return [pltpu.VMEM((16, 8, 128), F32), dma(16), dma(16)]


def take(refs, count):
    out = refs[:count]
    del refs[:count]
    return out


def step_kernel(*refs):
    refs = list(refs)
    ctx, resid, wt, wj, embedded, cotangent, gain_e, gain_j, wq, wk, wv, wo, mask = take(refs, 13)
    draft, join_out, query_out, key_out, value_out, output_out = take(refs, 6)
    ca, sb, rx, ry, s0, s1, r2x, r2y, fa, ea, xa, qh, gh, kw, vw, kg, kgot, gq, at, jg, joined, kvs, qps = take(refs, 23)
    s_loc, s_kv, r_kv, s_kg, r_kg = take(refs, 5)
    s_x, r_x, s_y, r_y, s_2x, r_2x, s_2y, r_2y = take(refs, 8)
    me = Place()
    x, y, z, c, t = me.x, me.y, me.z, me.c, me.t
    mv = Mover(me, s_loc.at[0])
    mine, half = rows(x * 64, 64), rows(c * 128, 128)
    plane = [me.at(x=rem(x + d % 4, 4), y=rem(y + d // 4, 4)) for d in range(1, 16)]
    line = [me.at(z=rem(z + d % 4, 4), c=rem(c + d // 4, 2)) for d in range(1, 8)]
    xn, back_ps, stage = sb.at[:, :, 1], sb.at[:, :, 0], sb.at[:, :, 2]
    context_rows = GatherG(mv, "ctx", lambda q, core: ca.at[q, :, rows(core * 128, 128), :], *take(refs, 4))
    early_rows = GatherG(mv, "end", lambda q, core: ea.at[:, q, rows(core * 128, 128), :], *take(refs, 4))
    hidden_rows = GatherG(mv, "xa", lambda q, core: xa.at[q, rows(core * 128, 128), :], *take(refs, 4))
    grad_rows = GatherG(mv, "end", lambda q, core: jg.at[q, rows(core * 128, 128), :], *take(refs, 4))
    embed_stats, hidden_stats, inner_stats = (StatsT(mv, *take(refs, 3)) for _ in range(3))
    embed_rates, hidden_rates, factors = (TilesG(mv, line, *take(refs, 3)) for _ in range(3))
    back = SumT(mv, back_ps, *take(refs, 14))
    qkv = SumT(mv, qps, *take(refs, 14))
    line_sum = SumG(mv, *take(refs, 8))
    output = SumG(mv, *take(refs, 8))
    feats = GatherT(mv, lambda h, q, p, lo, n: fa.at[h, q, :, pl.ds(pl.multiple_of(p * 64 + lo, 32), n), :], *take(refs, 4))
    ends = GatherT(mv, lambda h, q, p, lo, n: gq.at[h, q, pl.ds(pl.multiple_of(p * 64 + lo, 32), n), :], *take(refs, 4))
    attends = GatherT(mv, lambda h, q, p, lo, n: at.at[h, q, pl.ds(pl.multiple_of(p * 64 + lo, 32), n), :], *take(refs, 4))
    assert not refs
    outs = []

    def local_out(src, dst):
        copy = pltpu.make_async_copy(src, dst, s_loc.at[1 + len(outs)])
        copy.start()
        outs.append(copy)

    greet(plane + line)

    group = context_rows.group
    q0 = group[0]
    context_rows.to_sibling(0, ctx)
    context_rows.along_z(ctx)
    ca[q0, :, half, :] = ctx[...]
    ea[0, q0, half, :] = embedded[...]
    ea[1, q0, half, :] = cotangent[...]
    own_embedded = embedded[...].astype(F32)
    embed_stats.start(lanes(jnp.sum(own_embedded * own_embedded, -1, keepdims=True)))

    def target(e):
        def level(l, carry):
            for j in range(4):
                part = dot(ca[group[e], l], wt[l, :, j * 256 : (j + 1) * 256])
                sb[j // 2, e, l, :, (j % 2) * 256 : (j % 2 + 1) * 256] = part.astype(BF16)
            return carry

        lax.fori_loop(0, 3, level, 0)
        for d in NEAR:
            to = rem(x + d, 4)
            mv.send(
                sb.at[0, e, :, rows(to * 64, 64), :], rx.at[e, 3 - d], s_x.at[e, d - 1], r_x.at[e, 3 - d],
                me.at(x=to), tag="sb",
            )
        slot = rem(y - group[e] + 4, 4)
        to = jnp.maximum(slot - 1, 0)
        mv.send(sb.at[1, e], ry.at[to], s_y.at[e], r_y.at[to], me.at(y=group[e]), when=slot != 0, tag="sb")

    def collect_x(e):
        for d in NEAR:
            mv.arrived(rx.at[e, d - 1], r_x.at[e, d - 1])

        def level(l, carry):
            total = sb[0, e, l, mine, :].astype(F32)
            for d in range(3):
                total = total + rx[e, d, l].astype(F32)
            s0[e, l] = total.astype(BF16)
            return carry

        lax.fori_loop(0, 3, level, 0)
        slot = rem(y - group[e] + 4, 4)
        to = jnp.maximum(slot - 1, 0)
        mv.send(s0.at[e], r2x.at[to], s_2x.at[e], r_2x.at[to], me.at(y=group[e]), when=slot != 0)

    for e in (0, 1, 3):
        if e:
            context_rows.forward(e)
        context_rows.whole(e)
        target(e)
    early_rows.to_sibling(0)
    early_rows.along_z()
    collect_x(0)
    context_rows.forward(2)
    context_rows.whole(2)
    target(2)
    embed_rates.start(lax.rsqrt(embed_stats.total() / 8192.0 + epsilon))
    for e in (1, 3, 2):
        collect_x(e)
    for e in NEAR:
        early_rows.forward(e)
    own = rem(group_of(y) - z + 4, 4)
    for d in NEAR:
        mv.arrived(ry.at[d - 1], r_y.at[d - 1])
    for d in (2, 1, 3, 0):
        to = rem(x + d, 4)
        part = rows(to * 64, 64)

        def fold(l, carry):
            total = sb[1, own, l, part, :].astype(F32)
            for i in range(3):
                total = total + ry[i, l, part, :].astype(F32)
            s1[l, part, :] = total.astype(BF16)
            return carry

        lax.fori_loop(0, 3, fold, 0)
        if d:
            mv.send(s1.at[:, part, :], r2y.at[3 - d], s_2y.at[d - 1], r_2y.at[3 - d], me.at(x=to))

    def finish(h, part, got, sem):
        for d in NEAR:
            mv.arrived(got.at[d - 1], sem.at[d - 1])

        def level(l, carry):
            total = part(l).astype(F32)
            for d in range(3):
                total = total + got[d, l].astype(F32)
            fa[h, y, l, mine, :] = (resid[l, :, h * 512 : (h + 1) * 512].astype(F32) + total).astype(BF16)
            return carry

        lax.fori_loop(0, 3, level, 0)
        feats.start(h)

    finish(0, lambda l: s0[own, l], r2x, r_2x)
    finish(1, lambda l: s1[l, mine, :], r2y, r_2y)

    mv.settle("sb")
    for e in range(4):
        early_rows.whole(e)
    embed_rates.whole()
    scale_e = gain_e[...].astype(F32)
    scale_j = gain_j[...].astype(F32)

    def inputs_part(e, i, source, rates, scales):
        q = rem(y + e, 4)
        for k in range(2):
            part = slice(k * 128, (k + 1) * 128)
            xn[i, q, part, :] = (source(q)[part, :].astype(F32) * rates.column(q, k) * scales).astype(BF16)
        for h, first, there, width in (
            (0, 0, 0, 256), (0, 256, 256, 256), (0, 512, 512, 128), (1, 640, 0, 128), (1, 768, 128, 256), (1, 0, 384, 128), (1, 0, 512, 128),
        ):
            w = (wk if there == 384 else wv) if h == 1 and there >= 384 else wq
            total = dot(xn[i, q], w[i, :, first : first + width])
            if i:
                total = total + qps[h, e, :, there : there + width].astype(F32)
            qps[h, e, :, there : there + width] = total.astype(BF16)

    def embed_part(e):
        inputs_part(e, 0, lambda q: ea[0, q], embed_rates, scale_e)

    def back_part(e):
        q = rem(y + e, 4)
        for j in range(4):
            part = nt(ea[1, q], wo[j * 256 : (j + 1) * 256, :])
            back_ps[j // 2, e, :, (j % 2) * 256 : (j % 2 + 1) * 256] = part.astype(BF16)

    def join(e):
        q = feats.group(e)
        for j in range(2):
            columns = slice(j * 256, (j + 1) * 256)
            total = jnp.zeros((256, 256), F32)
            for l in range(3):
                for h in range(2):
                    total = total + dot(fa[h, q, l], wj[l, h * 512 : (h + 1) * 512, columns])
            line_sum.refs[0][e, :, columns] = total.astype(BF16)
        line_sum.swap(e)

    for h in range(2):
        feats.first(h)
    embed_part(2)
    embed_part(1)
    for h in range(2):
        feats.relay(h, 0)
    for h in range(2):
        feats.far(h)
    embed_part(3)
    embed_part(0)
    for h in range(2):
        feats.relay(h, 3)
    back_part(2)
    back_part(1)
    for h in range(2):
        feats.relay(h, 1)
    back_part(3)
    back_part(0)
    join(0)
    feats.end()
    join(1)
    line_sum.pair(0)
    for e in (2, 1, 3, 0):
        back.issue(e)
    join(3)
    line_sum.pair(1)
    join(2)
    line_sum.pair(3)
    line_sum.pair(2)
    value = line_sum.total()
    joined[...] = value

    xa[q0, half, :] = value.astype(BF16)
    hidden_rows.to_sibling(0)
    hidden_rows.along_z()
    hidden_stats.start(lanes(jnp.sum(value * value, -1, keepdims=True)))
    for e in NEAR:
        hidden_rows.forward(e)
    hidden_rates.start(lax.rsqrt(hidden_stats.total() / 8192.0 + epsilon))
    for e in (2, 1, 3, 0):
        back.collect_x(e)
    for e in range(4):
        hidden_rows.whole(e)
    hidden_rates.whole()
    for e in (2, 1, 3, 0):
        inputs_part(e, 1, lambda q: xa[q], hidden_rates, scale_j)
        qkv.issue(e)
    back.fold()
    for h in range(2):
        got = back.finish(h)
        for i in range(4):
            gh[(4 * h + i) * 64 : (4 * h + i + 1) * 64, :] = got[:, i * 128 : (i + 1) * 128]
    for e in (2, 1, 3, 0):
        qkv.collect_x(e)
    qkv.fold()

    got = qkv.finish(1)
    kw[0:64, :] = jnp.zeros((64, 128), BF16)
    vw[0:64, :] = jnp.zeros((64, 128), BF16)
    kw[192:256, :] = got[:, 384:512]
    vw[192:256, :] = got[:, 512:640]
    for i in range(1, 3):
        after = rem(t + i, 16)
        to = me.at(x=rem(after, 4), y=lax.div(after, jnp.int32(4)))
        place = slice(192 - 64 * i, 256 - 64 * i)
        mv.send(kw.at[192:256, :], kw.at[place, :], s_kv.at[0, i - 1], r_kv.at[0, i - 1], to)
        mv.send(vw.at[192:256, :], vw.at[place, :], s_kv.at[1, i - 1], r_kv.at[1, i - 1], to)
    for i in range(3):
        qh[(5 + i) * 64 : (6 + i) * 64, :] = got[:, i * 128 : (i + 1) * 128]
    got = qkv.finish(0)
    for i in range(5):
        qh[i * 64 : (i + 1) * 64, :] = got[:, i * 128 : (i + 1) * 128]
    for i in range(1, 3):
        place = slice(192 - 64 * i, 256 - 64 * i)
        mv.arrived(kw.at[place, :], r_kv.at[0, i - 1])
        mv.arrived(vw.at[place, :], r_kv.at[1, i - 1])

    scale = 128.0**-0.5
    allowed = jnp.concatenate([mask[...]] * 4, axis=0) > 0.5
    for i in range(2):
        part = slice(i * 256, (i + 1) * 256)
        scores = jnp.where(allowed, nt(qh[part, :], kw[...]) * scale, -1e30)
        powers = jnp.exp(scores - jnp.max(scores, -1, keepdims=True))
        probs = powers / jnp.sum(powers, -1, keepdims=True)
        low = probs.astype(BF16)
        attended = dot(low, vw[...]).astype(BF16)
        for j in range(4):
            at[i, y, mine, j * 128 : (j + 1) * 128] = attended[j * 64 : (j + 1) * 64, :]
        value_grad = tn(low, gh[part, :])
        probs_grad = nt(gh[part, :], vw[...])
        score_grad = probs * (probs_grad - jnp.sum(probs_grad * probs, -1, keepdims=True)) * scale
        score_grad = score_grad.astype(BF16)
        query_grad = dot(score_grad, kw[...]).astype(BF16)
        for j in range(4):
            head = 4 * i + j
            h, at_head = (0, head) if head < 5 else (1, head - 5)
            gq[h, y, mine, at_head * 128 : (at_head + 1) * 128] = query_grad[j * 64 : (j + 1) * 64, :]
        key_grad = tn(score_grad, qh[part, :])
        if i == 0:
            kg[0, :, :] = key_grad
            kg[1, :, :] = value_grad
        else:
            kg[0, :, :] = kg[0, :, :] + key_grad
            kg[1, :, :] = kg[1, :, :] + value_grad
    for i in range(1, 3):
        before = rem(t + 16 - i, 16)
        to = me.at(x=rem(before, 4), y=lax.div(before, jnp.int32(4)))
        mv.send(kg.at[:, 192 - 64 * i : 256 - 64 * i, :], kgot.at[i - 1], s_kg.at[i - 1], r_kg.at[i - 1], to)
    ends.start(0)
    for i in range(2):
        mv.arrived(kgot.at[i], r_kg.at[i])
    for i in range(2):
        total = kg[i, 192:256, :] + kgot[0, i] + kgot[1, i]
        gq[1, y, mine, 384 + 128 * i : 512 + 128 * i] = total.astype(BF16)
    ends.start(1)
    mv.settle(line_sum)
    mv.settle("xa")
    mv.settle("ctx")
    mv.settle(back)
    ends.middle()

    def hidden_part(e):
        q = ends.group(e)
        for j in range(2):
            columns = slice(j * 256, (j + 1) * 256)
            total = nt(gq[0, q], wq[1, columns, 0:640])
            total = total + nt(gq[1, q, :, 0:384], wq[1, columns, 640:1024])
            total = total + nt(gq[1, q, :, 384:512], wk[1, columns, :])
            total = total + nt(gq[1, q, :, 512:640], wv[1, columns, :])
            line_sum.refs[0][e, :, columns] = total.astype(BF16)
        line_sum.swap(e)

    hidden_part(0)
    ends.end()
    attends.start(0)
    attends.start(1)
    hidden_part(1)
    line_sum.pair(0)
    hidden_part(3)
    line_sum.pair(1)
    hidden_part(2)
    line_sum.pair(3)
    line_sum.pair(2)

    def query_weight(h):
        for first in (0, 256, 512, 640, 896):
            width = 128 if first in (512, 896) else 256
            i, there = (0, first) if first < 640 else (1, first - 640)
            total = jnp.zeros((512, width), F32)
            for q in range(4):
                total = total + tn(xn[h, q], gq[i, q, :, there : there + width])
            total = total.astype(BF16)
            place = first % 512
            for k in range(2):
                stage[h, 2 * k + first // 512, :, place : place + width] = total[k * 256 : (k + 1) * 256, :]
        for k in range(4):
            local_out(stage.at[h, k], query_out.at[h, (k // 2) * 256 : (k // 2 + 1) * 256, (k % 2) * 512 : (k % 2 + 1) * 512])

    def key_value_weight(h):
        total = jnp.zeros((512, 256), F32)
        for q in range(4):
            total = total + tn(xn[h, q], gq[1, q, :, 384:640])
        kvs[0, h] = total[:, 0:128].astype(BF16)
        kvs[1, h] = total[:, 128:256].astype(BF16)
        local_out(kvs.at[0, h], key_out.at[h])
        local_out(kvs.at[1, h], value_out.at[h])

    def output_weight(h):
        for j in range(2):
            columns = slice(j * 256, (j + 1) * 256)
            total = jnp.zeros((512, 256), F32)
            for q in range(4):
                total = total + tn(at[h, q], ea[1, q, :, columns])
            total = total.astype(BF16)
            for k in range(2):
                back_ps[h, k, :, columns] = total[k * 256 : (k + 1) * 256, :]
        for k in range(2):
            local_out(back_ps.at[h, k], output_out.at[(2 * h + k) * 256 : (2 * h + k + 1) * 256, :])

    key_value_weight(0)
    key_value_weight(1)
    for h in range(2):
        attends.first(h)
    hidden_grad = line_sum.total()
    scaled = hidden_grad * scale_j
    value = joined[...]
    inner_stats.start(lanes(jnp.sum(scaled * value, -1, keepdims=True)))
    own_rate = hidden_rates.tiles[2 * q0 + c]
    jg[q0, half, :] = (cotangent[...].astype(F32) + column(own_rate[0:1, :]) * scaled).astype(BF16)
    grad_rows.to_sibling(0)
    grad_rows.along_z()
    for h in range(2):
        attends.relay(h, 0)
    for h in range(2):
        attends.far(h)
    query_weight(0)
    mean = inner_stats.total() / 8192.0
    factors.start(own_rate * own_rate * own_rate * mean)
    for a in (3, 1):
        for h in range(2):
            attends.relay(h, a)
    attends.end()

    def output_part(e):
        q = attends.group(e)
        for j in range(2):
            columns = slice(j * 256, (j + 1) * 256)
            total = dot(at[0, q], wo[0:512, columns]) + dot(at[1, q], wo[512:1024, columns])
            output.refs[0][e, :, columns] = total.astype(BF16)
        output.swap(e)

    for e in NEAR:
        grad_rows.forward(e)
    output_part(0)
    output_part(1)
    output.pair(0)
    output_part(3)
    output.pair(1)
    output_part(2)
    output.pair(3)
    output.pair(2)
    query_weight(1)
    for e in range(4):
        grad_rows.whole(e)
    factors.whole()
    for q in range(4):
        for k in range(2):
            part = slice(k * 128, (k + 1) * 128)
            grad = jg[q, part, :].astype(F32) - xa[q, part, :].astype(F32) * factors.column(q, k)
            xa[q, part, :] = grad.astype(BF16)

    def join_weight(l, carry):
        for h in range(2):
            for j in range(2):
                columns = slice(j * 256, (j + 1) * 256)
                total = jnp.zeros((512, 256), F32)
                for q in range(4):
                    total = total + tn(fa[h, q, l], xa[q, :, columns])
                total = total.astype(BF16)
                for k in range(2):
                    ca[2 * h + k, l, :, columns] = total[k * 256 : (k + 1) * 256, :]
        return carry

    lax.fori_loop(0, 3, join_weight, 0)
    for k in range(4):
        local_out(ca.at[k], join_out.at[:, k * 256 : (k + 1) * 256, :])
    output_weight(0)
    output_weight(1)
    draft[...] = (value + output.total()).astype(BF16)
    mv.drain()
    for copy in outs:
        copy.wait()


def step_call(*args):
    def gather_g():
        return [dma(3), dma(3), dma(4), dma(4)]

    shape = jax.ShapeDtypeStruct
    return pl.pallas_call(
        step_kernel,
        name="step",
        out_shape=(
            shape((128, 512), BF16),
            shape((3, 1024, 512), BF16),
            shape((2, 512, 1024), BF16),
            shape((2, 512, 128), BF16),
            shape((2, 512, 128), BF16),
            shape((1024, 512), BF16),
        ),
        in_specs=[IN_VMEM] * 13,
        out_specs=(IN_VMEM, *[ANYWHERE] * 5),
        scratch_shapes=[
            vmem(4, 3, 256, 512),
            vmem(2, 4, 3, 256, 512),
            vmem(4, 3, 3, 64, 512),
            vmem(3, 3, 256, 512),
            vmem(4, 3, 64, 512),
            vmem(3, 256, 512),
            vmem(3, 3, 64, 512),
            vmem(3, 3, 64, 512),
            vmem(2, 4, 3, 256, 512),
            vmem(2, 4, 256, 512),
            vmem(4, 256, 512),
            vmem(512, 128),
            vmem(512, 128),
            vmem(256, 128),
            vmem(256, 128),
            vmem(2, 256, 128, dtype=F32),
            vmem(2, 2, 64, 128, dtype=F32),
            vmem(2, 4, 256, 640),
            vmem(2, 4, 256, 512),
            vmem(4, 256, 512),
            vmem(128, 512, dtype=F32),
            vmem(2, 2, 512, 128),
            vmem(2, 4, 256, 640),
            dma(26), dma(2, 2), dma(2, 2), dma(2), dma(2),
            dma(4, 3), dma(4, 3), dma(4), dma(3), dma(4), dma(3), dma(3), dma(3),
            *gather_g(), *gather_g(), *gather_g(), *gather_g(),
            *StatsT.scratch(), *StatsT.scratch(), *StatsT.scratch(),
            *TilesG.scratch(), *TilesG.scratch(), *TilesG.scratch(),
            *SumT.scratch(512), *SumT.scratch(640), *SumG.scratch(), *SumG.scratch(),
            *GatherT.scratch(), *GatherT.scratch(), *GatherT.scratch(),
        ],
        compiler_params=pltpu.CompilerParams(
            collective_id=0, has_side_effects=True, vmem_limit_bytes=VMEM_LIMIT
        ),
        cost_estimate=pl.CostEstimate(flops=20000000000, bytes_accessed=24000000, transcendentals=0),
    )(*args)


def local(
    context,
    resid_in,
    target_out_w,
    embedded,
    join_w,
    embed_gain,
    joined_gain,
    query_w,
    key_w,
    value_w,
    out_w,
    segment_ids,
    grad_hidden,
):
    first_query = lax.axis_index("tensor") * 64
    seq_start = first_query // 512 * 512
    segments = jnp.pad(segment_ids.reshape(-1), (192, 0))
    key_segment = lax.dynamic_slice_in_dim(segments, first_query, 256, 0)
    query_segment = lax.dynamic_slice_in_dim(segments, first_query + 192, 64, 0)
    key_pos = first_query - 192 + jnp.arange(256, dtype=jnp.int32)
    query_pos = first_query + jnp.arange(64, dtype=jnp.int32)
    mask = (
        (query_segment[:, None] == key_segment[None, :])
        & (key_pos[None, :] <= query_pos[:, None])
        & (key_pos[None, :] >= seq_start)
    ).astype(F32)
    return step_call(
        context.transpose(1, 0, 2),
        resid_in.transpose(1, 0, 2),
        target_out_w,
        join_w,
        embedded,
        grad_hidden,
        embed_gain.reshape(1, -1),
        joined_gain.reshape(1, -1),
        query_w,
        key_w,
        value_w,
        out_w,
        mask,
    )


def solution(mesh):
    in_specs = (
        P(("group", "seq"), None, "tensor"),
        P("tensor", None, ("group", "seq")),
        P(None, "tensor", ("group", "seq")),
        P(("group", "seq"), "tensor"),
        P(None, ("group", "seq"), "tensor"),
        P("tensor"),
        P("tensor"),
        P(None, "tensor", ("group", "seq")),
        P(None, "tensor", ("group", "seq")),
        P(None, "tensor", ("group", "seq")),
        P(("group", "seq"), "tensor"),
        P(),
        P(("group", "seq"), "tensor"),
    )
    out_specs = (
        P(("group", "seq"), "tensor"),
        P(None, ("group", "seq"), "tensor"),
        P(None, "tensor", ("group", "seq")),
        P(None, "tensor", ("group", "seq")),
        P(None, "tensor", ("group", "seq")),
        P(("group", "seq"), "tensor"),
    )
    return jax.shard_map(local, mesh=mesh, in_specs=in_specs, out_specs=out_specs, check_vma=False)
```

time: 276 us -> 247 us (0.89)
  Pallas kernels: 249 us -> 232 us
  matrix products: 15.6 us -> 0 us
  local copies, waits for them, and re-layouts: 6.42 us -> 12.4 us
    pallas_call x2 -> x1, Pallas kernels: 249 us -> 232 us  [step_call(): pl.pallas_call(step_kernel, name='step', out_shape=(shape((128, 512), BF1...]
    dot_general x5 -> x0, matrix products: 15.6 us -> none  [over_tokens(): jnp.einsum(spec, left, right, preferred_element_type=F32).astype(BF16)]
    unnamed x12 -> x15, local copies, waits for them, and re-layouts: 2.81 us -> 9.87 us
where the time goes in v3:
time: 247 us; the launch traced here: 246 us
  Pallas kernels  232 us (94%)
  local copies, waits for them, and re-layouts  12.4 us (5%)
    pallas_call x1, Pallas kernels, step_call(): pl.pallas_call(step_kernel, name='step', out_shape=(shape((128, 512), BF1...  232 us
    unnamed x15, local copies, waits for them, and re-layouts  9.87 us

profile of v3, /device:TPU:1, one launch (start us, length us, event | category | flops | bytes accessed | tf_op | source)
XLA Modules:
  0.0 246.3 jit_solution(10531319724759550780)
XLA Ops:
  0.7 1.3 reshape.35.refs_6_
  1.9 1.3 reshape.36.refs_7_
  3.2 0.7 copy.19
  3.9 0.1 pad_dynamic-slice_fusion.1
  3.9 0.1 pad_dynamic-slice_fusion
  4.0 0.7 and_convert_fusion.refs_12_
  4.7 232.4 %step.1 = (bf16[128,512]{1,0:T(8,128)(2,1)}, bf16[3,1024,512]{2,1,0:T(8,128)(2,1)}, bf16[2,512,1024]{2,1,0:T(8,128)(2,1)}, bf16[2,512,128]{2,1,0:T(8,128)(2,1)},...) custom-call(bf16[3,128,512]{2,1,0:T(8,128)(2,1)} %bitcast.7, bf16[3,64,1024]{2,1,0:T(8,128)(2,1)} %bitcast.8, ...), custom_call_target="tpu_custom_call" | custom-call | flops 20000000000 | bytes 24000000 | tf_op jit(solution)/shard_map/step/pallas_call | solution.py:815
  237.1 1.6 copy.26
  238.7 0.0 copy-start
  238.7 3.9 %copy.27 = bf16[3,1024,512]{2,1,0:T(8,128)(2,1)} copy(bf16[3,1024,512]{2,1,0:T(8,128)(2,1)} %get-tuple-element.17) | data formatting | bytes 6291456
  242.6 0.0 copy-done
  242.6 0.0 copy-start.3
  242.6 0.0 copy-start.2
  242.6 0.0 copy-start.1
  242.6 1.3 copy.28
  243.9 0.0 copy-done.3
  243.9 0.7 copy.29
  244.6 0.0 copy-done.2
  244.6 0.7 copy.30
  245.3 0.0 copy-done.1
  245.4 1.0 copy.31
  (1 shorter events, 0.0 us)
Async XLA Ops:
  238.7 3.9 %copy-start = (bf16[2,512,1024]{2,1,0:T(8,128)(2,1)S(1)}, bf16[2,512,1024]{2,1,0:T(8,128)(2,1)}, u32[]{:S(2)}) copy-start(bf16[2,512,1024]{2,1,0:T(8,128)(2,1)} %get-tuple-element.18) | copy-start | bytes 6291460
  242.6 1.3 copy-start.3
  242.6 2.0 copy-start.2
  242.6 2.7 %copy-start.1 = (bf16[1024,512]{1,0:T(8,128)(2,1)S(1)}, bf16[1024,512]{1,0:T(8,128)(2,1)}, u32[]{:S(2)}) copy-start(bf16[1024,512]{1,0:T(8,128)(2,1)} %get-tuple-element.21) | copy-start | bytes 3145732

commit v4 on v3

--- a/solution.py
+++ b/solution.py
@@ -255,61 +255,80 @@
 
 
 class SumT:
-    def __init__(self, mv, ps, rx, ry, s0, s1, r2x, r2y, *sems):
-        self.mv, self.ps, self.rx, self.ry, self.s0, self.s1, self.r2x, self.r2y = mv, ps, rx, ry, s0, s1, r2x, r2y
+    def __init__(self, mv, ps, hx, rx, hy, ry, s0, s1, r2x, r2y, *sems):
+        self.mv, self.ps, self.hx, self.rx, self.hy, self.ry = mv, ps, hx, rx, hy, ry
+        self.s0, self.s1, self.r2x, self.r2y = s0, s1, r2x, r2y
         self.sems = sems
 
     def issue(self, e):
         mv, me = self.mv, self.mv.me
-        s_x, r_x, s_y, r_y = self.sems[:4]
-        for d in NEAR:
-            to = rem(me.x + d, 4)
-            mv.send(self.ps.at[0, e, rows(to * 64, 64), :], self.rx.at[e, 3 - d], s_x.at[e, d - 1], r_x.at[e, 3 - d], me.at(x=to), tag=self)
-        if e:
-            mv.send(self.ps.at[1, e], self.ry.at[3 - e], s_y.at[e], r_y.at[3 - e], me.to_y(e), tag=self)
+        s_hx, r_hx, _, _, s_hy, r_hy = self.sems[:6]
+        opposite = rem(me.x + 2, 4) * 64
+        for i, step in enumerate((1, 3)):
+            part = self.ps.at[0, e, rows(opposite + 32 * i, 32), :]
+            mv.send(part, self.hx.at[e, i], s_hx.at[e, i], r_hx.at[e, i], me.to_x(step), tag=self)
+            if e == 2:
+                part = self.ps.at[1, 2, 128 * i : 128 * i + 128, :]
+                mv.send(part, self.hy.at[i], s_hy.at[i], r_hy.at[i], me.to_y(step), tag=self)
+
+    def second(self, e):
+        mv, me = self.mv, self.mv.me
+        _, r_hx, s_x, r_x, _, r_hy, s_y, r_y = self.sems[:8]
+        for i, step in enumerate((1, 3)):
+            if e == step:
+                mv.arrived(self.hy.at[i], r_hy.at[i])
+                part = slice(128 * i, 128 * i + 128)
+                self.ps[1, e, part, :] = (self.ps[1, e, part, :].astype(F32) + self.hy[i].astype(F32)).astype(BF16)
+                mv.send(self.ps.at[1, e], self.ry.at[i], s_y.at[i], r_y.at[i], me.to_y(step), tag=self)
+        for i, step in enumerate((1, 3)):
+            to = rem(me.x + step, 4) * 64
+            mv.arrived(self.hx.at[e, i], r_hx.at[e, i])
+            part = rows(to + 32 * i, 32)
+            self.ps[0, e, part, :] = (self.ps[0, e, part, :].astype(F32) + self.hx[e, i].astype(F32)).astype(BF16)
+            mv.send(self.ps.at[0, e, rows(to, 64), :], self.rx.at[e, i], s_x.at[e, i], r_x.at[e, i], me.to_x(step), tag=self)
 
     def collect_x(self, e):
         mv, me = self.mv, self.mv.me
-        r_x, s_2x, r_2x = self.sems[1], self.sems[4], self.sems[5]
-        for d in NEAR:
-            mv.arrived(self.rx.at[e, d - 1], r_x.at[e, d - 1])
+        r_x, s_2x, r_2x = self.sems[3], self.sems[8], self.sems[9]
         total = self.ps[0, e, rows(me.x * 64, 64), :].astype(F32)
-        for d in range(3):
-            total = total + self.rx[e, d].astype(F32)
+        for i in range(2):
+            mv.arrived(self.rx.at[e, i], r_x.at[e, i])
+            total = total + self.rx[e, i].astype(F32)
         self.s0[e] = total.astype(BF16)
         if e:
-            mv.send(self.s0.at[e], self.r2x.at[3 - e], s_2x.at[e], r_2x.at[3 - e], me.to_y(e))
+            mv.send(self.s0.at[e], self.r2x.at[3 - e], s_2x.at[e], r_2x.at[3 - e], me.to_y(e), tag=self)
 
     def fold(self):
         mv, me = self.mv, self.mv.me
-        r_y, s_2y, r_2y = self.sems[3], self.sems[6], self.sems[7]
-        for d in NEAR:
-            mv.arrived(self.ry.at[d - 1], r_y.at[d - 1])
+        r_y, s_2y, r_2y = self.sems[7], self.sems[10], self.sems[11]
+        for i in range(2):
+            mv.arrived(self.ry.at[i], r_y.at[i])
         for d in (2, 1, 3, 0):
             to = rem(me.x + d, 4)
             part = rows(to * 64, 64)
             total = self.ps[1, 0, part, :].astype(F32)
-            for i in range(3):
+            for i in range(2):
                 total = total + self.ry[i, part, :].astype(F32)
             self.s1[part, :] = total.astype(BF16)
             if d:
-                mv.send(self.s1.at[part, :], self.r2y.at[3 - d], s_2y.at[d - 1], r_2y.at[3 - d], me.at(x=to))
+                mv.send(self.s1.at[part, :], self.r2y.at[3 - d], s_2y.at[d - 1], r_2y.at[3 - d], me.at(x=to), tag=self)
 
     def finish(self, h):
         mv, me = self.mv, self.mv.me
-        got, sem = ((self.r2x, self.sems[5]), (self.r2y, self.sems[7]))[h]
+        got, sem = ((self.r2x, self.sems[9]), (self.r2y, self.sems[11]))[h]
         for d in NEAR:
             mv.arrived(got.at[d - 1], sem.at[d - 1])
         total = (self.s0[0] if h == 0 else self.s1[rows(me.x * 64, 64), :]).astype(F32)
         for d in range(3):
             total = total + got[d].astype(F32)
-        return total.astype(BF16)
+        return total
 
     @staticmethod
     def scratch(w):
         return [
-            vmem(4, 3, 64, w), vmem(3, 256, w), vmem(4, 64, w), vmem(256, w), vmem(3, 64, w), vmem(3, 64, w),
-            dma(4, 3), dma(4, 3), dma(4), dma(3), dma(4), dma(3), dma(3), dma(3),
+            vmem(4, 2, 32, w), vmem(4, 2, 64, w), vmem(2, 128, w), vmem(2, 256, w),
+            vmem(4, 64, w), vmem(256, w), vmem(3, 64, w), vmem(3, 64, w),
+            dma(4, 2), dma(4, 2), dma(4, 2), dma(4, 2), dma(2), dma(2), dma(2), dma(2), dma(4), dma(3), dma(3), dma(3),
         ]
 
 
@@ -382,11 +401,12 @@
 
 def step_kernel(*refs):
     refs = list(refs)
-    ctx, resid, wt, wj, embedded, cotangent, gain_e, gain_j, wq, wk, wv, wo, mask = take(refs, 13)
+    ctx, resid, embedded, cotangent, gains, mask = take(refs, 6)
+    weights = take(refs, 6)
     draft, join_out, query_out, key_out, value_out, output_out = take(refs, 6)
-    ca, sb, rx, ry, s0, s1, r2x, r2y, fa, ea, xa, qh, gh, kw, vw, kg, kgot, gq, at, jg, joined, kvs, qps = take(refs, 23)
-    s_loc, s_kv, r_kv, s_kg, r_kg = take(refs, 5)
-    s_x, r_x, s_y, r_y, s_2x, r_2x, s_2y, r_2y = take(refs, 8)
+    wt, wj, wq, wk, wv, wo = held = take(refs, 6)
+    ca, sb, fa, ea, xa, qh, gh, kw, vw, kg, kgot, gq, at, jg, joined, kvs, qps, sums = take(refs, 18)
+    s_loc, s_kv, r_kv, s_kg, r_kg, s_w = take(refs, 6)
     me = Place()
     x, y, z, c, t = me.x, me.y, me.z, me.c, me.t
     mv = Mover(me, s_loc.at[0])
@@ -394,17 +414,23 @@
     plane = [me.at(x=rem(x + d % 4, 4), y=rem(y + d // 4, 4)) for d in range(1, 16)]
     line = [me.at(z=rem(z + d % 4, 4), c=rem(c + d // 4, 2)) for d in range(1, 8)]
     xn, back_ps, stage = sb.at[:, :, 1], sb.at[:, :, 0], sb.at[:, :, 2]
-    context_rows = GatherG(mv, "ctx", lambda q, core: ca.at[q, :, rows(core * 128, 128), :], *take(refs, 4))
+    context_rows = [
+        GatherG(mv, "ctx", lambda q, core, l=l: ca.at[q, l, rows(core * 128, 128), :], *take(refs, 4)) for l in range(3)
+    ]
+    levels = [SumT(mv, sb.at[:, :, l], *take(refs, 20)) for l in range(3)]
     early_rows = GatherG(mv, "end", lambda q, core: ea.at[:, q, rows(core * 128, 128), :], *take(refs, 4))
     hidden_rows = GatherG(mv, "xa", lambda q, core: xa.at[q, rows(core * 128, 128), :], *take(refs, 4))
     grad_rows = GatherG(mv, "end", lambda q, core: jg.at[q, rows(core * 128, 128), :], *take(refs, 4))
     embed_stats, hidden_stats, inner_stats = (StatsT(mv, *take(refs, 3)) for _ in range(3))
     embed_rates, hidden_rates, factors = (TilesG(mv, line, *take(refs, 3)) for _ in range(3))
-    back = SumT(mv, back_ps, *take(refs, 14))
-    qkv = SumT(mv, qps, *take(refs, 14))
+    back = SumT(mv, back_ps, *take(refs, 20))
+    qkv = SumT(mv, qps, *take(refs, 20))
     line_sum = SumG(mv, *take(refs, 8))
     output = SumG(mv, *take(refs, 8))
-    feats = GatherT(mv, lambda h, q, p, lo, n: fa.at[h, q, :, pl.ds(pl.multiple_of(p * 64 + lo, 32), n), :], *take(refs, 4))
+    feats = [
+        GatherT(mv, lambda h, q, p, lo, n, l=l: fa.at[h, q, l, pl.ds(pl.multiple_of(p * 64 + lo, 32), n), :], *take(refs, 4))
+        for l in range(3)
+    ]
     ends = GatherT(mv, lambda h, q, p, lo, n: gq.at[h, q, pl.ds(pl.multiple_of(p * 64 + lo, 32), n), :], *take(refs, 4))
     attends = GatherT(mv, lambda h, q, p, lo, n: at.at[h, q, pl.ds(pl.multiple_of(p * 64 + lo, 32), n), :], *take(refs, 4))
     assert not refs
@@ -415,109 +441,94 @@
         copy.start()
         outs.append(copy)
 
+    loads = [pltpu.make_async_copy(src, dst, s_w.at[i]) for i, (src, dst) in enumerate(zip(weights, held))]
+    for load in loads:
+        load.start()
     greet(plane + line)
 
-    group = context_rows.group
-    q0 = group[0]
-    context_rows.to_sibling(0, ctx)
-    context_rows.along_z(ctx)
+    q0 = group_of(z)
+
+    def context_out(l):
+        context_rows[l].to_sibling(0, ctx.at[l])
+        context_rows[l].along_z(ctx.at[l])
+
+    context_out(0)
+    context_out(1)
     ca[q0, :, half, :] = ctx[...]
     ea[0, q0, half, :] = embedded[...]
     ea[1, q0, half, :] = cotangent[...]
     own_embedded = embedded[...].astype(F32)
     embed_stats.start(lanes(jnp.sum(own_embedded * own_embedded, -1, keepdims=True)))
 
-    def target(e):
-        def level(l, carry):
+    def context_in(l):
+        for e in NEAR:
+            context_rows[l].forward(e)
+        for e in range(4):
+            context_rows[l].whole(e)
+
+    def target(l):
+        for e in (2, 1, 3, 0):
+            q = rem(y + e, 4)
             for j in range(4):
-                part = dot(ca[group[e], l], wt[l, :, j * 256 : (j + 1) * 256])
+                part = dot(ca[q, l], wt[l, :, j * 256 : (j + 1) * 256])
                 sb[j // 2, e, l, :, (j % 2) * 256 : (j % 2 + 1) * 256] = part.astype(BF16)
-            return carry
-
-        lax.fori_loop(0, 3, level, 0)
-        for d in NEAR:
-            to = rem(x + d, 4)
-            mv.send(
-                sb.at[0, e, :, rows(to * 64, 64), :], rx.at[e, 3 - d], s_x.at[e, d - 1], r_x.at[e, 3 - d],
-                me.at(x=to), tag="sb",
-            )
-        slot = rem(y - group[e] + 4, 4)
-        to = jnp.maximum(slot - 1, 0)
-        mv.send(sb.at[1, e], ry.at[to], s_y.at[e], r_y.at[to], me.at(y=group[e]), when=slot != 0, tag="sb")
-
-    def collect_x(e):
-        for d in NEAR:
-            mv.arrived(rx.at[e, d - 1], r_x.at[e, d - 1])
-
-        def level(l, carry):
-            total = sb[0, e, l, mine, :].astype(F32)
-            for d in range(3):
-                total = total + rx[e, d, l].astype(F32)
-            s0[e, l] = total.astype(BF16)
-            return carry
-
-        lax.fori_loop(0, 3, level, 0)
-        slot = rem(y - group[e] + 4, 4)
-        to = jnp.maximum(slot - 1, 0)
-        mv.send(s0.at[e], r2x.at[to], s_2x.at[e], r_2x.at[to], me.at(y=group[e]), when=slot != 0)
-
-    for e in (0, 1, 3):
-        if e:
-            context_rows.forward(e)
-        context_rows.whole(e)
-        target(e)
+            levels[l].issue(e)
+
+    def second(l):
+        for e in (1, 3, 2, 0):
+            levels[l].second(e)
+
+    def collect(l):
+        for e in (2, 1, 3, 0):
+            levels[l].collect_x(e)
+        levels[l].fold()
+
+    def finish(l):
+        for h in range(2):
+            total = levels[l].finish(h)
+            fa[h, y, l, mine, :] = (resid[l, :, h * 512 : (h + 1) * 512].astype(F32) + total).astype(BF16)
+            feats[l].start(h)
+
+    def both(step, *args):
+        for h in range(2):
+            step(h, *args)
+
+    loads[0].wait()
+    context_in(0)
+    context_out(2)
+    target(0)
+    context_in(1)
     early_rows.to_sibling(0)
     early_rows.along_z()
-    collect_x(0)
-    context_rows.forward(2)
-    context_rows.whole(2)
+    target(1)
+    second(0)
+    context_in(2)
     target(2)
+    second(1)
     embed_rates.start(lax.rsqrt(embed_stats.total() / 8192.0 + epsilon))
-    for e in (1, 3, 2):
-        collect_x(e)
+    collect(0)
+    second(2)
     for e in NEAR:
         early_rows.forward(e)
-    own = rem(group_of(y) - z + 4, 4)
-    for d in NEAR:
-        mv.arrived(ry.at[d - 1], r_y.at[d - 1])
-    for d in (2, 1, 3, 0):
-        to = rem(x + d, 4)
-        part = rows(to * 64, 64)
-
-        def fold(l, carry):
-            total = sb[1, own, l, part, :].astype(F32)
-            for i in range(3):
-                total = total + ry[i, l, part, :].astype(F32)
-            s1[l, part, :] = total.astype(BF16)
-            return carry
-
-        lax.fori_loop(0, 3, fold, 0)
-        if d:
-            mv.send(s1.at[:, part, :], r2y.at[3 - d], s_2y.at[d - 1], r_2y.at[3 - d], me.at(x=to))
-
-    def finish(h, part, got, sem):
-        for d in NEAR:
-            mv.arrived(got.at[d - 1], sem.at[d - 1])
-
-        def level(l, carry):
-            total = part(l).astype(F32)
-            for d in range(3):
-                total = total + got[d, l].astype(F32)
-            fa[h, y, l, mine, :] = (resid[l, :, h * 512 : (h + 1) * 512].astype(F32) + total).astype(BF16)
-            return carry
-
-        lax.fori_loop(0, 3, level, 0)
-        feats.start(h)
-
-    finish(0, lambda l: s0[own, l], r2x, r_2x)
-    finish(1, lambda l: s1[l, mine, :], r2y, r_2y)
-
-    mv.settle("sb")
+    finish(0)
+    collect(1)
+    both(feats[0].first)
+    finish(1)
+    both(feats[0].relay, 0)
+    collect(2)
+    both(feats[0].far)
+    both(feats[1].first)
+    finish(2)
+
     for e in range(4):
         early_rows.whole(e)
     embed_rates.whole()
-    scale_e = gain_e[...].astype(F32)
-    scale_j = gain_j[...].astype(F32)
+    scale_e = gains[0:1, :].astype(F32)
+    scale_j = gains[1:2, :].astype(F32)
+    for l in range(3):
+        mv.settle(levels[l])
+    for load in loads[1:]:
+        load.wait()
 
     def inputs_part(e, i, source, rates, scales):
         q = rem(y + e, 4)
@@ -542,44 +553,54 @@
             part = nt(ea[1, q], wo[j * 256 : (j + 1) * 256, :])
             back_ps[j // 2, e, :, (j % 2) * 256 : (j % 2 + 1) * 256] = part.astype(BF16)
 
-    def join(e):
-        q = feats.group(e)
+    def join(l, e):
+        q = feats[l].group(e)
         for j in range(2):
             columns = slice(j * 256, (j + 1) * 256)
-            total = jnp.zeros((256, 256), F32)
-            for l in range(3):
-                for h in range(2):
-                    total = total + dot(fa[h, q, l], wj[l, h * 512 : (h + 1) * 512, columns])
-            line_sum.refs[0][e, :, columns] = total.astype(BF16)
-        line_sum.swap(e)
-
-    for h in range(2):
-        feats.first(h)
+            total = dot(fa[0, q, l], wj[l, 0:512, columns]) + dot(fa[1, q, l], wj[l, 512:1024, columns])
+            if l:
+                total = total + sums[e, :, columns]
+            if l < 2:
+                sums[e, :, columns] = total
+            else:
+                line_sum.refs[0][e, :, columns] = total.astype(BF16)
+        if l == 2:
+            line_sum.swap(e)
+
+    both(feats[0].relay, 3)
+    both(feats[0].relay, 1)
     embed_part(2)
+    both(feats[1].relay, 0)
+    both(feats[0].relay, 2)
+    both(feats[1].far)
+    both(feats[2].first)
     embed_part(1)
-    for h in range(2):
-        feats.relay(h, 0)
-    for h in range(2):
-        feats.far(h)
+    both(feats[1].relay, 3)
+    both(feats[1].relay, 1)
+    both(feats[2].relay, 0)
     embed_part(3)
+    both(feats[1].relay, 2)
+    both(feats[2].far)
     embed_part(0)
-    for h in range(2):
-        feats.relay(h, 3)
-    back_part(2)
-    back_part(1)
-    for h in range(2):
-        feats.relay(h, 1)
-    back_part(3)
-    back_part(0)
-    join(0)
-    feats.end()
-    join(1)
-    line_sum.pair(0)
+    for e in (0, 1, 3, 2):
+        join(0, e)
+    both(feats[2].relay, 3)
+    both(feats[2].relay, 1)
+    for e in (2, 1, 3, 0):
+        back_part(e)
+    join(1, 0)
+    join(1, 1)
+    both(feats[2].relay, 2)
+    join(1, 3)
+    join(1, 2)
+    join(2, 0)
     for e in (2, 1, 3, 0):
         back.issue(e)
-    join(3)
+    join(2, 1)
+    line_sum.pair(0)
+    join(2, 3)
     line_sum.pair(1)
-    join(2)
+    join(2, 2)
     line_sum.pair(3)
     line_sum.pair(2)
     value = line_sum.total()
@@ -589,6 +610,8 @@
     hidden_rows.to_sibling(0)
     hidden_rows.along_z()
     hidden_stats.start(lanes(jnp.sum(value * value, -1, keepdims=True)))
+    for e in (1, 3, 2, 0):
+        back.second(e)
     for e in NEAR:
         hidden_rows.forward(e)
     hidden_rates.start(lax.rsqrt(hidden_stats.total() / 8192.0 + epsilon))
@@ -601,15 +624,17 @@
         inputs_part(e, 1, lambda q: xa[q], hidden_rates, scale_j)
         qkv.issue(e)
     back.fold()
+    for e in (1, 3, 2, 0):
+        qkv.second(e)
     for h in range(2):
-        got = back.finish(h)
+        got = back.finish(h).astype(BF16)
         for i in range(4):
             gh[(4 * h + i) * 64 : (4 * h + i + 1) * 64, :] = got[:, i * 128 : (i + 1) * 128]
     for e in (2, 1, 3, 0):
         qkv.collect_x(e)
     qkv.fold()
 
-    got = qkv.finish(1)
+    got = qkv.finish(1).astype(BF16)
     kw[0:64, :] = jnp.zeros((64, 128), BF16)
     vw[0:64, :] = jnp.zeros((64, 128), BF16)
     kw[192:256, :] = got[:, 384:512]
@@ -622,7 +647,7 @@
         mv.send(vw.at[192:256, :], vw.at[place, :], s_kv.at[1, i - 1], r_kv.at[1, i - 1], to)
     for i in range(3):
         qh[(5 + i) * 64 : (6 + i) * 64, :] = got[:, i * 128 : (i + 1) * 128]
-    got = qkv.finish(0)
+    got = qkv.finish(0).astype(BF16)
     for i in range(5):
         qh[i * 64 : (i + 1) * 64, :] = got[:, i * 128 : (i + 1) * 128]
     for i in range(1, 3):
@@ -823,17 +848,17 @@
             shape((2, 512, 128), BF16),
             shape((1024, 512), BF16),
         ),
-        in_specs=[IN_VMEM] * 13,
+        in_specs=[IN_VMEM] * 6 + [ANYWHERE] * 6,
         out_specs=(IN_VMEM, *[ANYWHERE] * 5),
         scratch_shapes=[
+            vmem(3, 512, 1024),
+            vmem(3, 1024, 512),
+            vmem(2, 512, 1024),
+            vmem(2, 512, 128),
+            vmem(2, 512, 128),
+            vmem(1024, 512),
             vmem(4, 3, 256, 512),
             vmem(2, 4, 3, 256, 512),
-            vmem(4, 3, 3, 64, 512),
-            vmem(3, 3, 256, 512),
-            vmem(4, 3, 64, 512),
-            vmem(3, 256, 512),
-            vmem(3, 3, 64, 512),
-            vmem(3, 3, 64, 512),
             vmem(2, 4, 3, 256, 512),
             vmem(2, 4, 256, 512),
             vmem(4, 256, 512),
@@ -849,13 +874,15 @@
             vmem(128, 512, dtype=F32),
             vmem(2, 2, 512, 128),
             vmem(2, 4, 256, 640),
-            dma(26), dma(2, 2), dma(2, 2), dma(2), dma(2),
-            dma(4, 3), dma(4, 3), dma(4), dma(3), dma(4), dma(3), dma(3), dma(3),
-            *gather_g(), *gather_g(), *gather_g(), *gather_g(),
+            vmem(4, 256, 512, dtype=F32),
+            dma(26), dma(2, 2), dma(2, 2), dma(2), dma(2), dma(6),
+            *gather_g(), *gather_g(), *gather_g(),
+            *SumT.scratch(512), *SumT.scratch(512), *SumT.scratch(512),
+            *gather_g(), *gather_g(), *gather_g(),
             *StatsT.scratch(), *StatsT.scratch(), *StatsT.scratch(),
             *TilesG.scratch(), *TilesG.scratch(), *TilesG.scratch(),
             *SumT.scratch(512), *SumT.scratch(640), *SumG.scratch(), *SumG.scratch(),
-            *GatherT.scratch(), *GatherT.scratch(), *GatherT.scratch(),
+            *GatherT.scratch(), *GatherT.scratch(), *GatherT.scratch(), *GatherT.scratch(), *GatherT.scratch(),
         ],
         compiler_params=pltpu.CompilerParams(
             collective_id=0, has_side_effects=True, vmem_limit_bytes=VMEM_LIMIT
@@ -894,17 +921,16 @@
     return step_call(
         context.transpose(1, 0, 2),
         resid_in.transpose(1, 0, 2),
+        embedded,
+        grad_hidden,
+        jnp.stack([embed_gain, joined_gain]),
+        mask,
         target_out_w,
         join_w,
-        embedded,
-        grad_hidden,
-        embed_gain.reshape(1, -1),
-        joined_gain.reshape(1, -1),
         query_w,
         key_w,
         value_w,
         out_w,
-        mask,
     )
 
 

time: 247 us -> 218 us (0.88)
  Pallas kernels: 232 us -> 204 us
    pallas_call x1, Pallas kernels: 232 us -> 204 us  [step_call(): pl.pallas_call(step_kernel, name='step', out_shape=(shape((128, 512), BF1...]
    reshape x2 -> x0, local copies, waits for them, and re-layouts: 2.52 us -> none  [the longest x1 1.26 us: local(): embed_gain.reshape(1, -1)]
where the time goes in v4:
time: 218 us; the launch traced here: 217 us
  Pallas kernels  204 us (94%)
  local copies, waits for them, and re-layouts  11.2 us (5%)
    pallas_call x1, Pallas kernels, step_call(): pl.pallas_call(step_kernel, name='step', out_shape=(shape((128, 512), BF1...  204 us
    unnamed x15, local copies, waits for them, and re-layouts  9.87 us

profile of v4, /device:TPU:1, one launch (start us, length us, event | category | flops | bytes accessed | tf_op | source)
XLA Modules:
  0.0 217.5 jit_solution(3648353079335352670)
XLA Ops:
  0.7 0.7 stack.9
  1.3 0.7 stack.10
  2.0 0.6 pad_maximum_fusion.refs_4_
  2.6 0.7 copy.19
  3.3 0.1 pad_dynamic-slice_fusion.1
  3.4 0.1 pad_dynamic-slice_fusion
  3.5 0.7 and_convert_fusion.refs_5_
  4.2 204.1 %step.1 = (bf16[128,512]{1,0:T(8,128)(2,1)}, bf16[3,1024,512]{2,1,0:T(8,128)(2,1)}, bf16[2,512,1024]{2,1,0:T(8,128)(2,1)}, bf16[2,512,128]{2,1,0:T(8,128)(2,1)},...) custom-call(bf16[3,128,512]{2,1,0:T(8,128)(2,1)} %bitcast.7, bf16[3,64,1024]{2,1,0:T(8,128)(2,1)} %bitcast.8, ...), custom_call_target="tpu_custom_call" | custom-call | flops 20000000000 | bytes 24000000 | tf_op jit(solution)/shard_map/step/pallas_call | solution.py:840
  208.3 1.6 copy.26
  209.8 0.0 copy-start
  209.8 3.9 %copy.27 = bf16[3,1024,512]{2,1,0:T(8,128)(2,1)} copy(bf16[3,1024,512]{2,1,0:T(8,128)(2,1)} %get-tuple-element.17) | data formatting | bytes 6291456
  213.7 0.0 copy-done
  213.7 0.0 copy-start.3
  213.7 0.0 copy-start.2
  213.7 0.0 copy-start.1
  213.7 1.3 copy.28
  215.1 0.0 copy-done.3
  215.1 0.7 copy.29
  215.8 0.0 copy-done.2
  215.8 0.7 copy.30
  216.5 0.0 copy-done.1
  216.5 1.0 copy.31
  (1 shorter events, 0.0 us)
Async XLA Ops:
  209.8 3.9 %copy-start = (bf16[2,512,1024]{2,1,0:T(8,128)(2,1)S(1)}, bf16[2,512,1024]{2,1,0:T(8,128)(2,1)}, u32[]{:S(2)}) copy-start(bf16[2,512,1024]{2,1,0:T(8,128)(2,1)} %get-tuple-element.18) | copy-start | bytes 6291460
  213.7 1.3 copy-start.3
  213.7 2.0 copy-start.2
  213.7 2.7 %copy-start.1 = (bf16[1024,512]{1,0:T(8,128)(2,1)S(1)}, bf16[1024,512]{1,0:T(8,128)(2,1)}, u32[]{:S(2)}) copy-start(bf16[1024,512]{1,0:T(8,128)(2,1)} %get-tuple-element.21) | copy-start | bytes 3145732

commit v5 on v4

--- a/solution.py
+++ b/solution.py
@@ -399,11 +399,24 @@
     return out
 
 
+def attention_mask(segments, t):
+    ids = segments[...].astype(F32)
+    own = jnp.where(t < 8, ids[0:1, :], ids[1:2, :])
+    padded = jnp.concatenate([jnp.full((1, 256), -1.0, F32), own], axis=1)
+    window = padded[:, 64:320]
+    for i in range(1, 8):
+        window = jnp.where(rem(t, 8) == i, padded[:, 64 * i + 64 : 64 * i + 320], window)
+    query = column(window[:, 128:256])[64:128, :]
+    key_at = lax.broadcasted_iota(jnp.int32, (64, 256), 1)
+    query_at = lax.broadcasted_iota(jnp.int32, (64, 256), 0) + 192
+    return jnp.where((query == window) & (key_at <= query_at), 1.0, 0.0)
+
+
 def step_kernel(*refs):
     refs = list(refs)
-    ctx, resid, embedded, cotangent, gains, mask = take(refs, 6)
+    ctx, resid, embedded, cotangent, gain_e, gain_j, segments = take(refs, 7)
     weights = take(refs, 6)
-    draft, join_out, query_out, key_out, value_out, output_out = take(refs, 6)
+    draft, feats_out, grads_out, query_out, key_out, value_out, output_out = take(refs, 7)
     wt, wj, wq, wk, wv, wo = held = take(refs, 6)
     ca, sb, fa, ea, xa, qh, gh, kw, vw, kg, kgot, gq, at, jg, joined, kvs, qps, sums = take(refs, 18)
     s_loc, s_kv, r_kv, s_kg, r_kg, s_w = take(refs, 6)
@@ -523,8 +536,8 @@
     for e in range(4):
         early_rows.whole(e)
     embed_rates.whole()
-    scale_e = gains[0:1, :].astype(F32)
-    scale_j = gains[1:2, :].astype(F32)
+    scale_e = gain_e[...].astype(F32)[None, :]
+    scale_j = gain_j[...].astype(F32)[None, :]
     for l in range(3):
         mv.settle(levels[l])
     for load in loads[1:]:
@@ -603,6 +616,7 @@
     join(2, 2)
     line_sum.pair(3)
     line_sum.pair(2)
+    local_out(fa, feats_out)
     value = line_sum.total()
     joined[...] = value
 
@@ -656,7 +670,7 @@
         mv.arrived(vw.at[place, :], r_kv.at[1, i - 1])
 
     scale = 128.0**-0.5
-    allowed = jnp.concatenate([mask[...]] * 4, axis=0) > 0.5
+    allowed = jnp.concatenate([attention_mask(segments, t)] * 4, axis=0) > 0.5
     for i in range(2):
         part = slice(i * 256, (i + 1) * 256)
         scores = jnp.where(allowed, nt(qh[part, :], kw[...]) * scale, -1e30)
@@ -800,6 +814,8 @@
     output.pair(3)
     output.pair(2)
     query_weight(1)
+    output_weight(0)
+    output_weight(1)
     for e in range(4):
         grad_rows.whole(e)
     factors.whole()
@@ -809,23 +825,7 @@
             grad = jg[q, part, :].astype(F32) - xa[q, part, :].astype(F32) * factors.column(q, k)
             xa[q, part, :] = grad.astype(BF16)
 
-    def join_weight(l, carry):
-        for h in range(2):
-            for j in range(2):
-                columns = slice(j * 256, (j + 1) * 256)
-                total = jnp.zeros((512, 256), F32)
-                for q in range(4):
-                    total = total + tn(fa[h, q, l], xa[q, :, columns])
-                total = total.astype(BF16)
-                for k in range(2):
-                    ca[2 * h + k, l, :, columns] = total[k * 256 : (k + 1) * 256, :]
-        return carry
-
-    lax.fori_loop(0, 3, join_weight, 0)
-    for k in range(4):
-        local_out(ca.at[k], join_out.at[:, k * 256 : (k + 1) * 256, :])
-    output_weight(0)
-    output_weight(1)
+    local_out(xa, grads_out)
     draft[...] = (value + output.total()).astype(BF16)
     mv.drain()
     for copy in outs:
@@ -842,14 +842,15 @@
         name="step",
         out_shape=(
             shape((128, 512), BF16),
-            shape((3, 1024, 512), BF16),
+            shape((2, 4, 3, 256, 512), BF16),
+            shape((4, 256, 512), BF16),
             shape((2, 512, 1024), BF16),
             shape((2, 512, 128), BF16),
             shape((2, 512, 128), BF16),
             shape((1024, 512), BF16),
         ),
-        in_specs=[IN_VMEM] * 6 + [ANYWHERE] * 6,
-        out_specs=(IN_VMEM, *[ANYWHERE] * 5),
+        in_specs=[IN_VMEM] * 7 + [ANYWHERE] * 6,
+        out_specs=(IN_VMEM, *[ANYWHERE] * 6),
         scratch_shapes=[
             vmem(3, 512, 1024),
             vmem(3, 1024, 512),
@@ -891,6 +892,57 @@
     )(*args)
 
 
+def join_weight_kernel(feats, grads, *refs):
+    given, join_out, results = refs[:5], refs[5], refs[6:11]
+    fa, jg, stage, s_in, s_out, s_on = refs[11:17]
+    held = refs[17:]
+    taken = [pltpu.make_async_copy(src, dst, s_on.at[i]) for i, (src, dst) in enumerate(zip(given, held))]
+    handed = [pltpu.make_async_copy(src, dst, s_on.at[5 + i]) for i, (src, dst) in enumerate(zip(held, results))]
+    loads = [pltpu.make_async_copy(grads, jg, s_in.at[3])]
+    loads += [pltpu.make_async_copy(feats.at[:, :, l], fa.at[:, :, l], s_in.at[l]) for l in range(3)]
+    for copy in loads + taken:
+        copy.start()
+    loads[0].wait()
+    outs = []
+    for l in range(3):
+        loads[1 + l].wait()
+        if l == 1:
+            for there, back in zip(taken, handed):
+                there.wait()
+                back.start()
+        for h in range(2):
+            for j in range(2):
+                columns = slice(j * 256, (j + 1) * 256)
+                total = jnp.zeros((512, 256), F32)
+                for q in range(4):
+                    total = total + tn(fa[h, q, l], jg[q, :, columns])
+                stage[l, h, :, columns] = total.astype(BF16)
+            copy = pltpu.make_async_copy(stage.at[l, h], join_out.at[l, h * 512 : (h + 1) * 512, :], s_out.at[2 * l + h])
+            copy.start()
+            outs.append(copy)
+    for copy in outs + handed:
+        copy.wait()
+
+
+def join_weight_call(feats, grads, *given):
+    return pl.pallas_call(
+        join_weight_kernel,
+        name="join_weight",
+        out_shape=(
+            jax.ShapeDtypeStruct((3, 1024, 512), BF16),
+            *[jax.ShapeDtypeStruct(array.shape, array.dtype) for array in given],
+        ),
+        in_specs=[ANYWHERE] * (2 + len(given)),
+        out_specs=tuple([ANYWHERE] * (1 + len(given))),
+        scratch_shapes=[
+            vmem(2, 4, 3, 256, 512), vmem(4, 256, 512), vmem(3, 2, 512, 512), dma(4), dma(6), dma(10),
+            *[pltpu.VMEM(array.shape, array.dtype) for array in given],
+        ],
+        compiler_params=pltpu.CompilerParams(vmem_limit_bytes=VMEM_LIMIT),
+        cost_estimate=pl.CostEstimate(flops=3300000000, bytes_accessed=20000000, transcendentals=0),
+    )(feats, grads, *given)
+
+
 def local(
     context,
     resid_in,
@@ -906,25 +958,14 @@
     segment_ids,
     grad_hidden,
 ):
-    first_query = lax.axis_index("tensor") * 64
-    seq_start = first_query // 512 * 512
-    segments = jnp.pad(segment_ids.reshape(-1), (192, 0))
-    key_segment = lax.dynamic_slice_in_dim(segments, first_query, 256, 0)
-    query_segment = lax.dynamic_slice_in_dim(segments, first_query + 192, 64, 0)
-    key_pos = first_query - 192 + jnp.arange(256, dtype=jnp.int32)
-    query_pos = first_query + jnp.arange(64, dtype=jnp.int32)
-    mask = (
-        (query_segment[:, None] == key_segment[None, :])
-        & (key_pos[None, :] <= query_pos[:, None])
-        & (key_pos[None, :] >= seq_start)
-    ).astype(F32)
-    return step_call(
+    draft_hidden, feats, grads, *weights = step_call(
         context.transpose(1, 0, 2),
         resid_in.transpose(1, 0, 2),
         embedded,
         grad_hidden,
-        jnp.stack([embed_gain, joined_gain]),
-        mask,
+        embed_gain,
+        joined_gain,
+        segment_ids,
         target_out_w,
         join_w,
         query_w,
@@ -932,6 +973,8 @@
         value_w,
         out_w,
     )
+    grad_join, draft_hidden, *weights = join_weight_call(feats, grads, draft_hidden, *weights)
+    return (draft_hidden, grad_join, *weights)
 
 
 def solution(mesh):

time: 218 us -> 210 us (0.963)
  local copies, waits for them, and re-layouts: 11.2 us -> 0 us
  Pallas kernels: 204 us -> 209 us
    unnamed x15 -> x0, local copies, waits for them, and re-layouts: 9.87 us -> none
    pallas_call x0 -> x1, Pallas kernels: none -> 7.8 us  [join_weight_call(): pl.pallas_call(join_weight_kernel, name='join_weight', out_shape=(jax.Sha...]
    pallas_call x1, Pallas kernels: 204 us -> 201 us  [step_call(): pl.pallas_call(step_kernel, name='step', out_shape=(shape((128, 512), BF1...]
where the time goes in v5:
time: 210 us
  Pallas kernels  209 us (100%)
    pallas_call x1, Pallas kernels, step_call(): pl.pallas_call(step_kernel, name='step', out_shape=(shape((128, 512), BF1...  201 us
    pallas_call x1, Pallas kernels, join_weight_call(): pl.pallas_call(join_weight_kernel, name='join_weight', out_shape=(jax.Sha...  7.8 us

profile of v5, /device:TPU:1, one launch (start us, length us, event | category | flops | bytes accessed | tf_op | source)
XLA Modules:
  0.0 210.1 jit_solution(1892728319581480757)
XLA Ops:
  0.6 201.5 %step.1 = (bf16[128,512]{1,0:T(8,128)(2,1)}, bf16[2,4,3,256,512]{4,3,2,1,0:T(8,128)(2,1)}, bf16[4,256,512]{2,1,0:T(8,128)(2,1)}, bf16[2,512,1024]{2,1,0:T(8,128)...) custom-call(bf16[3,128,512]{2,1,0:T(8,128)(2,1)} %bitcast.2, ...), custom_call_target="tpu_custom_call" | custom-call | flops 20000000000 | bytes 24000000 | tf_op jit(solution)/shard_map/step/pallas_call | solution.py:840
  202.1 7.8 %join_weight.1 = (bf16[3,1024,512]{2,1,0:T(8,128)(2,1)}, bf16[128,512]{1,0:T(8,128)(2,1)}, bf16[2,512,1024]{2,1,0:T(8,128)(2,1)}, bf16[2,512,128]{2,1,0:T(8,128)...) custom-call(bf16[2,4,3,256,512]{4,3,2,1,0:T(8,128)(2,1)} %get-tuple-element.19.feats, ...), custom_call_target="tpu_custom_call" | custom-call | flops 3300000000 | bytes 20000000 | tf_op jit(solution)/shard_map/join_weight/pallas_call | solution.py:928

commit v6 on v5

--- a/solution.py
+++ b/solution.py
@@ -221,6 +221,41 @@
     @staticmethod
     def scratch():
         return [dma(2, 4), dma(2, 4), dma(2, 4, 4), dma(2, 4, 4)]
+
+
+class DirectT(GatherT):
+    def to_second(self, h, a):
+        me, (s_2, r_2) = self.mv.me, self.sems[2:]
+        for d in NEAR:
+            to = me.to_y(d) if h == 0 else me.to_x(d)
+            self.mv.send(self.block(h, a, 0), self.block(h, a, 0), s_2.at[h, a, d], r_2.at[h, a, 4 - d], to)
+
+    def start(self, h):
+        me, (s_1, r_1) = self.mv.me, self.sems[:2]
+        for d in NEAR:
+            to = me.to_x(d) if h == 0 else me.to_y(d)
+            self.mv.send(self.block(h, 0, 0), self.block(h, 0, 0), s_1.at[h, d], r_1.at[h, 4 - d], to)
+        self.to_second(h, 0)
+
+    def first(self, h):
+        for a in (1, 3):
+            self.mv.arrived(self.block(h, a, 0), self.sems[1].at[h, a])
+            self.to_second(h, a)
+
+    def far(self, h):
+        self.mv.arrived(self.block(h, 2, 0), self.sems[1].at[h, 2])
+        self.to_second(h, 2)
+
+    def relay(self, h, a):
+        pass
+
+    def group(self, e):
+        if e:
+            for a in range(4):
+                self.mv.arrived(self.block(0, a, e), self.sems[3].at[0, a, e])
+        for b in NEAR:
+            self.mv.arrived(self.block(1, e, b), self.sems[3].at[1, e, b])
+        return rem(self.mv.me.y + e, 4)
 
 
 class SumG:
@@ -445,7 +480,7 @@
         for l in range(3)
     ]
     ends = GatherT(mv, lambda h, q, p, lo, n: gq.at[h, q, pl.ds(pl.multiple_of(p * 64 + lo, 32), n), :], *take(refs, 4))
-    attends = GatherT(mv, lambda h, q, p, lo, n: at.at[h, q, pl.ds(pl.multiple_of(p * 64 + lo, 32), n), :], *take(refs, 4))
+    attends = DirectT(mv, lambda h, q, p, lo, n: at.at[h, q, pl.ds(pl.multiple_of(p * 64 + lo, 32), n), :], *take(refs, 4))
     assert not refs
     outs = []
 
@@ -712,6 +747,7 @@
     mv.settle("ctx")
     mv.settle(back)
     ends.middle()
+    both(attends.start)
 
     def hidden_part(e):
         q = ends.group(e)
@@ -723,18 +759,6 @@
             total = total + nt(gq[1, q, :, 512:640], wv[1, columns, :])
             line_sum.refs[0][e, :, columns] = total.astype(BF16)
         line_sum.swap(e)
-
-    hidden_part(0)
-    ends.end()
-    attends.start(0)
-    attends.start(1)
-    hidden_part(1)
-    line_sum.pair(0)
-    hidden_part(3)
-    line_sum.pair(1)
-    hidden_part(2)
-    line_sum.pair(3)
-    line_sum.pair(2)
 
     def query_weight(h):
         for first in (0, 256, 512, 640, 896):
@@ -771,10 +795,31 @@
         for k in range(2):
             local_out(back_ps.at[h, k], output_out.at[(2 * h + k) * 256 : (2 * h + k + 1) * 256, :])
 
+    def output_part(e):
+        q = attends.group(e)
+        for j in range(2):
+            columns = slice(j * 256, (j + 1) * 256)
+            total = dot(at[0, q], wo[0:512, columns]) + dot(at[1, q], wo[512:1024, columns])
+            output.refs[0][e, :, columns] = total.astype(BF16)
+        output.swap(e)
+
+    hidden_part(0)
+    ends.end()
+    hidden_part(1)
+    both(attends.first)
+    line_sum.pair(0)
+    hidden_part(3)
+    line_sum.pair(1)
+    both(attends.relay, 0)
+    both(attends.far)
+    hidden_part(2)
+    line_sum.pair(3)
+    line_sum.pair(2)
+    both(attends.relay, 3)
     key_value_weight(0)
     key_value_weight(1)
-    for h in range(2):
-        attends.first(h)
+    both(attends.relay, 1)
+    query_weight(0)
     hidden_grad = line_sum.total()
     scaled = hidden_grad * scale_j
     value = joined[...]
@@ -783,49 +828,27 @@
     jg[q0, half, :] = (cotangent[...].astype(F32) + column(own_rate[0:1, :]) * scaled).astype(BF16)
     grad_rows.to_sibling(0)
     grad_rows.along_z()
-    for h in range(2):
-        attends.relay(h, 0)
-    for h in range(2):
-        attends.far(h)
-    query_weight(0)
+    attends.end()
+    query_weight(1)
+    for e in (0, 1, 3, 2):
+        output_part(e)
     mean = inner_stats.total() / 8192.0
     factors.start(own_rate * own_rate * own_rate * mean)
-    for a in (3, 1):
-        for h in range(2):
-            attends.relay(h, a)
-    attends.end()
-
-    def output_part(e):
-        q = attends.group(e)
-        for j in range(2):
-            columns = slice(j * 256, (j + 1) * 256)
-            total = dot(at[0, q], wo[0:512, columns]) + dot(at[1, q], wo[512:1024, columns])
-            output.refs[0][e, :, columns] = total.astype(BF16)
-        output.swap(e)
-
+    for e in (0, 1, 3, 2):
+        output.pair(e)
     for e in NEAR:
         grad_rows.forward(e)
-    output_part(0)
-    output_part(1)
-    output.pair(0)
-    output_part(3)
-    output.pair(1)
-    output_part(2)
-    output.pair(3)
-    output.pair(2)
-    query_weight(1)
     output_weight(0)
     output_weight(1)
-    for e in range(4):
+    factors.whole()
+    for e in (0, 1, 3, 2):
         grad_rows.whole(e)
-    factors.whole()
-    for q in range(4):
+        q = grad_rows.group[e]
         for k in range(2):
             part = slice(k * 128, (k + 1) * 128)
             grad = jg[q, part, :].astype(F32) - xa[q, part, :].astype(F32) * factors.column(q, k)
             xa[q, part, :] = grad.astype(BF16)
-
-    local_out(xa, grads_out)
+        local_out(xa.at[q], grads_out.at[q])
     draft[...] = (value + output.total()).astype(BF16)
     mv.drain()
     for copy in outs:

time: 210 us -> 211 us (level); the launches traced: 210 us -> 209 us
  no operation moved by 1% of the time
where the time goes in v6:
time: 211 us; the launch traced here: 209 us
  Pallas kernels  208 us (99%)
    pallas_call x1, Pallas kernels, step_call(): pl.pallas_call(step_kernel, name='step', out_shape=(shape((128, 512), BF1...  200 us
    pallas_call x1, Pallas kernels, join_weight_call(): pl.pallas_call(join_weight_kernel, name='join_weight', out_shape=(jax.Sha...  7.8 us

profile of v6, /device:TPU:1, one launch (start us, length us, event | category | flops | bytes accessed | tf_op | source)
XLA Modules:
  0.0 208.6 jit_solution(8013643051859971872)
XLA Ops:
  0.6 200.0 %step.1 = (bf16[128,512]{1,0:T(8,128)(2,1)}, bf16[2,4,3,256,512]{4,3,2,1,0:T(8,128)(2,1)}, bf16[4,256,512]{2,1,0:T(8,128)(2,1)}, bf16[2,512,1024]{2,1,0:T(8,128)...) custom-call(bf16[3,128,512]{2,1,0:T(8,128)(2,1)} %bitcast.2, ...), custom_call_target="tpu_custom_call" | custom-call | flops 20000000000 | bytes 24000000 | tf_op jit(solution)/shard_map/step/pallas_call | solution.py:863
  200.6 7.8 %join_weight.1 = (bf16[3,1024,512]{2,1,0:T(8,128)(2,1)}, bf16[128,512]{1,0:T(8,128)(2,1)}, bf16[2,512,1024]{2,1,0:T(8,128)(2,1)}, bf16[2,512,128]{2,1,0:T(8,128)...) custom-call(bf16[2,4,3,256,512]{4,3,2,1,0:T(8,128)(2,1)} %get-tuple-element.19.feats, ...), custom_call_target="tpu_custom_call" | custom-call | flops 3300000000 | bytes 20000000 | tf_op jit(solution)/shard_map/join_weight/pallas_call | solution.py:951
